TPU v7x, 32 devices: a whole 2x2x4 slice. The times are simulated.
32 devices in a mesh: vid: 2 (over x), tm: 16 (over z, y, core).
Axes of the slice: x: 2, y: 2, z: 4, core: 2. Of those that a mesh axis runs over, the one named last changes fastest.
Arguments:
- queries: bfloat16 [4096, 1536], P(('vid', 'tm')), parts along dimension 0, may hold values from -6 to 6
- keys: bfloat16 [4096, 1536], P(('vid', 'tm')), parts along dimension 0, may hold values from -6 to 6
- values: bfloat16 [4096, 1536], P(('vid', 'tm')), parts along dimension 0, may hold values from -6 to 6
- far_picks: int32 [64, 8], P(('vid', 'tm')), parts along dimension 0, may hold values from 0 to 1
- out_weight: bfloat16 [1536, 1536], replicated, may hold values from -0.15625 to 0.15625
Outputs:
- mixed: bfloat16 [4096, 1536], P(('vid', 'tm')), parts along dimension 0
There are 2 independent parts, one for each index of `vid`. A program takes and returns all parts, laid end to end along the dimension named above; an argument that names none is the same for every part. Nothing has to cross between parts.
All inputs are finite; a program needn't handle non-finite values.
Results may differ from a plain program's by a relative error of at most 0.0056.
Values may be sent and summed in bfloat16 or wider, within the bound.
No kernel may reach another device: no remote copies, remote signals or barrier semaphores. Data moves between devices by JAX's collectives and lax.ppermute only.
A program may use at most 64 MiB of HBM per device.

v0:
```python
import jax
import jax.numpy as jnp
from jax import lax
from jax.sharding import PartitionSpec as P

HEADS = 12
HEAD_DIM = 128
BLK = 64
LEVELS = 2
PICKS = 2
FAR = 8


def padded(cells, sides, width):
    for axis, dim in sides:
        count = lax.axis_size(axis)
        ends = count - 1
        head = lax.slice_in_dim(cells, 0, width, axis=dim)
        tail = lax.slice_in_dim(cells, cells.shape[dim] - width, cells.shape[dim], axis=dim)
        cells = jnp.concatenate(
            [
                lax.ppermute(tail, axis, [(i, (i + 1) % count) for i in range(ends)]),
                cells,
                lax.ppermute(head, axis, [((i + 1) % count, i) for i in range(ends)]),
            ],
            axis=dim,
        )
    return cells


def shifted(block, axis, distance):
    devices = range(lax.axis_size(axis))
    route = [(i - distance, i) for i in devices if i - distance in devices]
    return lax.ppermute(block, axis, route)


def far_offsets():
    offset_list = []
    for column in range(FAR):
        magnitude = 2 ** (1 + column // PICKS % LEVELS)
        offset_list.append(-magnitude if column < FAR // 2 else magnitude)
    return offset_list


def attend(query_rows, near_pair, near_valid, far_pair, far_valid, out_weight):
    blocks = query_rows.shape[0] // BLK
    width = query_rows.shape[1]
    scale = HEAD_DIM ** (-0.5)
    query_heads = query_rows.reshape(blocks, BLK, HEADS, HEAD_DIM)
    near_keys = near_pair[0].reshape(-1, HEADS, HEAD_DIM)
    near_values = near_pair[1].reshape(-1, HEADS, HEAD_DIM)
    far_keys = far_pair[0].reshape(blocks, -1, HEADS, HEAD_DIM)
    far_values = far_pair[1].reshape(blocks, -1, HEADS, HEAD_DIM)
    near_scores = (
        jnp.einsum("bqhd,khd->bhqk", query_heads, near_keys, preferred_element_type=jnp.float32)
        * scale
    )
    near_scores = jnp.where(near_valid, near_scores, jnp.float32(-1e30))
    far_scores = (
        jnp.einsum("bqhd,bkhd->bhqk", query_heads, far_keys, preferred_element_type=jnp.float32)
        * scale
    )
    far_scores = jnp.where(far_valid, far_scores, jnp.float32(-1e30))
    top_score = jnp.maximum(jnp.max(near_scores, -1), jnp.max(far_scores, -1))[..., None]
    near_exp = jnp.exp(near_scores - top_score)
    far_exp = jnp.exp(far_scores - top_score)
    total = jnp.sum(near_exp, -1) + jnp.sum(far_exp, -1)
    summed = jnp.einsum(
        "bhqk,khd->bqhd",
        near_exp.astype(jnp.bfloat16),
        near_values,
        preferred_element_type=jnp.float32,
    )
    summed = summed + jnp.einsum(
        "bhqk,bkhd->bqhd",
        far_exp.astype(jnp.bfloat16),
        far_values,
        preferred_element_type=jnp.float32,
    )
    attended = (
        (summed / jnp.transpose(total, (0, 2, 1))[..., None])
        .reshape(blocks * BLK, width)
        .astype(jnp.bfloat16)
    )
    return jnp.dot(attended, out_weight, preferred_element_type=jnp.float32).astype(jnp.bfloat16)


def body(queries, keys, values, far_picks, out_weight):
    tok_rows = queries.shape[0]
    width = queries.shape[1]
    blocks = tok_rows // BLK
    devices = lax.axis_size("tm")
    device_index = lax.axis_index("tm")
    pair = jnp.stack([keys, values])
    near_pair = padded(pair, (("tm", 1),), tok_rows)
    shards = {}
    for section_level in range(LEVELS):
        distance = 2 ** (section_level + 1)
        for direction in (-1, 1):
            shards[direction * distance] = shifted(pair, "tm", -direction * distance)
    offset_list = far_offsets()
    chosen_list = []
    valid_list = []
    for column in range(FAR):
        offset = offset_list[column]
        source = shards[offset].reshape(2, blocks, BLK, width)
        chosen_list.append(jnp.take(source, far_picks[:, column], axis=1))
        valid_list.append((device_index + offset >= 0) & (device_index + offset < devices))
    far_pair = jnp.stack(chosen_list, 2).reshape(2, blocks, FAR * BLK, width)
    far_valid = jnp.repeat(jnp.stack(valid_list), BLK)
    near_valid = jnp.repeat(
        jnp.stack([device_index > 0, jnp.array(True), device_index < devices - 1]), tok_rows
    )
    return attend(queries, near_pair, near_valid, far_pair, far_valid, out_weight)


def solution(mesh):
    placed = (
        P(("vid", "tm"), None),
        P(("vid", "tm"), None),
        P(("vid", "tm"), None),
        P(("vid", "tm"), None),
        P(),
    )
    return jax.shard_map(
        body, mesh=mesh, in_specs=placed, out_specs=P(("vid", "tm"), None), check_vma=False
    )
```

profile of v0, /device:TPU:0, one launch (start us, length us, event | category | flops | bytes accessed | tf_op | source)
XLA Modules:
  0.0 94.8 jit_solution(6004676493157633338)
XLA Ops:
  0.0 1.3 %copy.56 = bf16[128,1536]{0,1:T(8,128)(2,1)S(1)} copy(bf16[128,1536]{1,0:T(8,128)(2,1)} %param.8) | data formatting | bytes 786432 | tf_op args[1]
  1.3 1.2 %copy.57 = bf16[128,1536]{0,1:T(8,128)(2,1)S(1)} copy(bf16[128,1536]{1,0:T(8,128)(2,1)} %param.9) | data formatting | bytes 786432 | tf_op args[2]
  2.5 1.0 %pad_maximum_fusion.1 = bf16[2,128,1536]{1,2,0:T(8,128)(2,1)} fusion(bf16[1,128,1536]{1,2,0:T(8,128)(2,1)S(1)} %bitcast.116, bf16[1,128,1536]{1,2,0:T(8,128)(2,1)S(1)} %bitcast.114), kind=kLoop, calls=%fused_computation.36 | loop fusion | flops 393216 | bytes 1572864 | tf_op jit(solution)/shard_map/stack | solution.py:94
  3.5 4.9 %collective-permute-start.2 = (bf16[2,128,1536]{1,2,0:T(8,128)(2,1)}, bf16[2,128,1536]{1,2,0:T(8,128)(2,1)S(1)}, u32[]{:S(2)}, u32[]{:S(2)}) collective-permute-start(bf16[2,128,1536]{1,2,0:T(8,128)(2,1)} %pad_maximum_fusion.1), channel_id=1, source_target_pairs={{0,2},{1,3},{2,4},{3,5},{4,6},{5,7},{6,8},{7,9},{8,10},{9,11},{10,... | collective-permute-start | bytes 2359304 | tf_op jit(solution)/shard_map/ppermute | solution.py:34
  8.4 3.5 %collective-permute-start.3 = (bf16[2,128,1536]{1,2,0:T(8,128)(2,1)}, bf16[2,128,1536]{1,2,0:T(8,128)(2,1)S(1)}, u32[]{:S(2)}, u32[]{:S(2)}) collective-permute-start(bf16[2,128,1536]{1,2,0:T(8,128)(2,1)} %pad_maximum_fusion.1), channel_id=1, source_target_pairs={{0,4},{1,5},{2,6},{3,7},{4,8},{5,9},{6,10},{7,11},{8,12},{9,13},{1... | collective-permute-start | bytes 2359304 | tf_op jit(solution)/shard_map/ppermute | solution.py:34
  11.9 1.3 %collective-permute-start.4 = (bf16[2,128,1536]{1,2,0:T(8,128)(2,1)}, bf16[2,128,1536]{1,2,0:T(8,128)(2,1)}, u32[]{:S(2)}, u32[]{:S(2)}) collective-permute-start(bf16[2,128,1536]{1,2,0:T(8,128)(2,1)} %pad_maximum_fusion.1), channel_id=1, source_target_pairs={{2,0},{3,1},{4,2},{5,3},{6,4},{7,5},{8,6},{9,7},{10,8},{11,9},{12,... | collective-permute-start | bytes 2359304 | tf_op jit(solution)/shard_map/ppermute | solution.py:34
  13.2 1.3 %collective-permute-start.5 = (bf16[2,128,1536]{1,2,0:T(8,128)(2,1)}, bf16[2,128,1536]{1,2,0:T(8,128)(2,1)}, u32[]{:S(2)}, u32[]{:S(2)}) collective-permute-start(bf16[2,128,1536]{1,2,0:T(8,128)(2,1)} %pad_maximum_fusion.1), channel_id=1, source_target_pairs={{4,0},{5,1},{6,2},{7,3},{8,4},{9,5},{10,6},{11,7},{12,8},{13,9},{1... | collective-permute-start | bytes 2359304 | tf_op jit(solution)/shard_map/ppermute | solution.py:34
  14.5 2.2 %collective-permute-start = (bf16[2,128,1536]{1,2,0:T(8,128)(2,1)}, bf16[2,128,1536]{1,2,0:T(8,128)(2,1)}, u32[]{:S(2)}, u32[]{:S(2)}) collective-permute-start(bf16[2,128,1536]{1,2,0:T(8,128)(2,1)} %pad_maximum_fusion.1), channel_id=1, source_target_pairs={{0,1},{1,2},{2,3},{3,4},{4,5},{5,6},{6,7},{7,8},{8,9},{9,10},{10,1... | collective-permute-start | bytes 2359304 | tf_op jit(solution)/shard_map/ppermute | solution.py:22
  16.8 0.3 slice_reduce_fusion
  17.1 0.6 compare_and_fusion.7
  17.6 0.6 pad_clamp_fusion.7
  18.2 0.6 pad_clamp_fusion.6
  18.9 0.6 compare_and_fusion
  19.5 0.6 broadcast_bitcast_fusion
  20.1 0.6 pad_clamp_fusion.1
  20.9 0.6 reshape.45
  21.5 0.3 reshape.44
  21.8 0.9 copy.59
  22.7 0.6 pad_clamp_fusion
  23.3 0.5 compare_and_fusion.5
  23.8 0.6 compare_and_fusion.3
  24.4 0.5 compare_and_fusion.1
  25.0 18.5 %collective-permute-done.2 = bf16[2,128,1536]{1,2,0:T(8,128)(2,1)S(1)} collective-permute-done((bf16[2,128,1536]{1,2,0:T(8,128)(2,1)}, bf16[2,128,1536]{1,2,0:T(8,128)(2,1)S(1)}, u32[]{:S(2)}, u32[]{:S(2)}) %collective-permute-start.2) | collective-permute-done | bytes 786464 | tf_op jit(solution)/shard_map/ppermute | solution.py:34
  43.5 1.3 %collective-permute-start.1 = (bf16[2,128,1536]{1,2,0:T(8,128)(2,1)}, bf16[2,128,1536]{1,2,0:T(8,128)(2,1)}, u32[]{:S(2)}, u32[]{:S(2)}) collective-permute-start(bf16[2,128,1536]{1,2,0:T(8,128)(2,1)} %pad_maximum_fusion.1), channel_id=1, source_target_pairs={{1,0},{2,1},{3,2},{4,3},{5,4},{6,5},{7,6},{8,7},{9,8},{10,9},{11,1... | collective-permute-start | bytes 2359304 | tf_op jit(solution)/shard_map/ppermute | solution.py:24
  44.8 0.3 copy.60
  45.1 0.7 gather_fusion
  45.8 0.7 gather_fusion.1
  46.5 0.3 copy.61
  46.8 1.5 %gather_fusion.2 = bf16[2,2,64,1536]{3,2,1,0:T(8,128)(2,1)} fusion(bf16[2,2,64,1536]{3,2,1,0:T(8,128)(2,1)S(1)} %bitcast.105, s32[1024]{0:T(1024)S(1)} %pad_clamp_fusion.5), kind=kCustom, calls=%fused_computation.2.clone | custom fusion | bytes 1572872 | tf_op jit(solution)/shard_map/jit(_take)/gather | solution.py:107
  48.3 0.6 gather_fusion.3
  48.9 1.4 %copy.62 = bf16[2,128,1536]{2,1,0:T(8,128)(2,1)S(1)} copy(bf16[2,128,1536]{1,2,0:T(8,128)(2,1)} %collective-permute-done.4) | data formatting | bytes 1572864 | tf_op jit(solution)/shard_map/ppermute | solution.py:34
  50.3 1.5 %gather_fusion.4 = bf16[2,2,64,1536]{3,2,1,0:T(8,128)(2,1)} fusion(bf16[2,2,64,1536]{3,2,1,0:T(8,128)(2,1)S(1)} %bitcast.107, s32[1024]{0:T(1024)S(1)} %pad_clamp_fusion.3), kind=kCustom, calls=%fused_computation.4.clone | custom fusion | bytes 1572872 | tf_op jit(solution)/shard_map/jit(_take)/gather | solution.py:107
  51.8 1.5 %gather_fusion.5 = bf16[2,2,64,1536]{3,2,1,0:T(8,128)(2,1)} fusion(bf16[2,2,64,1536]{3,2,1,0:T(8,128)(2,1)S(1)} %bitcast.108, s32[1024]{0:T(1024)S(1)} %pad_clamp_fusion.2), kind=kCustom, calls=%fused_computation.5.clone | custom fusion | bytes 1572872 | tf_op jit(solution)/shard_map/jit(_take)/gather | solution.py:107
  53.3 1.4 %copy.63 = bf16[2,128,1536]{2,1,0:T(8,128)(2,1)S(1)} copy(bf16[2,128,1536]{1,2,0:T(8,128)(2,1)} %collective-permute-done.5) | data formatting | bytes 1572864 | tf_op jit(solution)/shard_map/ppermute | solution.py:34
  54.7 1.6 %gather_fusion.6 = bf16[2,2,64,1536]{3,2,1,0:T(8,128)(2,1)} fusion(bf16[2,2,64,1536]{3,2,1,0:T(8,128)(2,1)S(1)} %bitcast.109, s32[1024]{0:T(1024)} %pad_clamp_fusion.1), kind=kCustom, calls=%fused_computation.6.clone | custom fusion | bytes 1572872 | tf_op jit(solution)/shard_map/jit(_take)/gather | solution.py:107
  56.4 1.7 %gather_fusion.7 = bf16[2,2,64,1536]{3,2,1,0:T(8,128)(2,1)} fusion(bf16[2,2,64,1536]{3,2,1,0:T(8,128)(2,1)S(1)} %bitcast.110, s32[1024]{0:T(1024)} %pad_clamp_fusion), kind=kCustom, calls=%fused_computation.7.clone | custom fusion | bytes 1572872 | tf_op jit(solution)/shard_map/jit(_take)/gather | solution.py:107
  58.1 0.2 bitcast_dynamic-update-slice_fusion.7
  58.3 0.2 bitcast_dynamic-update-slice_fusion.6
  58.5 0.7 copy-done.5
  59.2 0.2 bitcast_dynamic-update-slice_fusion.5
  59.4 0.2 bitcast_dynamic-update-slice_fusion.4
  59.7 0.2 bitcast_dynamic-update-slice_fusion.3
  59.9 0.2 bitcast_dynamic-update-slice_fusion.2
  60.1 0.4 copy-done.8
  60.5 0.2 bitcast_dynamic-update-slice_fusion.1
  60.7 0.2 bitcast_dynamic-update-slice_fusion
  60.9 2.3 %fusion.30 = (bf16[1,2,8,64,1536]{4,3,0,1,2:T(8,128)(2,1)S(1)}, bf16[1,2,8,64,1536]{4,3,0,1,2:T(8,128)(2,1)}) fusion(bf16[2,2,8,64,1536]{4,3,0,1,2:T(8,128)(2,1)S(1)} %bitcast_dynamic-update-slice_fusion), kind=kLoop, calls=%fused_computation.87 | loop fusion | bytes 12582912 | tf_op jit(solution)/shard_map/slice | solution.py:52
  63.2 0.3 copy.64
  63.4 3.8 %reshape_squeeze.14 = bf16[2,512,12,128]{3,2,1,0:T(8,128)(2,1)} reshape(bf16[1,2,8,64,1536]{4,3,2,1,0:T(8,128)(2,1)S(1)} %copy.64) | data formatting | bytes 6291456 | tf_op jit(solution)/shard_map/reshape;squeeze | solution.py:52
  67.3 1.8 %pad_maximum_fusion = bf16[2,384,1536]{1,2,0:T(8,128)(2,1)S(1)} fusion(bf16[2,128,1536]{1,2,0:T(8,128)(2,1)} %collective-permute-done.1, bf16[1,128,1536]{1,2,0:T(8,128)(2,1)} %bitcast.117, bf16[1,128,1536]{1,2,0:T(8,128)(2,1)S(1)} %bitcast.115, bf16[2,128,1536]{1,2,0:T(8,128)(2,1)} %collective-permute-done), kind=kLoop, calls=%fused_computation.19 | loop fusion | flops 9437184 | bytes 4718592 | tf_op jit(solution)/shard_map/concatenate | solution.py:20
  69.1 0.2 fusion.31
  69.4 1.9 %copy-done.1 = bf16[2,512,12,128]{3,2,1,0:T(8,128)(2,1)S(1)} copy-done((bf16[2,512,12,128]{3,2,1,0:T(8,128)(2,1)S(1)}, bf16[2,512,12,128]{3,2,1,0:T(8,128)(2,1)}, u32[]{:S(2)}) %copy-start.1) | copy-done | bytes 3145752
  71.4 3.8 %bitcast_reduce_fusion = (f32[2,12,64]{2,1,0:T(8,128)S(1)}, f32[2,12,512,64]{2,3,1,0:T(8,128)}) fusion(pred[512]{0:T(512)(128)(4,1)S(1)} %copy-done.24, bf16[2,64,12,128]{3,2,1,0:T(8,128)(2,1)S(1)} %copy-done.10, bf16[2,512,12,128]{3,2,1,0:T(8,128)(2,1)S(1)} %copy-done.1), kind=kOutput, calls=%fused_computation.9 | convolution fusion | flops 203684352 | bytes 6691328 | tf_op jit(solution)/shard_map/bqhd,bkhd->bhqk/dot_general | solution.py:60
  75.2 0.5 fusion.32
  75.8 0.3 bitcast_reduce_fusion.1
  76.2 1.4 %fusion.8 = f32[2,12,64]{2,0,1:T(2,128)} fusion(f32[12,384,2,64]{1,3,2,0:T(8,128)S(1)} %bitcast.101, f32[2,12,64]{2,0,1:T(2,128)S(1)} %copy_maximum_fusion, pred[384]{0:T(512)(128)(4,1)S(1)} %copy-done.21), kind=kLoop, calls=%fused_computation.24 | loop fusion | flops 2357760 | bytes 2371968 | tf_op jit(solution)/shard_map/reduce_sum | solution.py:67
  77.6 0.6 copy.70
  78.2 2.0 %copy.69 = bf16[1,2,8,64,1536]{4,3,2,1,0:T(8,128)(2,1)} copy(bf16[1,2,8,64,1536]{4,3,0,1,2:T(8,128)(2,1)S(1)} %copy-done) | data formatting | bytes 6291456 | tf_op jit(solution)/shard_map/slice | solution.py:53
  80.2 6.9 %reshape_squeeze.15 = bf16[2,512,12,128]{3,2,1,0:T(8,128)(2,1)} reshape(bf16[1,2,8,64,1536]{4,3,2,1,0:T(8,128)(2,1)} %copy.69) | data formatting | bytes 6291456 | tf_op jit(solution)/shard_map/reshape;squeeze | solution.py:53
  87.0 3.0 %fusion.5 = (f32[2,12,64]{2,1,0:T(8,128)S(1)}, bf16[2,12,64,512]{3,2,1,0:T(8,128)(2,1)S(1)}) fusion(f32[2,12,512,64]{2,3,1,0:T(8,128)} %get-tuple-element.21, f32[2,12,64]{2,1,0:T(8,128)} %copy.70, pred[512]{0:T(512)(128)(4,1)} %reshape.45), kind=kLoop, calls=%fused_computation.17 | loop fusion | flops 3930624 | bytes 4731392 | tf_op jit(solution)/shard_map/reduce_sum | solution.py:67
  90.2 1.8 %fusion.11 = f32[2,64,12,128]{3,1,0,2:T(8,128)S(1)} fusion(bf16[2,512,12,128]{3,2,1,0:T(8,128)(2,1)S(1)} %copy-done.2, bf16[2,12,64,512]{3,2,1,0:T(8,128)(2,1)S(1)} %get-tuple-element.17), kind=kOutput, calls=%fused_computation.27 | convolution fusion | flops 201326592 | bytes 5505024 | tf_op jit(solution)/shard_map/bhqk,bkhd->bqhd/dot_general | solution.py:74
  92.0 0.9 fusion.18
  93.0 0.3 copy.74
  93.3 1.6 %convolution_convert_fusion = bf16[128,1536]{1,0:T(8,128)(2,1)} fusion(bf16[1536,1536]{1,0:T(8,128)(2,1)S(1)} %bitcast.112, bf16[16,8,12,128]{3,2,1,0:T(8,128)(2,1)S(1)} %bitcast.118), kind=kOutput, calls=%fused_computation.16 | convolution fusion | flops 604176384 | bytes 5505024 | tf_op jit(solution)/shard_map/dot_general | solution.py:85
  (70 shorter events, 0.8 us)
Async XLA Ops:
  0.0 16.8 %copy-start.13 = (s32[2,8]{1,0:T(2,128)S(1)}, s32[2,8]{1,0:T(2,128)}, u32[]{:S(2)}) copy-start(s32[2,8]{1,0:T(2,128)} %param.10) | copy-start | bytes 196
  0.0 21.5 %copy-start.12 = (bf16[128,1536]{1,0:T(8,128)(2,1)S(1)}, bf16[128,1536]{1,0:T(8,128)(2,1)}, u32[]{:S(2)}) copy-start(bf16[128,1536]{1,0:T(8,128)(2,1)} %param.7) | copy-start | bytes 1179652
  2.5 41.0 %copy-start.3 = (bf16[128,1536]{0,1:T(8,128)(2,1)}, bf16[128,1536]{0,1:T(8,128)(2,1)S(1)}, u32[]{:S(2)}) copy-start(bf16[128,1536]{0,1:T(8,128)(2,1)S(1)} %copy.57) | copy-start | bytes 1179652
  3.5 40.0 %collective-permute-start.2 = (bf16[2,128,1536]{1,2,0:T(8,128)(2,1)}, bf16[2,128,1536]{1,2,0:T(8,128)(2,1)S(1)}, u32[]{:S(2)}, u32[]{:S(2)}) collective-permute-start(bf16[2,128,1536]{1,2,0:T(8,128)(2,1)} %pad_maximum_fusion.1), channel_id=1, source_target_pairs={{0,2},{1,3},{2,4},{3,5},{4,6},{5,7},{6,8},{7,9},{8,10},{9,11},{10,... | collective-permute-start | bytes 2359304 | tf_op jit(solution)/shard_map/ppermute | solution.py:34
  8.4 38.1 %collective-permute-start.3 = (bf16[2,128,1536]{1,2,0:T(8,128)(2,1)}, bf16[2,128,1536]{1,2,0:T(8,128)(2,1)S(1)}, u32[]{:S(2)}, u32[]{:S(2)}) collective-permute-start(bf16[2,128,1536]{1,2,0:T(8,128)(2,1)} %pad_maximum_fusion.1), channel_id=1, source_target_pairs={{0,4},{1,5},{2,6},{3,7},{4,8},{5,9},{6,10},{7,11},{8,12},{9,13},{1... | collective-permute-start | bytes 2359304 | tf_op jit(solution)/shard_map/ppermute | solution.py:34
  11.9 37.0 %collective-permute-start.4 = (bf16[2,128,1536]{1,2,0:T(8,128)(2,1)}, bf16[2,128,1536]{1,2,0:T(8,128)(2,1)}, u32[]{:S(2)}, u32[]{:S(2)}) collective-permute-start(bf16[2,128,1536]{1,2,0:T(8,128)(2,1)} %pad_maximum_fusion.1), channel_id=1, source_target_pairs={{2,0},{3,1},{4,2},{5,3},{6,4},{7,5},{8,6},{9,7},{10,8},{11,9},{12,... | collective-permute-start | bytes 2359304 | tf_op jit(solution)/shard_map/ppermute | solution.py:34
  13.2 40.1 %collective-permute-start.5 = (bf16[2,128,1536]{1,2,0:T(8,128)(2,1)}, bf16[2,128,1536]{1,2,0:T(8,128)(2,1)}, u32[]{:S(2)}, u32[]{:S(2)}) collective-permute-start(bf16[2,128,1536]{1,2,0:T(8,128)(2,1)} %pad_maximum_fusion.1), channel_id=1, source_target_pairs={{4,0},{5,1},{6,2},{7,3},{8,4},{9,5},{10,6},{11,7},{12,8},{13,9},{1... | collective-permute-start | bytes 2359304 | tf_op jit(solution)/shard_map/ppermute | solution.py:34
  14.5 52.8 %collective-permute-start = (bf16[2,128,1536]{1,2,0:T(8,128)(2,1)}, bf16[2,128,1536]{1,2,0:T(8,128)(2,1)}, u32[]{:S(2)}, u32[]{:S(2)}) collective-permute-start(bf16[2,128,1536]{1,2,0:T(8,128)(2,1)} %pad_maximum_fusion.1), channel_id=1, source_target_pairs={{0,1},{1,2},{2,3},{3,4},{4,5},{5,6},{6,7},{7,8},{8,9},{9,10},{10,1... | collective-permute-start | bytes 2359304 | tf_op jit(solution)/shard_map/ppermute | solution.py:22
  21.8 21.7 %copy-start.9 = (bf16[2,64,12,128]{3,2,1,0:T(8,128)(2,1)}, bf16[2,64,12,128]{3,2,1,0:T(8,128)(2,1)S(1)}, u32[]{:S(2)}) copy-start(bf16[2,64,12,128]{3,2,1,0:T(8,128)(2,1)S(1)} %reshape.44) | copy-start | bytes 1179652
  43.5 23.8 %collective-permute-start.1 = (bf16[2,128,1536]{1,2,0:T(8,128)(2,1)}, bf16[2,128,1536]{1,2,0:T(8,128)(2,1)}, u32[]{:S(2)}, u32[]{:S(2)}) collective-permute-start(bf16[2,128,1536]{1,2,0:T(8,128)(2,1)} %pad_maximum_fusion.1), channel_id=1, source_target_pairs={{1,0},{2,1},{3,2},{4,3},{5,4},{6,5},{7,6},{8,7},{9,8},{10,9},{11,1... | collective-permute-start | bytes 2359304 | tf_op jit(solution)/shard_map/ppermute | solution.py:24
  51.8 6.3 %copy-start.23 = (pred[2]{0:T(512)(128)(4,1)S(1)}, pred[2]{0:T(512)(128)(4,1)}, u32[]{:S(2)}) copy-start(pred[2]{0:T(512)(128)(4,1)} %compare_and_fusion.7) | copy-start | bytes 10
  53.3 5.0 %copy-start.20 = (pred[2]{0:T(512)(128)(4,1)S(1)}, pred[2]{0:T(512)(128)(4,1)}, u32[]{:S(2)}) copy-start(pred[2]{0:T(512)(128)(4,1)} %get-tuple-element.35) | copy-start | bytes 10
  54.7 3.8 %copy-start.19 = (pred[2]{0:T(512)(128)(4,1)S(1)}, pred[2]{0:T(512)(128)(4,1)}, u32[]{:S(2)}) copy-start(pred[2]{0:T(512)(128)(4,1)} %get-tuple-element.34) | copy-start | bytes 10
  56.4 3.1 %copy-start.18 = (pred[2]{0:T(512)(128)(4,1)S(1)}, pred[2]{0:T(512)(128)(4,1)}, u32[]{:S(2)}) copy-start(pred[2]{0:T(512)(128)(4,1)} %get-tuple-element.33) | copy-start | bytes 10
  58.1 1.1 %copy-start.5 = (bf16[2,2,64,1536]{3,2,1,0:T(8,128)(2,1)S(1)}, bf16[2,2,64,1536]{3,2,1,0:T(8,128)(2,1)}, u32[]{:S(2)}) copy-start(bf16[2,2,64,1536]{3,2,1,0:T(8,128)(2,1)} %gather_fusion.2) | copy-start | bytes 2359300
  58.1 1.6 %copy-start.7 = (bf16[2,2,64,1536]{3,2,1,0:T(8,128)(2,1)S(1)}, bf16[2,2,64,1536]{3,2,1,0:T(8,128)(2,1)}, u32[]{:S(2)}) copy-start(bf16[2,2,64,1536]{3,2,1,0:T(8,128)(2,1)} %gather_fusion.4) | copy-start | bytes 2359300
  58.1 1.6 %copy-start.17 = (pred[2]{0:T(512)(128)(4,1)S(1)}, pred[2]{0:T(512)(128)(4,1)}, u32[]{:S(2)}) copy-start(pred[2]{0:T(512)(128)(4,1)} %get-tuple-element.32) | copy-start | bytes 10
  58.3 1.6 %copy-start.4 = (bf16[2,2,64,1536]{3,2,1,0:T(8,128)(2,1)S(1)}, bf16[2,2,64,1536]{3,2,1,0:T(8,128)(2,1)}, u32[]{:S(2)}) copy-start(bf16[2,2,64,1536]{3,2,1,0:T(8,128)(2,1)} %gather_fusion.5) | copy-start | bytes 2359300
  58.3 1.6 %copy-start.16 = (pred[2]{0:T(512)(128)(4,1)S(1)}, pred[2]{0:T(512)(128)(4,1)}, u32[]{:S(2)}) copy-start(pred[2]{0:T(512)(128)(4,1)} %get-tuple-element.31) | copy-start | bytes 10
  59.2 1.3 %copy-start.8 = (bf16[2,2,64,1536]{3,2,1,0:T(8,128)(2,1)S(1)}, bf16[2,2,64,1536]{3,2,1,0:T(8,128)(2,1)}, u32[]{:S(2)}) copy-start(bf16[2,2,64,1536]{3,2,1,0:T(8,128)(2,1)} %gather_fusion.6) | copy-start | bytes 2359300
  59.2 1.3 %copy-start.15 = (pred[2]{0:T(512)(128)(4,1)S(1)}, pred[2]{0:T(512)(128)(4,1)}, u32[]{:S(2)}) copy-start(pred[2]{0:T(512)(128)(4,1)} %get-tuple-element.30) | copy-start | bytes 10
  59.4 1.2 %copy-start.6 = (bf16[2,2,64,1536]{3,2,1,0:T(8,128)(2,1)S(1)}, bf16[2,2,64,1536]{3,2,1,0:T(8,128)(2,1)}, u32[]{:S(2)}) copy-start(bf16[2,2,64,1536]{3,2,1,0:T(8,128)(2,1)} %gather_fusion.7) | copy-start | bytes 2359300
  59.4 1.2 %copy-start.22 = (pred[2]{0:T(512)(128)(4,1)S(1)}, pred[2]{0:T(512)(128)(4,1)}, u32[]{:S(2)}) copy-start(pred[2]{0:T(512)(128)(4,1)} %compare_and_fusion) | copy-start | bytes 10
  67.3 2.1 %copy-start.24 = (pred[512]{0:T(512)(128)(4,1)S(1)}, pred[512]{0:T(512)(128)(4,1)}, u32[]{:S(2)}) copy-start(pred[512]{0:T(512)(128)(4,1)} %reshape.45) | copy-start | bytes 1540
  69.1 2.2 %copy-start.1 = (bf16[2,512,12,128]{3,2,1,0:T(8,128)(2,1)S(1)}, bf16[2,512,12,128]{3,2,1,0:T(8,128)(2,1)}, u32[]{:S(2)}) copy-start(bf16[2,512,12,128]{3,2,1,0:T(8,128)(2,1)} %reshape_squeeze.14) | copy-start | bytes 9437188
  69.1 2.3 %copy-start.10 = (bf16[2,64,12,128]{3,2,1,0:T(8,128)(2,1)S(1)}, bf16[2,64,12,128]{3,2,1,0:T(8,128)(2,1)}, u32[]{:S(2)}) copy-start(bf16[2,64,12,128]{3,2,1,0:T(8,128)(2,1)} %copy-done.9) | copy-start | bytes 1179652
  71.4 3.8 %copy-start.11 = (bf16[2,64,12,128]{3,1,0,2:T(8,128)(2,1)S(1)}, bf16[2,64,12,128]{3,1,0,2:T(8,128)(2,1)}, u32[]{:S(2)}) copy-start(bf16[2,64,12,128]{3,1,0,2:T(8,128)(2,1)} %copy.59) | copy-start | bytes 1179652
  75.2 0.6 copy-start.21
  75.7 2.5 %copy-start = (bf16[1,2,8,64,1536]{4,3,0,1,2:T(8,128)(2,1)S(1)}, bf16[1,2,8,64,1536]{4,3,0,1,2:T(8,128)(2,1)}, u32[]{:S(2)}) copy-start(bf16[1,2,8,64,1536]{4,3,0,1,2:T(8,128)(2,1)} %get-tuple-element.15) | copy-start | bytes 9437188
  87.0 3.0 %copy-start.14 = (f32[2,12,64]{2,0,1:T(2,128)S(1)}, f32[2,12,64]{2,0,1:T(2,128)}, u32[]{:S(2)}) copy-start(f32[2,12,64]{2,0,1:T(2,128)} %fusion.8) | copy-start | bytes 18436
  87.0 3.2 %copy-start.2 = (bf16[2,512,12,128]{3,2,1,0:T(8,128)(2,1)S(1)}, bf16[2,512,12,128]{3,2,1,0:T(8,128)(2,1)}, u32[]{:S(2)}) copy-start(bf16[2,512,12,128]{3,2,1,0:T(8,128)(2,1)} %reshape_squeeze.15) | copy-start | bytes 9437188
  90.2 3.1 %slice-start = ((s8[4718592]{0:T(1024)(128)(4,1)}), s8[4194304]{0:T(1024)(128)(4,1)S(1)}, s32[]{:S(2)}) async-start(s8[4718592]{0:T(1024)(128)(4,1)} %bitcast.111), calls=%async_computation | async-start | bytes 8388608
  92.0 1.3 %slice-start.1 = ((s8[4718592]{0:T(1024)(128)(4,1)}), s8[524288]{0:T(1024)(128)(4,1)S(1)}, s32[]{:S(2)}) async-start(s8[4718592]{0:T(1024)(128)(4,1)} %bitcast.111), calls=%async_computation.1 | async-start | bytes 1048576
where the time goes:
time: 96.2 us; the launch traced here: 94.8 us
  local copies, waits for them, and re-layouts  38.3 us (40%)
  waiting for transfers between devices  18.5 us (19%)
  other arithmetic  14.5 us (15%)
  starting transfers between devices  14.5 us (15%)
  matrix products  8.6 us (9%)
    ppermute x4, waiting for transfers between devices, shifted(): return lax.ppermute(block, axis, route)  18.5 us
    ppermute x4, starting transfers between devices, shifted(): return lax.ppermute(block, axis, route)  11 us
    gather x8, local copies, waits for them, and re-layouts, body(): chosen_list.append(jnp.take(source, far_picks[:, column], axis=1))  9.84 us
    another operation x1, local copies, waits for them, and re-layouts, attend(): far_values = far_pair[1].reshape(blocks, -1, HEADS, HEAD_DIM)  6.86 us
    unnamed x56, local copies, waits for them, and re-layouts  5.89 us
    reduce_sum x2, other arithmetic, attend(): total = jnp.sum(near_exp, -1) + jnp.sum(far_exp, -1)  4.42 us
    another operation x1, local copies, waits for them, and re-layouts, attend(): far_keys = far_pair[0].reshape(blocks, -1, HEADS, HEAD_DIM)  3.84 us
    dot_general x1, matrix products, attend(): jnp.einsum('bqhd,bkhd->bhqk', query_heads, far_keys, preferred_element_ty...  3.81 us
  transfers between devices with their start and end apart: 6, of which 1 were waited for; matrix products, arithmetic and copies ran while one was open for 31% of the time, Pallas kernels for 0%

commit v1 on v0

v1 whole, which is shorter than its diff:
```python
import functools
import math

import jax
import jax.numpy as jnp
from jax import lax
from jax.experimental import pallas as pl
from jax.experimental.pallas import tpu as pltpu
from jax.sharding import PartitionSpec as P

HEAD_DIM = 128
BLK = 64
LEVELS = 2
PICKS = 2
FAR = 8
SCALE = HEAD_DIM ** (-0.5) * math.log2(math.e)
UNUSED = -1e30

VMEM = pl.BlockSpec(memory_space=pltpu.VMEM)
SMEM = pl.BlockSpec(memory_space=pltpu.SMEM)
ANY = pl.BlockSpec(memory_space=pl.ANY)
NT = (((1,), (1,)), ((), ()))


def column_offset(column):
    magnitude = 2 ** (1 + column // PICKS % LEVELS)
    return -magnitude if column < FAR // 2 else magnitude


def head_columns(head):
    return pl.ds(head * HEAD_DIM, HEAD_DIM)


def far_bias(picks_ref, device, offset, count, rows):
    usable = (device + offset >= 0) & (device + offset < count)
    lane = lax.broadcasted_iota(jnp.int32, (BLK, rows), 1)
    parts = []
    for block in range(rows // BLK):
        bias = jnp.full((BLK, rows), UNUSED, jnp.float32)
        for local in range(rows // BLK):
            named = jnp.int32(0)
            for column in range(FAR):
                hit = (picks_ref[block, column] == local) & (offset == column_offset(column))
                named = named + jnp.where(hit, 1, 0)
            named = jnp.where(usable, named, 0)
            value = jnp.where(named == 0, jnp.float32(UNUSED), (named - 1).astype(jnp.float32))
            bias = jnp.where(lane // BLK == local, value, bias)
        parts.append(bias)
    return jnp.concatenate(parts, axis=0)


def pack_kernel(keys_ref, values_ref, pair_ref, sems):
    first = pltpu.make_async_copy(keys_ref, pair_ref.at[0], sems.at[0])
    second = pltpu.make_async_copy(values_ref, pair_ref.at[1], sems.at[1])
    first.start()
    second.start()
    first.wait()
    second.wait()


def pack(keys, values):
    return pl.pallas_call(
        pack_kernel,
        out_shape=jax.ShapeDtypeStruct((2,) + keys.shape, keys.dtype),
        in_specs=[ANY, ANY],
        out_specs=VMEM,
        scratch_shapes=[pltpu.SemaphoreType.DMA((2,))],
        name="pack",
    )(keys, values)


def choose_kernel(index_ref, ends_ref, inner_ref, out_ref):
    place = lax.rem(index_ref[0], 4)
    ends = (place == 0) | (place == 3)

    @pl.when(ends)
    def _():
        out_ref[...] = ends_ref[...]

    @pl.when(jnp.logical_not(ends))
    def _():
        out_ref[...] = inner_ref[...]


def choose(index, ends, inner):
    return pl.pallas_call(
        choose_kernel,
        out_shape=jax.ShapeDtypeStruct(ends.shape, ends.dtype),
        in_specs=[SMEM, VMEM, VMEM],
        out_specs=VMEM,
        name="choose",
    )(index, ends, inner)


def first_kernel(
    count, index_ref, picks_ref, q_ref, own_ref, s0_ref, s1_ref, x1_ref, za_ref, zb_ref, acc_ref, top_ref, total_ref
):
    rows, width = q_ref.shape
    device = index_ref[0]
    sign = 1 - 2 * lax.rem(device, 2)
    shards = (own_ref, s0_ref, s1_ref, x1_ref, za_ref, zb_ref)
    outer = device - sign
    outer_bias = jnp.where((outer >= 0) & (outer < count), jnp.float32(0), jnp.float32(UNUSED))
    far = [far_bias(picks_ref, device, offset * sign, count, rows) for offset in (2, -4, 4)]
    for head in range(width // HEAD_DIM):
        cols = head_columns(head)
        queries = q_ref[:, cols]
        keys = jnp.concatenate([shard[0, :, cols] for shard in shards], axis=0)
        values = jnp.concatenate([shard[1, :, cols] for shard in shards], axis=0)
        scores = lax.dot_general(queries, keys, NT, preferred_element_type=jnp.float32) * SCALE
        parts = [scores[:, i * rows:(i + 1) * rows] for i in range(len(shards))]
        parts[2] = parts[2] + outer_bias
        for i in range(3):
            parts[3 + i] = parts[3 + i] + far[i]
        top = functools.reduce(jnp.maximum, parts)
        top = jnp.max(top, axis=1, keepdims=True)
        exps = [jnp.exp2(part - top) for part in parts]
        total = jnp.sum(functools.reduce(jnp.add, exps), axis=1, keepdims=True)
        weights = jnp.concatenate([e.astype(jnp.bfloat16) for e in exps], axis=1)
        acc_ref[:, cols] = jnp.dot(weights, values, preferred_element_type=jnp.float32)
        top_ref[head] = top
        total_ref[head] = total


def first(count, index, picks, queries, *shards):
    rows, width = queries.shape
    heads = width // HEAD_DIM
    column = jax.ShapeDtypeStruct((heads, rows, 1), jnp.float32)
    return pl.pallas_call(
        functools.partial(first_kernel, count),
        out_shape=(jax.ShapeDtypeStruct((rows, width), jnp.float32), column, column),
        in_specs=[SMEM, SMEM] + [VMEM] * 7,
        out_specs=(VMEM, VMEM, VMEM),
        compiler_params=pltpu.CompilerParams(vmem_limit_bytes=24 * 1024 * 1024),
        name="first",
    )(index, picks, queries, *shards)


def last_kernel(
    count, index_ref, picks_ref, q_ref, acc_ref, top_ref, total_ref, pair_ref, weight_ref, out_ref, attended_ref
):
    rows, width = q_ref.shape
    device = index_ref[0]
    sign = 1 - 2 * lax.rem(device, 2)
    bias = far_bias(picks_ref, device, -2 * sign, count, rows)
    for head in range(width // HEAD_DIM):
        cols = head_columns(head)
        scores = lax.dot_general(q_ref[:, cols], pair_ref[0, :, cols], NT, preferred_element_type=jnp.float32)
        scores = scores * SCALE + bias
        before = top_ref[head]
        top = jnp.maximum(before, jnp.max(scores, axis=1, keepdims=True))
        kept = jnp.exp2(before - top)
        exps = jnp.exp2(scores - top)
        total = total_ref[head] * kept + jnp.sum(exps, axis=1, keepdims=True)
        summed = acc_ref[:, cols] * kept + jnp.dot(
            exps.astype(jnp.bfloat16), pair_ref[1, :, cols], preferred_element_type=jnp.float32
        )
        attended_ref[:, cols] = (summed / total).astype(jnp.bfloat16)
    out_ref[...] = jnp.dot(attended_ref[...], weight_ref[...], preferred_element_type=jnp.float32).astype(jnp.bfloat16)


def last(count, index, picks, queries, acc, top, total, pair, weight):
    rows, width = queries.shape
    return pl.pallas_call(
        functools.partial(last_kernel, count),
        out_shape=jax.ShapeDtypeStruct((rows, width), jnp.bfloat16),
        in_specs=[SMEM, SMEM] + [VMEM] * 6,
        out_specs=VMEM,
        scratch_shapes=[pltpu.VMEM((rows, width), jnp.bfloat16)],
        compiler_params=pltpu.CompilerParams(vmem_limit_bytes=24 * 1024 * 1024),
        name="last",
    )(index, picks, queries, acc, top, total, pair, weight)


def moved(block, steps):
    count = lax.axis_size("tm")
    route = [(i, i + steps[i % 4]) for i in range(count)]
    return lax.ppermute(block, "tm", [(i, j) for i, j in route if 0 <= j < count])


def body(queries, keys, values, far_picks, out_weight):
    count = lax.axis_size("tm")
    index = lax.axis_index("tm").astype(jnp.int32).reshape(1)
    pair = pack(keys, values)
    x1 = moved(pair, (-2, 2, -2, 2))
    za = moved(pair, (4, -4, 4, -4))
    zb = moved(pair, (-4, 4, -4, 4))
    s0 = moved(pair, (1, -1, 1, -1))
    ahead = moved(choose(index, x1, s0), (4, 1, -1, -4))
    s1 = moved(x1, (1, -1, 1, -1))
    state = first(count, index, far_picks, queries, pair, s0, s1, x1, za, zb)
    return last(count, index, far_picks, queries, *state, ahead, out_weight)


def solution(mesh):
    placed = (
        P(("vid", "tm"), None),
        P(("vid", "tm"), None),
        P(("vid", "tm"), None),
        P(("vid", "tm"), None),
        P(),
    )
    return jax.shard_map(
        body, mesh=mesh, in_specs=placed, out_specs=P(("vid", "tm"), None), check_vma=False
    )
```

time: 96.2 us -> 52 us (0.54)
  local copies, waits for them, and re-layouts: 38.3 us -> 5.97 us
  Pallas kernels: 0 us -> 15.3 us
  other arithmetic: 14.5 us -> 0 us
  waiting for transfers between devices: 18.5 us -> 7.05 us
  starting transfers between devices: 14.5 us -> 23.1 us
  matrix products: 8.6 us -> 0 us
    pallas_call x0 -> x4, Pallas kernels: none -> 15.3 us  [the longest x1 5.95 us: last(): pl.pallas_call(functools.partial(last_kernel, count), out_shape=jax.Shape...]
    ppermute x6, waiting for transfers between devices: 18.5 us -> 7.05 us  [moved(): lax.ppermute(block, 'tm', [(i, j) for i, j in route if 0 <= j < count])]
    another operation x3 -> x0, local copies, waits for them, and re-layouts: 10.8 us -> none  [the longest x1 6.86 us: attend(): far_values = far_pair[1].reshape(blocks, -1, HEADS, HEAD_DIM)]
    gather x8 -> x0, local copies, waits for them, and re-layouts: 9.84 us -> none  [body(): chosen_list.append(jnp.take(source, far_picks[:, column], axis=1))]
    ppermute x6, starting transfers between devices: 14.5 us -> 23.1 us  [moved(): lax.ppermute(block, 'tm', [(i, j) for i, j in route if 0 <= j < count])]
    dot_general x4 -> x0, matrix products: 8.13 us -> none  [the longest x1 3.81 us: attend(): jnp.einsum('bqhd,bkhd->bhqk', query_heads, far_keys, preferred_element_ty...]
    slice x5 -> x0, local copies, waits for them, and re-layouts: 5.01 us -> none  [the longest x2 2.54 us: attend(): far_keys = far_pair[0].reshape(blocks, -1, HEADS, HEAD_DIM)]
    reduce_sum x2 -> x0, other arithmetic: 4.42 us -> none  [attend(): total = jnp.sum(near_exp, -1) + jnp.sum(far_exp, -1)]
  transfers between devices with their start and end apart: 6 -> 6, of which waited for: 1 -> 2; matrix products, arithmetic and copies ran while one was open for 31% -> 0% of each run, Pallas kernels for 0% -> 14%
where the time goes in v1:
time: 52 us; the launch traced here: 51.5 us
  starting transfers between devices  23.1 us (44%)
  Pallas kernels  15.3 us (29%)
  waiting for transfers between devices  7.05 us (14%)
  local copies, waits for them, and re-layouts  5.97 us (11%)
    ppermute x6, starting transfers between devices, moved(): lax.ppermute(block, 'tm', [(i, j) for i, j in route if 0 <= j < count])  23.1 us
    ppermute x6, waiting for transfers between devices, moved(): lax.ppermute(block, 'tm', [(i, j) for i, j in route if 0 <= j < count])  7.05 us
    unnamed x16, local copies, waits for them, and re-layouts  5.97 us
    pallas_call x1, Pallas kernels, last(): pl.pallas_call(functools.partial(last_kernel, count), out_shape=jax.Shape...  5.95 us
    pallas_call x1, Pallas kernels, first(): pl.pallas_call(functools.partial(first_kernel, count), out_shape=(jax.Sha...  5 us
    pallas_call x1, Pallas kernels, choose(): pl.pallas_call(choose_kernel, out_shape=jax.ShapeDtypeStruct(ends.shape,...  2.3 us
    pallas_call x1, Pallas kernels, pack(): pl.pallas_call(pack_kernel, out_shape=jax.ShapeDtypeStruct((2,) + keys.sh...  2.04 us
  transfers between devices with their start and end apart: 6, of which 2 were waited for; matrix products, arithmetic and copies ran while one was open for 0% of the time, Pallas kernels for 14%

profile of v1, /device:TPU:0, one launch (start us, length us, event | category | flops | bytes accessed | tf_op | source)
XLA Modules:
  0.0 51.5 jit_solution(13988191119469701154)
XLA Ops:
  0.0 2.0 %pack.1.own_ref = bf16[2,128,1536]{2,1,0:T(8,128)(2,1)} custom-call(bf16[128,1536]{1,0:T(8,128)(2,1)} %keys_ref.1, bf16[128,1536]{1,0:T(8,128)(2,1)} %values_ref.1), custom_call_target="tpu_custom_call" | custom-call | tf_op jit(solution)/shard_map/pack/pallas_call | solution.py:62
  2.0 1.3 %collective-permute-start.1 = (bf16[2,128,1536]{2,1,0:T(8,128)(2,1)}, bf16[2,128,1536]{2,1,0:T(8,128)(2,1)S(1)}, u32[]{:S(2)}, u32[]{:S(2)}) collective-permute-start(bf16[2,128,1536]{2,1,0:T(8,128)(2,1)} %pack.1.own_ref), channel_id=1, source_target_pairs={{1,3},{2,0},{3,5},{4,2},{5,7},{6,4},{7,9},{8,6},{9,11},{10,8},{11,... | collective-permute-start | bytes 2359304 | tf_op jit(solution)/shard_map/ppermute | solution.py:178
  3.3 3.2 %collective-permute-start = (bf16[2,128,1536]{2,1,0:T(8,128)(2,1)}, bf16[2,128,1536]{2,1,0:T(8,128)(2,1)S(1)}, u32[]{:S(2)}, u32[]{:S(2)}) collective-permute-start(bf16[2,128,1536]{2,1,0:T(8,128)(2,1)} %pack.1.own_ref), channel_id=1, source_target_pairs={{0,1},{1,0},{2,3},{3,2},{4,5},{5,4},{6,7},{7,6},{8,9},{9,8},{10,11... | collective-permute-start | bytes 2359304 | tf_op jit(solution)/shard_map/ppermute | solution.py:178
  6.6 1.3 %collective-permute-start.4 = (bf16[2,128,1536]{2,1,0:T(8,128)(2,1)}, bf16[2,128,1536]{2,1,0:T(8,128)(2,1)S(1)}, u32[]{:S(2)}, u32[]{:S(2)}) collective-permute-start(bf16[2,128,1536]{2,1,0:T(8,128)(2,1)} %pack.1.own_ref), channel_id=1, source_target_pairs={{1,5},{3,7},{4,0},{5,9},{6,2},{7,11},{8,4},{9,13},{10,6},{11,15},{... | collective-permute-start | bytes 2359304 | tf_op jit(solution)/shard_map/ppermute | solution.py:178
  7.9 4.6 %collective-permute-start.3 = (bf16[2,128,1536]{2,1,0:T(8,128)(2,1)}, bf16[2,128,1536]{2,1,0:T(8,128)(2,1)S(1)}, u32[]{:S(2)}, u32[]{:S(2)}) collective-permute-start(bf16[2,128,1536]{2,1,0:T(8,128)(2,1)} %pack.1.own_ref), channel_id=1, source_target_pairs={{0,4},{2,6},{4,8},{5,1},{6,10},{7,3},{8,12},{9,5},{10,14},{11,7},{... | collective-permute-start | bytes 2359304 | tf_op jit(solution)/shard_map/ppermute | solution.py:178
  12.5 4.6 %collective-permute-done.1.x1_ref.ends_ref = bf16[2,128,1536]{2,1,0:T(8,128)(2,1)S(1)} collective-permute-done((bf16[2,128,1536]{2,1,0:T(8,128)(2,1)}, bf16[2,128,1536]{2,1,0:T(8,128)(2,1)S(1)}, u32[]{:S(2)}, u32[]{:S(2)}) %collective-permute-start.1) | collective-permute-done | bytes 786464 | tf_op jit(solution)/shard_map/ppermute | solution.py:178
  17.1 0.0 copy-start.1
  17.1 7.0 %collective-permute-start.2 = (bf16[2,128,1536]{2,1,0:T(8,128)(2,1)S(1)}, bf16[2,128,1536]{2,1,0:T(8,128)(2,1)}, u32[]{:S(2)}, u32[]{:S(2)}) collective-permute-start(bf16[2,128,1536]{2,1,0:T(8,128)(2,1)S(1)} %collective-permute-done.1.x1_ref.ends_ref), channel_id=1, source_target_pairs={{0,1},{1,0},{2,3},{3,2},{4,5},{5,4},{6,7},{7,6},{8,9},{9,8},{10,11... | collective-permute-start | bytes 2359304 | tf_op jit(solution)/shard_map/ppermute | solution.py:178
  24.1 0.0 collective-permute-done.s0_ref.inner_ref
  24.1 0.0 copy-start.3
  24.1 0.0 copy-done.1
  24.2 0.9 %copy-done.3 = bf16[2,128,1536]{2,1,0:T(8,128)(2,1)} copy-done((bf16[2,128,1536]{2,1,0:T(8,128)(2,1)}, bf16[2,128,1536]{2,1,0:T(8,128)(2,1)S(1)}, u32[]{:S(2)}) %copy-start.3) | copy-done | bytes 786456
  25.0 2.3 %choose.1 = bf16[2,128,1536]{2,1,0:T(8,128)(2,1)} custom-call(s32[1]{0:T(128)} %bitcast.index_ref, bf16[2,128,1536]{2,1,0:T(8,128)(2,1)} %copy-done.1, bf16[2,128,1536]{2,1,0:T(8,128)(2,1)} %copy-done.3), custom_call_target="tpu_custom_call" | custom-call | tf_op jit(solution)/shard_map/choose/pallas_call | solution.py:86
  27.3 0.0 copy-start
  27.3 5.7 %collective-permute-start.5 = (bf16[2,128,1536]{2,1,0:T(8,128)(2,1)}, bf16[2,128,1536]{2,1,0:T(8,128)(2,1)S(1)}, u32[]{:S(2)}, u32[]{:S(2)}) collective-permute-start(bf16[2,128,1536]{2,1,0:T(8,128)(2,1)} %choose.1), channel_id=1, source_target_pairs={{0,4},{1,2},{2,1},{4,8},{5,6},{6,5},{7,3},{8,12},{9,10},{10,9},{11... | collective-permute-start | bytes 2359304 | tf_op jit(solution)/shard_map/ppermute | solution.py:178
  33.0 2.4 %collective-permute-done.4.zb_ref = bf16[2,128,1536]{2,1,0:T(8,128)(2,1)S(1)} collective-permute-done((bf16[2,128,1536]{2,1,0:T(8,128)(2,1)}, bf16[2,128,1536]{2,1,0:T(8,128)(2,1)S(1)}, u32[]{:S(2)}, u32[]{:S(2)}) %collective-permute-start.4) | collective-permute-done | bytes 786464 | tf_op jit(solution)/shard_map/ppermute | solution.py:178
  35.4 0.0 collective-permute-done.3.za_ref
  35.4 0.0 collective-permute-done.2.s1_ref
  35.5 0.0 copy-start.2
  35.5 1.1 %copy-done.2 = bf16[2,128,1536]{2,1,0:T(8,128)(2,1)S(1)} copy-done((bf16[2,128,1536]{2,1,0:T(8,128)(2,1)S(1)}, bf16[2,128,1536]{2,1,0:T(8,128)(2,1)}, u32[]{:S(2)}) %copy-start.2) | copy-done | bytes 786456
  36.6 0.0 copy-start.4
  36.6 1.1 %copy-done.4 = bf16[2,128,1536]{2,1,0:T(8,128)(2,1)S(1)} copy-done((bf16[2,128,1536]{2,1,0:T(8,128)(2,1)S(1)}, bf16[2,128,1536]{2,1,0:T(8,128)(2,1)}, u32[]{:S(2)}) %copy-start.4) | copy-done | bytes 786456
  37.7 0.0 copy-start.5
  37.7 1.1 %copy-done.5 = bf16[2,128,1536]{2,1,0:T(8,128)(2,1)S(1)} copy-done((bf16[2,128,1536]{2,1,0:T(8,128)(2,1)S(1)}, bf16[2,128,1536]{2,1,0:T(8,128)(2,1)}, u32[]{:S(2)}) %copy-start.5) | copy-done | bytes 786456
  38.9 0.0 copy-start.6
  38.9 1.0 %copy-done.6 = bf16[128,1536]{1,0:T(8,128)(2,1)S(1)} copy-done((bf16[128,1536]{1,0:T(8,128)(2,1)S(1)}, bf16[128,1536]{1,0:T(8,128)(2,1)}, u32[]{:S(2)}) %copy-start.6) | copy-done | bytes 393240
  39.9 0.0 copy-start.7
  39.9 0.7 %copy-done.7 = s32[2,8]{1,0:T(2,128)S(1)} copy-done((s32[2,8]{1,0:T(2,128)S(1)}, s32[2,8]{1,0:T(2,128)}, u32[]{:S(2)}) %copy-start.7) | copy-done | bytes 88
  40.5 5.0 %first.1 = (f32[128,1536]{1,0:T(8,128)S(1)}, f32[12,128,1]{2,1,0:T(8,128)S(1)}, f32[12,128,1]{2,1,0:T(8,128)S(1)}) custom-call(s32[1]{0:T(128)} %bitcast.index_ref, s32[2,8]{1,0:T(2,128)S(1)} %copy-done.7, bf16[128,1536]{1,0:T(8,128)(2,1)S(1)} %copy-done.6, bf16[2,128,1536]{2,1,0:T(8,128)(2,1)S(1)} %copy-done.5, bf16[2,128,1536]{2,1,0:T(8,128)(2,1)S(1)} %copy-done.4, ...), custom_call_target="tpu_custom_call" | custom-call | tf_op jit(solution)/shard_map/first/pallas_call | solution.py:129
  45.5 0.0 collective-permute-done.5.pair_ref
  45.5 0.0 copy-done
  45.6 6.0 %last.1 = bf16[128,1536]{1,0:T(8,128)(2,1)} custom-call(s32[1]{0:T(128)} %bitcast.index_ref, s32[2,8]{1,0:T(2,128)S(1)} %copy-done.7, bf16[128,1536]{1,0:T(8,128)(2,1)S(1)} %copy-done.6, f32[128,1536]{1,0:T(8,128)S(1)} %get-tuple-element.8.acc_ref, f32[12,128,1]{2,1,0:T(8,128)S(1)} %get-tuple-element.9.top_ref, ...), custom_call_target="tpu_custom_call" | custom-call | tf_op jit(solution)/shard_map/last/pallas_call | solution.py:164
Async XLA Ops:
  2.0 15.0 %collective-permute-start.1 = (bf16[2,128,1536]{2,1,0:T(8,128)(2,1)}, bf16[2,128,1536]{2,1,0:T(8,128)(2,1)S(1)}, u32[]{:S(2)}, u32[]{:S(2)}) collective-permute-start(bf16[2,128,1536]{2,1,0:T(8,128)(2,1)} %pack.1.own_ref), channel_id=1, source_target_pairs={{1,3},{2,0},{3,5},{4,2},{5,7},{6,4},{7,9},{8,6},{9,11},{10,8},{11,... | collective-permute-start | bytes 2359304 | tf_op jit(solution)/shard_map/ppermute | solution.py:178
  3.3 20.8 %collective-permute-start = (bf16[2,128,1536]{2,1,0:T(8,128)(2,1)}, bf16[2,128,1536]{2,1,0:T(8,128)(2,1)S(1)}, u32[]{:S(2)}, u32[]{:S(2)}) collective-permute-start(bf16[2,128,1536]{2,1,0:T(8,128)(2,1)} %pack.1.own_ref), channel_id=1, source_target_pairs={{0,1},{1,0},{2,3},{3,2},{4,5},{5,4},{6,7},{7,6},{8,9},{9,8},{10,11... | collective-permute-start | bytes 2359304 | tf_op jit(solution)/shard_map/ppermute | solution.py:178
  6.6 28.8 %collective-permute-start.4 = (bf16[2,128,1536]{2,1,0:T(8,128)(2,1)}, bf16[2,128,1536]{2,1,0:T(8,128)(2,1)S(1)}, u32[]{:S(2)}, u32[]{:S(2)}) collective-permute-start(bf16[2,128,1536]{2,1,0:T(8,128)(2,1)} %pack.1.own_ref), channel_id=1, source_target_pairs={{1,5},{3,7},{4,0},{5,9},{6,2},{7,11},{8,4},{9,13},{10,6},{11,15},{... | collective-permute-start | bytes 2359304 | tf_op jit(solution)/shard_map/ppermute | solution.py:178
  7.9 27.6 %collective-permute-start.3 = (bf16[2,128,1536]{2,1,0:T(8,128)(2,1)}, bf16[2,128,1536]{2,1,0:T(8,128)(2,1)S(1)}, u32[]{:S(2)}, u32[]{:S(2)}) collective-permute-start(bf16[2,128,1536]{2,1,0:T(8,128)(2,1)} %pack.1.own_ref), channel_id=1, source_target_pairs={{0,4},{2,6},{4,8},{5,1},{6,10},{7,3},{8,12},{9,5},{10,14},{11,7},{... | collective-permute-start | bytes 2359304 | tf_op jit(solution)/shard_map/ppermute | solution.py:178
  17.1 7.1 %copy-start.1 = (bf16[2,128,1536]{2,1,0:T(8,128)(2,1)}, bf16[2,128,1536]{2,1,0:T(8,128)(2,1)S(1)}, u32[]{:S(2)}) copy-start(bf16[2,128,1536]{2,1,0:T(8,128)(2,1)S(1)} %collective-permute-done.1.x1_ref.ends_ref) | copy-start | bytes 2359300
  17.1 18.4 %collective-permute-start.2 = (bf16[2,128,1536]{2,1,0:T(8,128)(2,1)S(1)}, bf16[2,128,1536]{2,1,0:T(8,128)(2,1)}, u32[]{:S(2)}, u32[]{:S(2)}) collective-permute-start(bf16[2,128,1536]{2,1,0:T(8,128)(2,1)S(1)} %collective-permute-done.1.x1_ref.ends_ref), channel_id=1, source_target_pairs={{0,1},{1,0},{2,3},{3,2},{4,5},{5,4},{6,7},{7,6},{8,9},{9,8},{10,11... | collective-permute-start | bytes 2359304 | tf_op jit(solution)/shard_map/ppermute | solution.py:178
  24.1 0.9 %copy-start.3 = (bf16[2,128,1536]{2,1,0:T(8,128)(2,1)}, bf16[2,128,1536]{2,1,0:T(8,128)(2,1)S(1)}, u32[]{:S(2)}) copy-start(bf16[2,128,1536]{2,1,0:T(8,128)(2,1)S(1)} %collective-permute-done.s0_ref.inner_ref) | copy-start | bytes 2359300
  27.3 18.2 %copy-start = (bf16[1536,1536]{1,0:T(8,128)(2,1)S(1)}, bf16[1536,1536]{1,0:T(8,128)(2,1)}, u32[]{:S(2)}) copy-start(bf16[1536,1536]{1,0:T(8,128)(2,1)} %weight_ref.1) | copy-start | bytes 14155780
  27.3 18.2 %collective-permute-start.5 = (bf16[2,128,1536]{2,1,0:T(8,128)(2,1)}, bf16[2,128,1536]{2,1,0:T(8,128)(2,1)S(1)}, u32[]{:S(2)}, u32[]{:S(2)}) collective-permute-start(bf16[2,128,1536]{2,1,0:T(8,128)(2,1)} %choose.1), channel_id=1, source_target_pairs={{0,4},{1,2},{2,1},{4,8},{5,6},{6,5},{7,3},{8,12},{9,10},{10,9},{11... | collective-permute-start | bytes 2359304 | tf_op jit(solution)/shard_map/ppermute | solution.py:178
  35.5 1.1 %copy-start.2 = (bf16[2,128,1536]{2,1,0:T(8,128)(2,1)S(1)}, bf16[2,128,1536]{2,1,0:T(8,128)(2,1)}, u32[]{:S(2)}) copy-start(bf16[2,128,1536]{2,1,0:T(8,128)(2,1)} %copy-done.1) | copy-start | bytes 2359300
  36.6 1.1 %copy-start.4 = (bf16[2,128,1536]{2,1,0:T(8,128)(2,1)S(1)}, bf16[2,128,1536]{2,1,0:T(8,128)(2,1)}, u32[]{:S(2)}) copy-start(bf16[2,128,1536]{2,1,0:T(8,128)(2,1)} %copy-done.3) | copy-start | bytes 2359300
  37.7 1.1 %copy-start.5 = (bf16[2,128,1536]{2,1,0:T(8,128)(2,1)S(1)}, bf16[2,128,1536]{2,1,0:T(8,128)(2,1)}, u32[]{:S(2)}) copy-start(bf16[2,128,1536]{2,1,0:T(8,128)(2,1)} %pack.1.own_ref) | copy-start | bytes 2359300
  38.9 1.0 %copy-start.6 = (bf16[128,1536]{1,0:T(8,128)(2,1)S(1)}, bf16[128,1536]{1,0:T(8,128)(2,1)}, u32[]{:S(2)}) copy-start(bf16[128,1536]{1,0:T(8,128)(2,1)} %q_ref.3) | copy-start | bytes 1179652
  39.9 0.7 %copy-start.7 = (s32[2,8]{1,0:T(2,128)S(1)}, s32[2,8]{1,0:T(2,128)}, u32[]{:S(2)}) copy-start(s32[2,8]{1,0:T(2,128)} %picks_ref.3) | copy-start | bytes 196

commit v2 on v1

--- a/solution.py
+++ b/solution.py
@@ -15,6 +15,7 @@
 FAR = 8
 SCALE = HEAD_DIM ** (-0.5) * math.log2(math.e)
 UNUSED = -1e30
+LEAD = 2
 
 VMEM = pl.BlockSpec(memory_space=pltpu.VMEM)
 SMEM = pl.BlockSpec(memory_space=pltpu.SMEM)
@@ -65,6 +66,7 @@
         in_specs=[ANY, ANY],
         out_specs=VMEM,
         scratch_shapes=[pltpu.SemaphoreType.DMA((2,))],
+        compiler_params=pltpu.CompilerParams(vmem_limit_bytes=4 * 1024 * 1024),
         name="pack",
     )(keys, values)
 
@@ -88,8 +90,19 @@
         out_shape=jax.ShapeDtypeStruct(ends.shape, ends.dtype),
         in_specs=[SMEM, VMEM, VMEM],
         out_specs=VMEM,
+        compiler_params=pltpu.CompilerParams(vmem_limit_bytes=4 * 1024 * 1024),
         name="choose",
     )(index, ends, inner)
+
+
+def staged(heads, score, soften, gather):
+    for step in range(heads + 2 * LEAD):
+        if step < heads:
+            score(step)
+        if 0 <= step - LEAD < heads:
+            soften(step - LEAD)
+        if 0 <= step - 2 * LEAD < heads:
+            gather(step - 2 * LEAD)
 
 
 def first_kernel(
@@ -102,36 +115,44 @@
     outer = device - sign
     outer_bias = jnp.where((outer >= 0) & (outer < count), jnp.float32(0), jnp.float32(UNUSED))
     far = [far_bias(picks_ref, device, offset * sign, count, rows) for offset in (2, -4, 4)]
-    for head in range(width // HEAD_DIM):
-        cols = head_columns(head)
-        queries = q_ref[:, cols]
+    scores, weights = {}, {}
+
+    def score(head):
+        cols = head_columns(head)
         keys = jnp.concatenate([shard[0, :, cols] for shard in shards], axis=0)
-        values = jnp.concatenate([shard[1, :, cols] for shard in shards], axis=0)
-        scores = lax.dot_general(queries, keys, NT, preferred_element_type=jnp.float32) * SCALE
-        parts = [scores[:, i * rows:(i + 1) * rows] for i in range(len(shards))]
+        scores[head] = lax.dot_general(q_ref[:, cols], keys, NT, preferred_element_type=jnp.float32)
+
+    def soften(head):
+        scaled = scores.pop(head) * SCALE
+        parts = [scaled[:, i * rows:(i + 1) * rows] for i in range(len(shards))]
         parts[2] = parts[2] + outer_bias
         for i in range(3):
             parts[3 + i] = parts[3 + i] + far[i]
-        top = functools.reduce(jnp.maximum, parts)
-        top = jnp.max(top, axis=1, keepdims=True)
+        top = jnp.max(functools.reduce(jnp.maximum, parts), axis=1, keepdims=True)
         exps = [jnp.exp2(part - top) for part in parts]
         total = jnp.sum(functools.reduce(jnp.add, exps), axis=1, keepdims=True)
-        weights = jnp.concatenate([e.astype(jnp.bfloat16) for e in exps], axis=1)
-        acc_ref[:, cols] = jnp.dot(weights, values, preferred_element_type=jnp.float32)
-        top_ref[head] = top
-        total_ref[head] = total
+        weights[head] = jnp.concatenate([e.astype(jnp.bfloat16) for e in exps], axis=1)
+        top_ref[head] = jnp.broadcast_to(top, top_ref.shape[1:])
+        total_ref[head] = jnp.broadcast_to(total, total_ref.shape[1:])
+
+    def gather(head):
+        cols = head_columns(head)
+        values = jnp.concatenate([shard[1, :, cols] for shard in shards], axis=0)
+        acc_ref[:, cols] = jnp.dot(weights.pop(head), values, preferred_element_type=jnp.float32)
+
+    staged(width // HEAD_DIM, score, soften, gather)
 
 
 def first(count, index, picks, queries, *shards):
     rows, width = queries.shape
     heads = width // HEAD_DIM
-    column = jax.ShapeDtypeStruct((heads, rows, 1), jnp.float32)
+    column = jax.ShapeDtypeStruct((heads, rows, HEAD_DIM), jnp.float32)
     return pl.pallas_call(
         functools.partial(first_kernel, count),
         out_shape=(jax.ShapeDtypeStruct((rows, width), jnp.float32), column, column),
         in_specs=[SMEM, SMEM] + [VMEM] * 7,
         out_specs=(VMEM, VMEM, VMEM),
-        compiler_params=pltpu.CompilerParams(vmem_limit_bytes=24 * 1024 * 1024),
+        compiler_params=pltpu.CompilerParams(vmem_limit_bytes=16 * 1024 * 1024),
         name="first",
     )(index, picks, queries, *shards)
 
@@ -143,19 +164,28 @@
     device = index_ref[0]
     sign = 1 - 2 * lax.rem(device, 2)
     bias = far_bias(picks_ref, device, -2 * sign, count, rows)
-    for head in range(width // HEAD_DIM):
-        cols = head_columns(head)
-        scores = lax.dot_general(q_ref[:, cols], pair_ref[0, :, cols], NT, preferred_element_type=jnp.float32)
-        scores = scores * SCALE + bias
+    scores, state = {}, {}
+
+    def score(head):
+        cols = head_columns(head)
+        scores[head] = lax.dot_general(q_ref[:, cols], pair_ref[0, :, cols], NT, preferred_element_type=jnp.float32)
+
+    def soften(head):
+        scaled = scores.pop(head) * SCALE + bias
         before = top_ref[head]
-        top = jnp.maximum(before, jnp.max(scores, axis=1, keepdims=True))
+        top = jnp.maximum(before, jnp.max(scaled, axis=1, keepdims=True))
         kept = jnp.exp2(before - top)
-        exps = jnp.exp2(scores - top)
+        exps = jnp.exp2(scaled - top)
         total = total_ref[head] * kept + jnp.sum(exps, axis=1, keepdims=True)
-        summed = acc_ref[:, cols] * kept + jnp.dot(
-            exps.astype(jnp.bfloat16), pair_ref[1, :, cols], preferred_element_type=jnp.float32
-        )
-        attended_ref[:, cols] = (summed / total).astype(jnp.bfloat16)
+        state[head] = (kept, total, exps.astype(jnp.bfloat16))
+
+    def gather(head):
+        cols = head_columns(head)
+        kept, total, weights = state.pop(head)
+        summed = jnp.dot(weights, pair_ref[1, :, cols], preferred_element_type=jnp.float32)
+        attended_ref[:, cols] = ((acc_ref[:, cols] * kept + summed) / total).astype(jnp.bfloat16)
+
+    staged(width // HEAD_DIM, score, soften, gather)
     out_ref[...] = jnp.dot(attended_ref[...], weight_ref[...], preferred_element_type=jnp.float32).astype(jnp.bfloat16)
 
 
@@ -167,7 +197,7 @@
         in_specs=[SMEM, SMEM] + [VMEM] * 6,
         out_specs=VMEM,
         scratch_shapes=[pltpu.VMEM((rows, width), jnp.bfloat16)],
-        compiler_params=pltpu.CompilerParams(vmem_limit_bytes=24 * 1024 * 1024),
+        compiler_params=pltpu.CompilerParams(vmem_limit_bytes=16 * 1024 * 1024),
         name="last",
     )(index, picks, queries, acc, top, total, pair, weight)
 

time: 52 us -> 43.7 us (0.84)
  Pallas kernels: 15.3 us -> 6.44 us
  waiting for transfers between devices: 7.05 us -> 9.62 us
  local copies, waits for them, and re-layouts: 5.97 us -> 3.72 us
    pallas_call x1, Pallas kernels: 5.95 us -> 2.95 us  [last(): pl.pallas_call(functools.partial(last_kernel, count), out_shape=jax.Shape...]
    ppermute x6, waiting for transfers between devices: 7.05 us -> 9.62 us  [moved(): lax.ppermute(block, 'tm', [(i, j) for i, j in route if 0 <= j < count])]
    unnamed x16 -> x12, local copies, waits for them, and re-layouts: 5.97 us -> 3.72 us
    pallas_call x1, Pallas kernels: 2.3 us -> 0.05 us  [choose(): pl.pallas_call(choose_kernel, out_shape=jax.ShapeDtypeStruct(ends.shape,...]
    pallas_call x1, Pallas kernels: 5 us -> 3.05 us  [first(): pl.pallas_call(functools.partial(first_kernel, count), out_shape=(jax.Sha...]
    pallas_call x1, Pallas kernels: 2.04 us -> 0.39 us  [pack(): pl.pallas_call(pack_kernel, out_shape=jax.ShapeDtypeStruct((2,) + keys.sh...]
  transfers between devices with their start and end apart: 6 -> 6, of which waited for: 2 -> 2; matrix products, arithmetic and copies ran while one was open for 0% -> 0% of each run, Pallas kernels for 14% -> 7%
where the time goes in v2:
time: 43.7 us; the launch traced here: 43.4 us
  starting transfers between devices  23.5 us (54%)
  waiting for transfers between devices  9.62 us (22%)
  Pallas kernels  6.44 us (15%)
  local copies, waits for them, and re-layouts  3.72 us (9%)
    ppermute x6, starting transfers between devices, moved(): lax.ppermute(block, 'tm', [(i, j) for i, j in route if 0 <= j < count])  23.5 us
    ppermute x6, waiting for transfers between devices, moved(): lax.ppermute(block, 'tm', [(i, j) for i, j in route if 0 <= j < count])  9.62 us
    unnamed x12, local copies, waits for them, and re-layouts  3.72 us
    pallas_call x1, Pallas kernels, first(): pl.pallas_call(functools.partial(first_kernel, count), out_shape=(jax.Sha...  3.05 us
    pallas_call x1, Pallas kernels, last(): pl.pallas_call(functools.partial(last_kernel, count), out_shape=jax.Shape...  2.95 us
  transfers between devices with their start and end apart: 6, of which 2 were waited for; matrix products, arithmetic and copies ran while one was open for 0% of the time, Pallas kernels for 7%

profile of v2, /device:TPU:0, one launch (start us, length us, event | category | flops | bytes accessed | tf_op | source)
XLA Modules:
  0.0 43.4 jit_solution(12345971750439602733)
XLA Ops:
  0.0 0.0 copy-start.2
  0.0 0.0 copy-start.3
  0.0 1.0 %copy-done.3 = bf16[128,1536]{1,0:T(8,128)(2,1)S(1)} copy-done((bf16[128,1536]{1,0:T(8,128)(2,1)S(1)}, bf16[128,1536]{1,0:T(8,128)(2,1)}, u32[]{:S(2)}) %copy-start.3) | copy-done | bytes 393240
  1.1 0.0 copy-start.4
  1.1 1.0 %copy-done.4 = bf16[128,1536]{1,0:T(8,128)(2,1)S(1)} copy-done((bf16[128,1536]{1,0:T(8,128)(2,1)S(1)}, bf16[128,1536]{1,0:T(8,128)(2,1)}, u32[]{:S(2)}) %copy-start.4) | copy-done | bytes 393240
  2.0 0.4 pack.1.own_ref
  2.4 1.3 %collective-permute-start.1 = (bf16[2,128,1536]{2,1,0:T(8,128)(2,1)S(1)}, bf16[2,128,1536]{2,1,0:T(8,128)(2,1)S(1)}, u32[]{:S(2)}, u32[]{:S(2)}) collective-permute-start(bf16[2,128,1536]{2,1,0:T(8,128)(2,1)S(1)} %pack.1.own_ref), channel_id=1, source_target_pairs={{1,3},{2,0},{3,5},{4,2},{5,7},{6,4},{7,9},{8,6},{9,11},{10,8},{11,... | collective-permute-start | bytes 2359304 | tf_op jit(solution)/shard_map/ppermute | solution.py:208
  3.7 3.2 %collective-permute-start = (bf16[2,128,1536]{2,1,0:T(8,128)(2,1)S(1)}, bf16[2,128,1536]{2,1,0:T(8,128)(2,1)S(1)}, u32[]{:S(2)}, u32[]{:S(2)}) collective-permute-start(bf16[2,128,1536]{2,1,0:T(8,128)(2,1)S(1)} %pack.1.own_ref), channel_id=1, source_target_pairs={{0,1},{1,0},{2,3},{3,2},{4,5},{5,4},{6,7},{7,6},{8,9},{9,8},{10,11... | collective-permute-start | bytes 2359304 | tf_op jit(solution)/shard_map/ppermute | solution.py:208
  7.0 1.3 %collective-permute-start.4 = (bf16[2,128,1536]{2,1,0:T(8,128)(2,1)S(1)}, bf16[2,128,1536]{2,1,0:T(8,128)(2,1)S(1)}, u32[]{:S(2)}, u32[]{:S(2)}) collective-permute-start(bf16[2,128,1536]{2,1,0:T(8,128)(2,1)S(1)} %pack.1.own_ref), channel_id=1, source_target_pairs={{1,5},{3,7},{4,0},{5,9},{6,2},{7,11},{8,4},{9,13},{10,6},{11,15},{... | collective-permute-start | bytes 2359304 | tf_op jit(solution)/shard_map/ppermute | solution.py:208
  8.3 5.4 %collective-permute-start.3 = (bf16[2,128,1536]{2,1,0:T(8,128)(2,1)S(1)}, bf16[2,128,1536]{2,1,0:T(8,128)(2,1)}, u32[]{:S(2)}, u32[]{:S(2)}) collective-permute-start(bf16[2,128,1536]{2,1,0:T(8,128)(2,1)S(1)} %pack.1.own_ref), channel_id=1, source_target_pairs={{0,4},{2,6},{4,8},{5,1},{6,10},{7,3},{8,12},{9,5},{10,14},{11,7},{... | collective-permute-start | bytes 2359304 | tf_op jit(solution)/shard_map/ppermute | solution.py:208
  13.7 0.0 copy-start
  13.7 3.6 %collective-permute-done.1.x1_ref.ends_ref = bf16[2,128,1536]{2,1,0:T(8,128)(2,1)S(1)} collective-permute-done((bf16[2,128,1536]{2,1,0:T(8,128)(2,1)S(1)}, bf16[2,128,1536]{2,1,0:T(8,128)(2,1)S(1)}, u32[]{:S(2)}, u32[]{:S(2)}) %collective-permute-start.1) | collective-permute-done | bytes 786464 | tf_op jit(solution)/shard_map/ppermute | solution.py:208
  17.3 6.9 %collective-permute-start.2 = (bf16[2,128,1536]{2,1,0:T(8,128)(2,1)S(1)}, bf16[2,128,1536]{2,1,0:T(8,128)(2,1)S(1)}, u32[]{:S(2)}, u32[]{:S(2)}) collective-permute-start(bf16[2,128,1536]{2,1,0:T(8,128)(2,1)S(1)} %collective-permute-done.1.x1_ref.ends_ref), channel_id=1, source_target_pairs={{0,1},{1,0},{2,3},{3,2},{4,5},{5,4},{6,7},{7,6},{8,9},{9,8},{10,11... | collective-permute-start | bytes 2359304 | tf_op jit(solution)/shard_map/ppermute | solution.py:208
  24.2 0.0 collective-permute-done.s0_ref.inner_ref
  24.2 0.1 choose.1
  24.3 5.3 %collective-permute-start.5 = (bf16[2,128,1536]{2,1,0:T(8,128)(2,1)S(1)}, bf16[2,128,1536]{2,1,0:T(8,128)(2,1)S(1)}, u32[]{:S(2)}, u32[]{:S(2)}) collective-permute-start(bf16[2,128,1536]{2,1,0:T(8,128)(2,1)S(1)} %choose.1), channel_id=1, source_target_pairs={{0,4},{1,2},{2,1},{4,8},{5,6},{6,5},{7,3},{8,12},{9,10},{10,9},{11... | collective-permute-start | bytes 2359304 | tf_op jit(solution)/shard_map/ppermute | solution.py:208
  29.6 6.1 %collective-permute-done.4.zb_ref = bf16[2,128,1536]{2,1,0:T(8,128)(2,1)S(1)} collective-permute-done((bf16[2,128,1536]{2,1,0:T(8,128)(2,1)S(1)}, bf16[2,128,1536]{2,1,0:T(8,128)(2,1)S(1)}, u32[]{:S(2)}, u32[]{:S(2)}) %collective-permute-start.4) | collective-permute-done | bytes 786464 | tf_op jit(solution)/shard_map/ppermute | solution.py:208
  35.6 0.0 collective-permute-done.3.za_ref
  35.6 0.0 collective-permute-done.2.s1_ref
  35.6 0.0 copy-start.1
  35.6 1.0 %copy-done.1 = bf16[128,1536]{1,0:T(8,128)(2,1)S(1)} copy-done((bf16[128,1536]{1,0:T(8,128)(2,1)S(1)}, bf16[128,1536]{1,0:T(8,128)(2,1)}, u32[]{:S(2)}) %copy-start.1) | copy-done | bytes 393240
  36.6 0.0 copy-start.5
  36.6 0.7 %copy-done.5 = s32[2,8]{1,0:T(2,128)S(1)} copy-done((s32[2,8]{1,0:T(2,128)S(1)}, s32[2,8]{1,0:T(2,128)}, u32[]{:S(2)}) %copy-start.5) | copy-done | bytes 88
  37.3 3.0 %first.1 = (f32[128,1536]{1,0:T(8,128)S(1)}, f32[12,128,128]{2,1,0:T(8,128)S(1)}, f32[12,128,128]{2,1,0:T(8,128)S(1)}) custom-call(s32[1]{0:T(128)} %bitcast.index_ref, s32[2,8]{1,0:T(2,128)S(1)} %copy-done.5, bf16[128,1536]{1,0:T(8,128)(2,1)S(1)} %copy-done.1, bf16[2,128,1536]{2,1,0:T(8,128)(2,1)S(1)} %pack.1.own_ref, ...), custom_call_target="tpu_custom_call" | custom-call | tf_op jit(solution)/shard_map/first/pallas_call | solution.py:150
  40.4 0.0 collective-permute-done.5.pair_ref
  40.4 0.0 copy-done.2
  40.4 0.0 copy-done
  40.4 3.0 %last.1 = bf16[128,1536]{1,0:T(8,128)(2,1)} custom-call(s32[1]{0:T(128)} %bitcast.index_ref, s32[2,8]{1,0:T(2,128)S(1)} %copy-done.5, bf16[128,1536]{1,0:T(8,128)(2,1)S(1)} %copy-done.2, f32[128,1536]{1,0:T(8,128)S(1)} %get-tuple-element.8.acc_ref, f32[12,128,128]{2,1,0:T(8,128)S(1)} %get-tuple-element.9.top_ref, ...), custom_call_target="tpu_custom_call" | custom-call | tf_op jit(solution)/shard_map/last/pallas_call | solution.py:194
Async XLA Ops:
  0.0 40.4 %copy-start.2 = (bf16[128,1536]{1,0:T(8,128)(2,1)S(1)}, bf16[128,1536]{1,0:T(8,128)(2,1)}, u32[]{:S(2)}) copy-start(bf16[128,1536]{1,0:T(8,128)(2,1)} %q_ref.3) | copy-start | bytes 1179652
  0.0 1.0 %copy-start.3 = (bf16[128,1536]{1,0:T(8,128)(2,1)S(1)}, bf16[128,1536]{1,0:T(8,128)(2,1)}, u32[]{:S(2)}) copy-start(bf16[128,1536]{1,0:T(8,128)(2,1)} %keys_ref.1) | copy-start | bytes 1179652
  1.1 1.0 %copy-start.4 = (bf16[128,1536]{1,0:T(8,128)(2,1)S(1)}, bf16[128,1536]{1,0:T(8,128)(2,1)}, u32[]{:S(2)}) copy-start(bf16[128,1536]{1,0:T(8,128)(2,1)} %values_ref.1) | copy-start | bytes 1179652
  2.4 14.8 %collective-permute-start.1 = (bf16[2,128,1536]{2,1,0:T(8,128)(2,1)S(1)}, bf16[2,128,1536]{2,1,0:T(8,128)(2,1)S(1)}, u32[]{:S(2)}, u32[]{:S(2)}) collective-permute-start(bf16[2,128,1536]{2,1,0:T(8,128)(2,1)S(1)} %pack.1.own_ref), channel_id=1, source_target_pairs={{1,3},{2,0},{3,5},{4,2},{5,7},{6,4},{7,9},{8,6},{9,11},{10,8},{11,... | collective-permute-start | bytes 2359304 | tf_op jit(solution)/shard_map/ppermute | solution.py:208
  3.7 20.5 %collective-permute-start = (bf16[2,128,1536]{2,1,0:T(8,128)(2,1)S(1)}, bf16[2,128,1536]{2,1,0:T(8,128)(2,1)S(1)}, u32[]{:S(2)}, u32[]{:S(2)}) collective-permute-start(bf16[2,128,1536]{2,1,0:T(8,128)(2,1)S(1)} %pack.1.own_ref), channel_id=1, source_target_pairs={{0,1},{1,0},{2,3},{3,2},{4,5},{5,4},{6,7},{7,6},{8,9},{9,8},{10,11... | collective-permute-start | bytes 2359304 | tf_op jit(solution)/shard_map/ppermute | solution.py:208
  7.0 28.6 %collective-permute-start.4 = (bf16[2,128,1536]{2,1,0:T(8,128)(2,1)S(1)}, bf16[2,128,1536]{2,1,0:T(8,128)(2,1)S(1)}, u32[]{:S(2)}, u32[]{:S(2)}) collective-permute-start(bf16[2,128,1536]{2,1,0:T(8,128)(2,1)S(1)} %pack.1.own_ref), channel_id=1, source_target_pairs={{1,5},{3,7},{4,0},{5,9},{6,2},{7,11},{8,4},{9,13},{10,6},{11,15},{... | collective-permute-start | bytes 2359304 | tf_op jit(solution)/shard_map/ppermute | solution.py:208
  8.3 27.4 %collective-permute-start.3 = (bf16[2,128,1536]{2,1,0:T(8,128)(2,1)S(1)}, bf16[2,128,1536]{2,1,0:T(8,128)(2,1)}, u32[]{:S(2)}, u32[]{:S(2)}) collective-permute-start(bf16[2,128,1536]{2,1,0:T(8,128)(2,1)S(1)} %pack.1.own_ref), channel_id=1, source_target_pairs={{0,4},{2,6},{4,8},{5,1},{6,10},{7,3},{8,12},{9,5},{10,14},{11,7},{... | collective-permute-start | bytes 2359304 | tf_op jit(solution)/shard_map/ppermute | solution.py:208
  13.7 26.7 %copy-start = (bf16[1536,1536]{1,0:T(8,128)(2,1)S(1)}, bf16[1536,1536]{1,0:T(8,128)(2,1)}, u32[]{:S(2)}) copy-start(bf16[1536,1536]{1,0:T(8,128)(2,1)} %weight_ref.1) | copy-start | bytes 14155780
  17.3 18.4 %collective-permute-start.2 = (bf16[2,128,1536]{2,1,0:T(8,128)(2,1)S(1)}, bf16[2,128,1536]{2,1,0:T(8,128)(2,1)S(1)}, u32[]{:S(2)}, u32[]{:S(2)}) collective-permute-start(bf16[2,128,1536]{2,1,0:T(8,128)(2,1)S(1)} %collective-permute-done.1.x1_ref.ends_ref), channel_id=1, source_target_pairs={{0,1},{1,0},{2,3},{3,2},{4,5},{5,4},{6,7},{7,6},{8,9},{9,8},{10,11... | collective-permute-start | bytes 2359304 | tf_op jit(solution)/shard_map/ppermute | solution.py:208
  24.3 16.1 %collective-permute-start.5 = (bf16[2,128,1536]{2,1,0:T(8,128)(2,1)S(1)}, bf16[2,128,1536]{2,1,0:T(8,128)(2,1)S(1)}, u32[]{:S(2)}, u32[]{:S(2)}) collective-permute-start(bf16[2,128,1536]{2,1,0:T(8,128)(2,1)S(1)} %choose.1), channel_id=1, source_target_pairs={{0,4},{1,2},{2,1},{4,8},{5,6},{6,5},{7,3},{8,12},{9,10},{10,9},{11... | collective-permute-start | bytes 2359304 | tf_op jit(solution)/shard_map/ppermute | solution.py:208
  35.6 1.0 %copy-start.1 = (bf16[128,1536]{1,0:T(8,128)(2,1)S(1)}, bf16[128,1536]{1,0:T(8,128)(2,1)}, u32[]{:S(2)}) copy-start(bf16[128,1536]{1,0:T(8,128)(2,1)} %q_ref.3) | copy-start | bytes 1179652
  36.6 0.7 %copy-start.5 = (s32[2,8]{1,0:T(2,128)S(1)}, s32[2,8]{1,0:T(2,128)}, u32[]{:S(2)}) copy-start(s32[2,8]{1,0:T(2,128)} %picks_ref.3) | copy-start | bytes 196

commit v3 on v2

v3 whole, which is shorter than its diff:
```python
import functools
import math

import jax
import jax.numpy as jnp
from jax import lax
from jax.experimental import pallas as pl
from jax.experimental.pallas import tpu as pltpu
from jax.sharding import PartitionSpec as P

HEAD_DIM = 128
BLK = 64
LEVELS = 2
PICKS = 2
FAR = 8
SCALE = HEAD_DIM ** (-0.5) * math.log2(math.e)
UNUSED = -1e30
LEAD = 2
NONE = 1 << 20

STEPS = ((-4, 1, -1, 4), (4, 4, -4, -4), (3, -4, 4, -3))
SIDE_STEPS = (2, 0, 0, -2)
RELAY_STEPS = (0, 3, -3, 0)
SWAP_STEPS = (1, -1, 1, -1)
FIRST_OFFSETS = ((4, 1, -1, -4),)
SECOND_OFFSETS = ((-4, -4, 4, 4), (NONE, 2, -2, NONE))
MIDDLE_OFFSETS = ((-1, 4, -4, 1),)
LAST_OFFSETS = ((2, -2, 2, -2), (-2, NONE, NONE, 2))

VMEM = pl.BlockSpec(memory_space=pltpu.VMEM)
SMEM = pl.BlockSpec(memory_space=pltpu.SMEM)
ANY = pl.BlockSpec(memory_space=pl.ANY)
NT = (((1,), (1,)), ((), ()))


def after_kernel(block_ref, before_ref, out_ref):
    out_ref[...] = block_ref[...]


def after(block, before, flops):
    return pl.pallas_call(
        after_kernel,
        out_shape=jax.ShapeDtypeStruct(block.shape, block.dtype),
        in_specs=[VMEM, VMEM],
        out_specs=VMEM,
        cost_estimate=pl.CostEstimate(flops=flops, bytes_accessed=0, transcendentals=0),
        compiler_params=pltpu.CompilerParams(vmem_limit_bytes=4 * 1024 * 1024),
        name="after",
    )(block, before)


def column_offset(column):
    magnitude = 2 ** (1 + column // PICKS % LEVELS)
    return -magnitude if column < FAR // 2 else magnitude


def head_columns(head):
    return pl.ds(head * HEAD_DIM, HEAD_DIM)


def by_place(device, choices):
    place = lax.rem(device, 4)
    value = jnp.int32(choices[0])
    for i in range(1, 4):
        value = jnp.where(place == i, jnp.int32(choices[i]), value)
    return value


def shard_bias(picks_ref, device, offset, count, rows):
    usable = (device + offset >= 0) & (device + offset < count)
    near = (offset >= -1) & (offset <= 1)
    lane = lax.broadcasted_iota(jnp.int32, (BLK, rows), 1)
    parts = []
    for block in range(rows // BLK):
        bias = jnp.full((BLK, rows), UNUSED, jnp.float32)
        for local in range(rows // BLK):
            named = jnp.where(near, 1, 0)
            for column in range(FAR):
                hit = (picks_ref[block, column] == local) & (offset == column_offset(column))
                named = named + jnp.where(hit, 1, 0)
            named = jnp.where(usable, named, 0)
            value = jnp.where(named == 0, jnp.float32(UNUSED), (named - 1).astype(jnp.float32))
            bias = jnp.where(lane // BLK == local, value, bias)
        parts.append(bias)
    return jnp.concatenate(parts, axis=0)


def pack_kernel(keys_ref, values_ref, pair_ref, sems):
    first = pltpu.make_async_copy(keys_ref, pair_ref.at[0], sems.at[0])
    second = pltpu.make_async_copy(values_ref, pair_ref.at[1], sems.at[1])
    first.start()
    second.start()
    first.wait()
    second.wait()


def pack(keys, values):
    return pl.pallas_call(
        pack_kernel,
        out_shape=jax.ShapeDtypeStruct((2,) + keys.shape, keys.dtype),
        in_specs=[ANY, ANY],
        out_specs=VMEM,
        scratch_shapes=[pltpu.SemaphoreType.DMA((2,))],
        compiler_params=pltpu.CompilerParams(vmem_limit_bytes=4 * 1024 * 1024),
        name="pack",
    )(keys, values)


def choose_kernel(index_ref, ends_ref, inner_ref, out_ref):
    place = lax.rem(index_ref[0], 4)
    ends = (place == 0) | (place == 3)

    @pl.when(ends)
    def _():
        out_ref[...] = ends_ref[...]

    @pl.when(jnp.logical_not(ends))
    def _():
        out_ref[...] = inner_ref[...]


def choose(index, ends, inner):
    return pl.pallas_call(
        choose_kernel,
        out_shape=jax.ShapeDtypeStruct(ends.shape, ends.dtype),
        in_specs=[SMEM, VMEM, VMEM],
        out_specs=VMEM,
        compiler_params=pltpu.CompilerParams(vmem_limit_bytes=4 * 1024 * 1024),
        name="choose",
    )(index, ends, inner)


def staged(heads, score, soften, gather):
    for step in range(heads + 2 * LEAD):
        if step < heads:
            score(step)
        if 0 <= step - LEAD < heads:
            soften(step - LEAD)
        if 0 <= step - 2 * LEAD < heads:
            gather(step - 2 * LEAD)


def attend(q_ref, shards, biases, top_ref, total_ref, finish):
    rows, width = q_ref.shape
    scores, state = {}, {}

    def part(which, cols):
        return jnp.concatenate([shard[which, :, cols] for shard in shards], axis=0)

    def score(head):
        cols = head_columns(head)
        scores[head] = lax.dot_general(q_ref[:, cols], part(0, cols), NT, preferred_element_type=jnp.float32)

    def soften(head):
        scaled = scores.pop(head) * SCALE
        parts = [scaled[:, i * rows:(i + 1) * rows] for i in range(len(shards))]
        parts = [p if bias is None else p + bias for p, bias in zip(parts, biases)]
        top = jnp.max(functools.reduce(jnp.maximum, parts), axis=1, keepdims=True)
        kept = None
        if top_ref is not None:
            before = top_ref[head]
            top = jnp.maximum(before, top)
            kept = jnp.exp2(before - top)
        exps = [jnp.exp2(p - top) for p in parts]
        total = jnp.sum(functools.reduce(jnp.add, exps), axis=1, keepdims=True)
        if top_ref is not None:
            total = total_ref[head] * kept + total
        state[head] = (top, kept, total, jnp.concatenate([e.astype(jnp.bfloat16) for e in exps], axis=1))

    def gather(head):
        top, kept, total, weights = state.pop(head)
        summed = jnp.dot(weights, part(1, head_columns(head)), preferred_element_type=jnp.float32)
        finish(head, top, kept, total, summed)

    staged(width // HEAD_DIM, score, soften, gather)


def first_kernel(
    count, index_ref, picks_ref, q_ref, own_ref, mate_ref, one_ref, weight_ref, acc_ref, top_ref,
    total_ref, held_ref, sem
):
    fetch = pltpu.make_async_copy(weight_ref, held_ref, sem)
    fetch.start()
    rows = q_ref.shape[0]
    device = index_ref[0]
    offsets = FIRST_OFFSETS
    biases = [shard_bias(picks_ref, device, by_place(device, offset), count, rows) for offset in offsets]

    def finish(head, top, kept, total, summed):
        acc_ref[:, head_columns(head)] = summed
        top_ref[head] = jnp.broadcast_to(top, top_ref.shape[1:])
        total_ref[head] = jnp.broadcast_to(total, total_ref.shape[1:])

    attend(q_ref, (own_ref, mate_ref, one_ref), [None, None] + biases, None, None, finish)
    fetch.wait()


def first(count, index, picks, queries, weight, *shards):
    rows, width = queries.shape
    column = jax.ShapeDtypeStruct((width // HEAD_DIM, rows, HEAD_DIM), jnp.float32)
    return pl.pallas_call(
        functools.partial(first_kernel, count),
        out_shape=(jax.ShapeDtypeStruct((rows, width), jnp.float32), column, column,
                   jax.ShapeDtypeStruct(weight.shape, weight.dtype)),
        in_specs=[SMEM, SMEM] + [VMEM] * (1 + len(shards)) + [ANY],
        out_specs=(VMEM, VMEM, VMEM, VMEM),
        scratch_shapes=[pltpu.SemaphoreType.DMA],
        compiler_params=pltpu.CompilerParams(vmem_limit_bytes=16 * 1024 * 1024),
        name="first",
    )(index, picks, queries, *shards, weight)


def middle_kernel(count, offsets, index_ref, picks_ref, q_ref, acc_ref, top_ref, total_ref, *refs):
    shard_refs = refs[:len(offsets)]
    new_acc_ref, new_top_ref, new_total_ref = refs[len(offsets):]
    rows = q_ref.shape[0]
    device = index_ref[0]
    biases = [shard_bias(picks_ref, device, by_place(device, offset), count, rows) for offset in offsets]

    def finish(head, top, kept, total, summed):
        cols = head_columns(head)
        new_acc_ref[:, cols] = acc_ref[:, cols] * kept + summed
        new_top_ref[head] = top
        new_total_ref[head] = total

    attend(q_ref, shard_refs, biases, top_ref, total_ref, finish)


def middle(count, offsets, index, picks, queries, acc, top, total, *shards):
    return pl.pallas_call(
        functools.partial(middle_kernel, count, offsets),
        out_shape=[jax.ShapeDtypeStruct(x.shape, x.dtype) for x in (acc, top, total)],
        in_specs=[SMEM, SMEM] + [VMEM] * (4 + len(shards)),
        out_specs=[VMEM, VMEM, VMEM],
        compiler_params=pltpu.CompilerParams(vmem_limit_bytes=16 * 1024 * 1024),
        name="middle",
    )(index, picks, queries, acc, top, total, *shards)


def last_kernel(
    count, index_ref, picks_ref, q_ref, acc_ref, top_ref, total_ref, swap_ref, relay_ref, weight_ref, out_ref,
    attended_ref
):
    rows = q_ref.shape[0]
    device = index_ref[0]
    biases = [shard_bias(picks_ref, device, by_place(device, offset), count, rows) for offset in LAST_OFFSETS]

    def finish(head, top, kept, total, summed):
        cols = head_columns(head)
        attended_ref[:, cols] = ((acc_ref[:, cols] * kept + summed) / total).astype(jnp.bfloat16)

    attend(q_ref, (swap_ref, relay_ref), biases, top_ref, total_ref, finish)
    out_ref[...] = jnp.dot(attended_ref[...], weight_ref[...], preferred_element_type=jnp.float32).astype(jnp.bfloat16)


def last(count, index, picks, queries, acc, top, total, *rest):
    rows, width = queries.shape
    return pl.pallas_call(
        functools.partial(last_kernel, count),
        out_shape=jax.ShapeDtypeStruct((rows, width), jnp.bfloat16),
        in_specs=[SMEM, SMEM] + [VMEM] * (4 + len(rest)),
        out_specs=VMEM,
        scratch_shapes=[pltpu.VMEM((rows, width), jnp.bfloat16)],
        compiler_params=pltpu.CompilerParams(vmem_limit_bytes=16 * 1024 * 1024),
        name="last",
    )(index, picks, queries, acc, top, total, *rest)


def moved(block, steps):
    count = lax.axis_size("tm")
    route = [(i, i + steps[i % 4]) for i in range(count) if steps[i % 4]]
    return lax.ppermute(block, "tm", [(i, j) for i, j in route if 0 <= j < count])


def body(queries, keys, values, far_picks, out_weight):
    count = lax.axis_size("tm")
    index = lax.axis_index("tm").astype(jnp.int32).reshape(1)
    pair = jnp.stack([keys, values])
    one = moved(pair, STEPS[0])
    two = moved(pair, STEPS[1])
    side = moved(pair, SIDE_STEPS)
    three = moved(choose(index, one, pair), STEPS[2])
    relay = after(moved(one, RELAY_STEPS), two, 10000000000)
    swap = moved(choose(index, three, one), SWAP_STEPS)
    mate = moved(pair, SWAP_STEPS)
    *state, held = first(count, index, far_picks, queries, out_weight, pair, mate, one)
    state = middle(count, SECOND_OFFSETS, index, far_picks, queries, *state, two, side)
    state = middle(count, MIDDLE_OFFSETS, index, far_picks, queries, *state, three)
    return last(count, index, far_picks, queries, *state, swap, relay, held)


def solution(mesh):
    placed = (
        P(("vid", "tm"), None),
        P(("vid", "tm"), None),
        P(("vid", "tm"), None),
        P(("vid", "tm"), None),
        P(),
    )
    return jax.shard_map(
        body, mesh=mesh, in_specs=placed, out_specs=P(("vid", "tm"), None), check_vma=False
    )
```

time: 43.7 us -> 38.7 us (0.89)
  starting transfers between devices: 23.5 us -> 12.7 us
  Pallas kernels: 6.44 us -> 8.79 us
  waiting for transfers between devices: 9.62 us -> 11.4 us
  other arithmetic: 0 us -> 1.19 us
    ppermute x6 -> x7, starting transfers between devices: 23.5 us -> 12.7 us  [moved(): lax.ppermute(block, 'tm', [(i, j) for i, j in route if 0 <= j < count])]
    pallas_call x1 -> x3, Pallas kernels: 0.39 us -> 3.09 us  [the longest x2 3.04 us: middle(): pl.pallas_call(functools.partial(middle_kernel, count, offsets), out_shap...]
    ppermute x6 -> x7, waiting for transfers between devices: 9.62 us -> 11.4 us  [moved(): lax.ppermute(block, 'tm', [(i, j) for i, j in route if 0 <= j < count])]
    another operation x0 -> x1, other arithmetic: none -> 1.19 us  [body(): pair = jnp.stack([keys, values])]
    pallas_call x1, Pallas kernels: 3.05 us -> 2.6 us  [first(): pl.pallas_call(functools.partial(first_kernel, count), out_shape=(jax.Sha...]
    unnamed x12 -> x8, local copies, waits for them, and re-layouts: 3.72 us -> 4.01 us
  transfers between devices with their start and end apart: 6 -> 7, of which waited for: 2 -> 4; matrix products, arithmetic and copies ran while one was open for 0% -> 0% of each run, Pallas kernels for 7% -> 15%
where the time goes in v3:
time: 38.7 us; the launch traced here: 38.3 us
  starting transfers between devices  12.7 us (33%)
  waiting for transfers between devices  11.4 us (29%)
  Pallas kernels  8.79 us (23%)
  local copies, waits for them, and re-layouts  4.01 us (10%)
  other arithmetic  1.19 us (3%)
    ppermute x7, starting transfers between devices, moved(): lax.ppermute(block, 'tm', [(i, j) for i, j in route if 0 <= j < count])  12.7 us
    ppermute x7, waiting for transfers between devices, moved(): lax.ppermute(block, 'tm', [(i, j) for i, j in route if 0 <= j < count])  11.4 us
    unnamed x8, local copies, waits for them, and re-layouts  4.01 us
    pallas_call x2, Pallas kernels, middle(): pl.pallas_call(functools.partial(middle_kernel, count, offsets), out_shap...  3.04 us
    pallas_call x1, Pallas kernels, last(): pl.pallas_call(functools.partial(last_kernel, count), out_shape=jax.Shape...  3 us
    pallas_call x1, Pallas kernels, first(): pl.pallas_call(functools.partial(first_kernel, count), out_shape=(jax.Sha...  2.6 us
    another operation x1, other arithmetic, body(): pair = jnp.stack([keys, values])  1.19 us
  transfers between devices with their start and end apart: 7, of which 4 were waited for; matrix products, arithmetic and copies ran while one was open for 0% of the time, Pallas kernels for 15%

profile of v3, /device:TPU:0, one launch (start us, length us, event | category | flops | bytes accessed | tf_op | source)
XLA Modules:
  0.0 38.3 jit_solution(5160795746549596798)
XLA Ops:
  0.0 1.2 %pad_maximum_fusion.own_ref.inner_ref = bf16[2,128,1536]{2,1,0:T(8,128)(2,1)S(1)} fusion(bf16[1,128,1536]{2,1,0:T(8,128)(2,1)} %bitcast.3, bf16[1,128,1536]{2,1,0:T(8,128)(2,1)} %bitcast.4), kind=kLoop, calls=%fused_computation | loop fusion | flops 393216 | bytes 1572864 | tf_op jit(solution)/shard_map/stack | solution.py:278
  1.2 1.3 %collective-permute-start.1 = (bf16[2,128,1536]{2,1,0:T(8,128)(2,1)S(1)}, bf16[2,128,1536]{2,1,0:T(8,128)(2,1)S(1)}, u32[]{:S(2)}, u32[]{:S(2)}) collective-permute-start(bf16[2,128,1536]{2,1,0:T(8,128)(2,1)S(1)} %pad_maximum_fusion.own_ref.inner_ref), channel_id=1, source_target_pairs={{1,2},{2,1},{3,7},{4,0},{5,6},{6,5},{7,11},{8,4},{9,10},{10,9},{11... | collective-permute-start | bytes 2359304 | tf_op jit(solution)/shard_map/ppermute | solution.py:272
  2.5 3.8 %collective-permute-start = (bf16[2,128,1536]{2,1,0:T(8,128)(2,1)S(1)}, bf16[2,128,1536]{2,1,0:T(8,128)(2,1)}, u32[]{:S(2)}, u32[]{:S(2)}) collective-permute-start(bf16[2,128,1536]{2,1,0:T(8,128)(2,1)S(1)} %pad_maximum_fusion.own_ref.inner_ref), channel_id=1, source_target_pairs={{0,1},{1,0},{2,3},{3,2},{4,5},{5,4},{6,7},{7,6},{8,9},{9,8},{10,11... | collective-permute-start | bytes 2359304 | tf_op jit(solution)/shard_map/ppermute | solution.py:272
  6.3 3.5 %collective-permute-start.2 = (bf16[2,128,1536]{2,1,0:T(8,128)(2,1)S(1)}, bf16[2,128,1536]{2,1,0:T(8,128)(2,1)S(1)}, u32[]{:S(2)}, u32[]{:S(2)}) collective-permute-start(bf16[2,128,1536]{2,1,0:T(8,128)(2,1)S(1)} %pad_maximum_fusion.own_ref.inner_ref), channel_id=1, source_target_pairs={{0,4},{1,5},{4,8},{5,9},{6,2},{7,3},{8,12},{9,13},{10,6},{11,7},{1... | collective-permute-start | bytes 2359304 | tf_op jit(solution)/shard_map/ppermute | solution.py:272
  9.8 1.3 %collective-permute-start.3 = (bf16[2,128,1536]{2,1,0:T(8,128)(2,1)S(1)}, bf16[2,128,1536]{2,1,0:T(8,128)(2,1)S(1)}, u32[]{:S(2)}, u32[]{:S(2)}) collective-permute-start(bf16[2,128,1536]{2,1,0:T(8,128)(2,1)S(1)} %pad_maximum_fusion.own_ref.inner_ref), channel_id=1, source_target_pairs={{0,2},{3,1},{4,6},{7,5},{8,10},{11,9},{12,14},{15,13},{16,18},{19,... | collective-permute-start | bytes 2359304 | tf_op jit(solution)/shard_map/ppermute | solution.py:272
  11.1 5.0 %collective-permute-done.1.one_ref.ends_ref.inner_ref = bf16[2,128,1536]{2,1,0:T(8,128)(2,1)S(1)} collective-permute-done((bf16[2,128,1536]{2,1,0:T(8,128)(2,1)S(1)}, bf16[2,128,1536]{2,1,0:T(8,128)(2,1)S(1)}, u32[]{:S(2)}, u32[]{:S(2)}) %collective-permute-start.1) | collective-permute-done | bytes 786464 | tf_op jit(solution)/shard_map/ppermute | solution.py:272
  16.1 0.0 copy-start.1
  16.1 0.1 choose.2
  16.1 2.1 %collective-permute-start.4 = (bf16[2,128,1536]{2,1,0:T(8,128)(2,1)S(1)}, bf16[2,128,1536]{2,1,0:T(8,128)(2,1)S(1)}, u32[]{:S(2)}, u32[]{:S(2)}) collective-permute-start(bf16[2,128,1536]{2,1,0:T(8,128)(2,1)S(1)} %choose.2), channel_id=1, source_target_pairs={{0,3},{2,6},{3,0},{4,7},{5,1},{6,10},{7,4},{8,11},{9,5},{10,14},{1... | collective-permute-start | bytes 2359304 | tf_op jit(solution)/shard_map/ppermute | solution.py:272
  18.2 0.7 %collective-permute-start.6 = (bf16[2,128,1536]{2,1,0:T(8,128)(2,1)S(1)}, bf16[2,128,1536]{2,1,0:T(8,128)(2,1)S(1)}, u32[]{:S(2)}, u32[]{:S(2)}) collective-permute-start(bf16[2,128,1536]{2,1,0:T(8,128)(2,1)S(1)} %collective-permute-done.1.one_ref.ends_ref.inner_ref), channel_id=1, source_target_pairs={{1,4},{5,8},{6,3},{9,12},{10,7},{14,11},{17,20},{21,24},{22,19},{2... | collective-permute-start | bytes 2359304 | tf_op jit(solution)/shard_map/ppermute | solution.py:272
  18.9 0.0 collective-permute-done.mate_ref
  18.9 0.0 copy-start
  18.9 1.0 %copy-done = bf16[128,1536]{1,0:T(8,128)(2,1)S(1)} copy-done((bf16[128,1536]{1,0:T(8,128)(2,1)S(1)}, bf16[128,1536]{1,0:T(8,128)(2,1)}, u32[]{:S(2)}) %copy-start) | copy-done | bytes 393240
  19.9 0.0 copy-start.2
  19.9 2.3 %copy-done.2 = bf16[1536,1536]{1,0:T(8,128)(2,1)S(1)} copy-done((bf16[1536,1536]{1,0:T(8,128)(2,1)S(1)}, bf16[1536,1536]{1,0:T(8,128)(2,1)}, u32[]{:S(2)}) %copy-start.2) | copy-done | bytes 4718616
  22.3 0.0 copy-start.3
  22.3 0.7 %copy-done.3 = s32[2,8]{1,0:T(2,128)S(1)} copy-done((s32[2,8]{1,0:T(2,128)S(1)}, s32[2,8]{1,0:T(2,128)}, u32[]{:S(2)}) %copy-start.3) | copy-done | bytes 88
  23.0 2.6 %first.1 = (f32[128,1536]{1,0:T(8,128)S(1)}, f32[12,128,128]{2,1,0:T(8,128)S(1)}, f32[12,128,128]{2,1,0:T(8,128)S(1)}, bf16[1536,1536]{1,0:T(8,128)(2,1)S(1)}) custom-call(s32[1]{0:T(128)} %bitcast.index_ref, s32[2,8]{1,0:T(2,128)S(1)} %copy-done.3, bf16[128,1536]{1,0:T(8,128)(2,1)S(1)} %copy-done, ...), custom_call_target="tpu_custom_call" | custom-call | tf_op jit(solution)/shard_map/first/pallas_call | solution.py:201
  25.6 2.1 %collective-permute-done.2.refs_0_.before_ref = bf16[2,128,1536]{2,1,0:T(8,128)(2,1)S(1)} collective-permute-done((bf16[2,128,1536]{2,1,0:T(8,128)(2,1)S(1)}, bf16[2,128,1536]{2,1,0:T(8,128)(2,1)S(1)}, u32[]{:S(2)}, u32[]{:S(2)}) %collective-permute-start.2) | collective-permute-done | bytes 786464 | tf_op jit(solution)/shard_map/ppermute | solution.py:272
  27.6 0.0 collective-permute-done.3.refs_1_
  27.6 0.0 copy-done.1
  27.6 1.5 %middle.2 = (f32[128,1536]{1,0:T(8,128)S(1)}, f32[12,128,128]{2,1,0:T(8,128)S(1)}, f32[12,128,128]{2,1,0:T(8,128)S(1)}) custom-call(s32[1]{0:T(128)} %bitcast.index_ref, s32[2,8]{1,0:T(2,128)S(1)} %copy-done.3, bf16[128,1536]{1,0:T(8,128)(2,1)S(1)} %copy-done.1, f32[128,1536]{1,0:T(8,128)S(1)} %get-tuple-element.15.acc_ref, ...), custom_call_target="tpu_custom_call" | custom-call | tf_op jit(solution)/shard_map/middle/pallas_call | solution.py:230
  29.2 3.7 %collective-permute-done.4.refs_0_.ends_ref = bf16[2,128,1536]{2,1,0:T(8,128)(2,1)S(1)} collective-permute-done((bf16[2,128,1536]{2,1,0:T(8,128)(2,1)S(1)}, bf16[2,128,1536]{2,1,0:T(8,128)(2,1)S(1)}, u32[]{:S(2)}, u32[]{:S(2)}) %collective-permute-start.4) | collective-permute-done | bytes 786464 | tf_op jit(solution)/shard_map/ppermute | solution.py:272
  32.9 0.1 choose.3
  32.9 0.1 collective-permute-start.5
  33.0 1.5 %middle.3 = (f32[128,1536]{1,0:T(8,128)S(1)}, f32[12,128,128]{2,1,0:T(8,128)S(1)}, f32[12,128,128]{2,1,0:T(8,128)S(1)}) custom-call(s32[1]{0:T(128)} %bitcast.index_ref, s32[2,8]{1,0:T(2,128)S(1)} %copy-done.3, bf16[128,1536]{1,0:T(8,128)(2,1)S(1)} %copy-done.1, f32[128,1536]{1,0:T(8,128)S(1)} %get-tuple-element.18.acc_ref, ...), custom_call_target="tpu_custom_call" | custom-call | tf_op jit(solution)/shard_map/middle/pallas_call | solution.py:230
  34.6 0.0 collective-permute-done.6.block_ref
  34.6 0.1 after.1.relay_ref
  34.6 0.7 %collective-permute-done.5.swap_ref = bf16[2,128,1536]{2,1,0:T(8,128)(2,1)S(1)} collective-permute-done((bf16[2,128,1536]{2,1,0:T(8,128)(2,1)S(1)}, bf16[2,128,1536]{2,1,0:T(8,128)(2,1)S(1)}, u32[]{:S(2)}, u32[]{:S(2)}) %collective-permute-start.5) | collective-permute-done | bytes 786464 | tf_op jit(solution)/shard_map/ppermute | solution.py:272
  35.3 3.0 %last.1 = bf16[128,1536]{1,0:T(8,128)(2,1)} custom-call(s32[1]{0:T(128)} %bitcast.index_ref, s32[2,8]{1,0:T(2,128)S(1)} %copy-done.3, bf16[128,1536]{1,0:T(8,128)(2,1)S(1)} %copy-done.1, f32[128,1536]{1,0:T(8,128)S(1)} %get-tuple-element.21.acc_ref, f32[12,128,128]{2,1,0:T(8,128)S(1)} %get-tuple-element.22.top_ref, ...), custom_call_target="tpu_custom_call" | custom-call | tf_op jit(solution)/shard_map/last/pallas_call | solution.py:258
Async XLA Ops:
  1.2 14.9 %collective-permute-start.1 = (bf16[2,128,1536]{2,1,0:T(8,128)(2,1)S(1)}, bf16[2,128,1536]{2,1,0:T(8,128)(2,1)S(1)}, u32[]{:S(2)}, u32[]{:S(2)}) collective-permute-start(bf16[2,128,1536]{2,1,0:T(8,128)(2,1)S(1)} %pad_maximum_fusion.own_ref.inner_ref), channel_id=1, source_target_pairs={{1,2},{2,1},{3,7},{4,0},{5,6},{6,5},{7,11},{8,4},{9,10},{10,9},{11... | collective-permute-start | bytes 2359304 | tf_op jit(solution)/shard_map/ppermute | solution.py:272
  2.5 16.4 %collective-permute-start = (bf16[2,128,1536]{2,1,0:T(8,128)(2,1)S(1)}, bf16[2,128,1536]{2,1,0:T(8,128)(2,1)}, u32[]{:S(2)}, u32[]{:S(2)}) collective-permute-start(bf16[2,128,1536]{2,1,0:T(8,128)(2,1)S(1)} %pad_maximum_fusion.own_ref.inner_ref), channel_id=1, source_target_pairs={{0,1},{1,0},{2,3},{3,2},{4,5},{5,4},{6,7},{7,6},{8,9},{9,8},{10,11... | collective-permute-start | bytes 2359304 | tf_op jit(solution)/shard_map/ppermute | solution.py:272
  6.3 21.4 %collective-permute-start.2 = (bf16[2,128,1536]{2,1,0:T(8,128)(2,1)S(1)}, bf16[2,128,1536]{2,1,0:T(8,128)(2,1)S(1)}, u32[]{:S(2)}, u32[]{:S(2)}) collective-permute-start(bf16[2,128,1536]{2,1,0:T(8,128)(2,1)S(1)} %pad_maximum_fusion.own_ref.inner_ref), channel_id=1, source_target_pairs={{0,4},{1,5},{4,8},{5,9},{6,2},{7,3},{8,12},{9,13},{10,6},{11,7},{1... | collective-permute-start | bytes 2359304 | tf_op jit(solution)/shard_map/ppermute | solution.py:272
  9.8 17.9 %collective-permute-start.3 = (bf16[2,128,1536]{2,1,0:T(8,128)(2,1)S(1)}, bf16[2,128,1536]{2,1,0:T(8,128)(2,1)S(1)}, u32[]{:S(2)}, u32[]{:S(2)}) collective-permute-start(bf16[2,128,1536]{2,1,0:T(8,128)(2,1)S(1)} %pad_maximum_fusion.own_ref.inner_ref), channel_id=1, source_target_pairs={{0,2},{3,1},{4,6},{7,5},{8,10},{11,9},{12,14},{15,13},{16,18},{19,... | collective-permute-start | bytes 2359304 | tf_op jit(solution)/shard_map/ppermute | solution.py:272
  16.1 11.6 %copy-start.1 = (bf16[128,1536]{1,0:T(8,128)(2,1)S(1)}, bf16[128,1536]{1,0:T(8,128)(2,1)}, u32[]{:S(2)}) copy-start(bf16[128,1536]{1,0:T(8,128)(2,1)} %q_ref.7) | copy-start | bytes 1179652
  16.1 16.7 %collective-permute-start.4 = (bf16[2,128,1536]{2,1,0:T(8,128)(2,1)S(1)}, bf16[2,128,1536]{2,1,0:T(8,128)(2,1)S(1)}, u32[]{:S(2)}, u32[]{:S(2)}) collective-permute-start(bf16[2,128,1536]{2,1,0:T(8,128)(2,1)S(1)} %choose.2), channel_id=1, source_target_pairs={{0,3},{2,6},{3,0},{4,7},{5,1},{6,10},{7,4},{8,11},{9,5},{10,14},{1... | collective-permute-start | bytes 2359304 | tf_op jit(solution)/shard_map/ppermute | solution.py:272
  18.2 16.3 %collective-permute-start.6 = (bf16[2,128,1536]{2,1,0:T(8,128)(2,1)S(1)}, bf16[2,128,1536]{2,1,0:T(8,128)(2,1)S(1)}, u32[]{:S(2)}, u32[]{:S(2)}) collective-permute-start(bf16[2,128,1536]{2,1,0:T(8,128)(2,1)S(1)} %collective-permute-done.1.one_ref.ends_ref.inner_ref), channel_id=1, source_target_pairs={{1,4},{5,8},{6,3},{9,12},{10,7},{14,11},{17,20},{21,24},{22,19},{2... | collective-permute-start | bytes 2359304 | tf_op jit(solution)/shard_map/ppermute | solution.py:272
  18.9 1.0 %copy-start = (bf16[128,1536]{1,0:T(8,128)(2,1)S(1)}, bf16[128,1536]{1,0:T(8,128)(2,1)}, u32[]{:S(2)}) copy-start(bf16[128,1536]{1,0:T(8,128)(2,1)} %q_ref.7) | copy-start | bytes 1179652
  19.9 2.3 %copy-start.2 = (bf16[1536,1536]{1,0:T(8,128)(2,1)S(1)}, bf16[1536,1536]{1,0:T(8,128)(2,1)}, u32[]{:S(2)}) copy-start(bf16[1536,1536]{1,0:T(8,128)(2,1)} %weight_ref.1) | copy-start | bytes 14155780
  22.3 0.7 %copy-start.3 = (s32[2,8]{1,0:T(2,128)S(1)}, s32[2,8]{1,0:T(2,128)}, u32[]{:S(2)}) copy-start(s32[2,8]{1,0:T(2,128)} %picks_ref.7) | copy-start | bytes 196
  32.9 2.4 %collective-permute-start.5 = (bf16[2,128,1536]{2,1,0:T(8,128)(2,1)S(1)}, bf16[2,128,1536]{2,1,0:T(8,128)(2,1)S(1)}, u32[]{:S(2)}, u32[]{:S(2)}) collective-permute-start(bf16[2,128,1536]{2,1,0:T(8,128)(2,1)S(1)} %choose.3), channel_id=1, source_target_pairs={{0,1},{1,0},{2,3},{3,2},{4,5},{5,4},{6,7},{7,6},{8,9},{9,8},{10,11... | collective-permute-start | bytes 2359304 | tf_op jit(solution)/shard_map/ppermute | solution.py:272

commit v4 on v3

--- a/solution.py
+++ b/solution.py
@@ -23,9 +23,11 @@
 RELAY_STEPS = (0, 3, -3, 0)
 SWAP_STEPS = (1, -1, 1, -1)
 FIRST_OFFSETS = ((4, 1, -1, -4),)
-SECOND_OFFSETS = ((-4, -4, 4, 4), (NONE, 2, -2, NONE))
-MIDDLE_OFFSETS = ((-1, 4, -4, 1),)
-LAST_OFFSETS = ((2, -2, 2, -2), (-2, NONE, NONE, 2))
+LATER_OFFSETS = (
+    (-4, -4, 4, 4), (NONE, 2, -2, NONE),
+    (-1, 4, -4, 1),
+    (2, -2, 2, -2), (-2, NONE, NONE, 2),
+)
 
 VMEM = pl.BlockSpec(memory_space=pltpu.VMEM)
 SMEM = pl.BlockSpec(memory_space=pltpu.SMEM)
@@ -177,14 +179,15 @@
 
 def first_kernel(
     count, index_ref, picks_ref, q_ref, own_ref, mate_ref, one_ref, weight_ref, acc_ref, top_ref,
-    total_ref, held_ref, sem
+    total_ref, held_ref, later_ref, sem
 ):
     fetch = pltpu.make_async_copy(weight_ref, held_ref, sem)
     fetch.start()
     rows = q_ref.shape[0]
     device = index_ref[0]
-    offsets = FIRST_OFFSETS
-    biases = [shard_bias(picks_ref, device, by_place(device, offset), count, rows) for offset in offsets]
+    biases = [shard_bias(picks_ref, device, by_place(device, offset), count, rows) for offset in FIRST_OFFSETS]
+    for i, offset in enumerate(LATER_OFFSETS):
+        later_ref[i] = shard_bias(picks_ref, device, by_place(device, offset), count, rows)
 
     def finish(head, top, kept, total, summed):
         acc_ref[:, head_columns(head)] = summed
@@ -201,21 +204,19 @@
     return pl.pallas_call(
         functools.partial(first_kernel, count),
         out_shape=(jax.ShapeDtypeStruct((rows, width), jnp.float32), column, column,
-                   jax.ShapeDtypeStruct(weight.shape, weight.dtype)),
+                   jax.ShapeDtypeStruct(weight.shape, weight.dtype),
+                   jax.ShapeDtypeStruct((len(LATER_OFFSETS), rows, rows), jnp.float32)),
         in_specs=[SMEM, SMEM] + [VMEM] * (1 + len(shards)) + [ANY],
-        out_specs=(VMEM, VMEM, VMEM, VMEM),
+        out_specs=(VMEM, VMEM, VMEM, VMEM, VMEM),
         scratch_shapes=[pltpu.SemaphoreType.DMA],
         compiler_params=pltpu.CompilerParams(vmem_limit_bytes=16 * 1024 * 1024),
         name="first",
     )(index, picks, queries, *shards, weight)
 
 
-def middle_kernel(count, offsets, index_ref, picks_ref, q_ref, acc_ref, top_ref, total_ref, *refs):
-    shard_refs = refs[:len(offsets)]
-    new_acc_ref, new_top_ref, new_total_ref = refs[len(offsets):]
-    rows = q_ref.shape[0]
-    device = index_ref[0]
-    biases = [shard_bias(picks_ref, device, by_place(device, offset), count, rows) for offset in offsets]
+def middle_kernel(places, bias_ref, q_ref, acc_ref, top_ref, total_ref, *refs):
+    shard_refs = refs[:len(places)]
+    new_acc_ref, new_top_ref, new_total_ref = refs[len(places):]
 
     def finish(head, top, kept, total, summed):
         cols = head_columns(head)
@@ -223,47 +224,43 @@
         new_top_ref[head] = top
         new_total_ref[head] = total
 
-    attend(q_ref, shard_refs, biases, top_ref, total_ref, finish)
-
-
-def middle(count, offsets, index, picks, queries, acc, top, total, *shards):
-    return pl.pallas_call(
-        functools.partial(middle_kernel, count, offsets),
+    attend(q_ref, shard_refs, [bias_ref[i] for i in places], top_ref, total_ref, finish)
+
+
+def middle(places, bias, queries, acc, top, total, *shards):
+    return pl.pallas_call(
+        functools.partial(middle_kernel, places),
         out_shape=[jax.ShapeDtypeStruct(x.shape, x.dtype) for x in (acc, top, total)],
-        in_specs=[SMEM, SMEM] + [VMEM] * (4 + len(shards)),
+        in_specs=[VMEM] * (5 + len(shards)),
         out_specs=[VMEM, VMEM, VMEM],
         compiler_params=pltpu.CompilerParams(vmem_limit_bytes=16 * 1024 * 1024),
         name="middle",
-    )(index, picks, queries, acc, top, total, *shards)
+    )(bias, queries, acc, top, total, *shards)
 
 
 def last_kernel(
-    count, index_ref, picks_ref, q_ref, acc_ref, top_ref, total_ref, swap_ref, relay_ref, weight_ref, out_ref,
+    places, bias_ref, q_ref, acc_ref, top_ref, total_ref, swap_ref, relay_ref, weight_ref, out_ref,
     attended_ref
 ):
-    rows = q_ref.shape[0]
-    device = index_ref[0]
-    biases = [shard_bias(picks_ref, device, by_place(device, offset), count, rows) for offset in LAST_OFFSETS]
-
     def finish(head, top, kept, total, summed):
         cols = head_columns(head)
         attended_ref[:, cols] = ((acc_ref[:, cols] * kept + summed) / total).astype(jnp.bfloat16)
 
-    attend(q_ref, (swap_ref, relay_ref), biases, top_ref, total_ref, finish)
+    attend(q_ref, (swap_ref, relay_ref), [bias_ref[i] for i in places], top_ref, total_ref, finish)
     out_ref[...] = jnp.dot(attended_ref[...], weight_ref[...], preferred_element_type=jnp.float32).astype(jnp.bfloat16)
 
 
-def last(count, index, picks, queries, acc, top, total, *rest):
+def last(places, bias, queries, acc, top, total, *rest):
     rows, width = queries.shape
     return pl.pallas_call(
-        functools.partial(last_kernel, count),
+        functools.partial(last_kernel, places),
         out_shape=jax.ShapeDtypeStruct((rows, width), jnp.bfloat16),
-        in_specs=[SMEM, SMEM] + [VMEM] * (4 + len(rest)),
+        in_specs=[VMEM] * (5 + len(rest)),
         out_specs=VMEM,
         scratch_shapes=[pltpu.VMEM((rows, width), jnp.bfloat16)],
         compiler_params=pltpu.CompilerParams(vmem_limit_bytes=16 * 1024 * 1024),
         name="last",
-    )(index, picks, queries, acc, top, total, *rest)
+    )(bias, queries, acc, top, total, *rest)
 
 
 def moved(block, steps):
@@ -283,10 +280,10 @@
     relay = after(moved(one, RELAY_STEPS), two, 10000000000)
     swap = moved(choose(index, three, one), SWAP_STEPS)
     mate = moved(pair, SWAP_STEPS)
-    *state, held = first(count, index, far_picks, queries, out_weight, pair, mate, one)
-    state = middle(count, SECOND_OFFSETS, index, far_picks, queries, *state, two, side)
-    state = middle(count, MIDDLE_OFFSETS, index, far_picks, queries, *state, three)
-    return last(count, index, far_picks, queries, *state, swap, relay, held)
+    *state, held, bias = first(count, index, far_picks, queries, out_weight, pair, mate, one)
+    state = middle((0, 1), bias, queries, *state, two, side)
+    state = middle((2,), bias, queries, *state, three)
+    return last((3, 4), bias, queries, *state, swap, relay, held)
 
 
 def solution(mesh):

time: 38.7 us -> 38 us (0.982)
  Pallas kernels: 8.79 us -> 7.26 us
  waiting for transfers between devices: 11.4 us -> 12.3 us
    pallas_call x3, Pallas kernels: 6.04 us -> 4.36 us  [the longest x1 2.39 us: last(): pl.pallas_call(functools.partial(last_kernel, places), out_shape=jax.Shap...]
    ppermute x7, waiting for transfers between devices: 11.4 us -> 12.3 us  [moved(): lax.ppermute(block, 'tm', [(i, j) for i, j in route if 0 <= j < count])]
  transfers between devices with their start and end apart: 7 -> 7, of which waited for: 4 -> 4; matrix products, arithmetic and copies ran while one was open for 0% -> 0% of each run, Pallas kernels for 15% -> 13%
where the time goes in v4:
time: 38 us; the launch traced here: 37.7 us
  starting transfers between devices  12.7 us (33%)
  waiting for transfers between devices  12.3 us (32%)
  Pallas kernels  7.26 us (19%)
  local copies, waits for them, and re-layouts  4.01 us (11%)
  other arithmetic  1.19 us (3%)
    ppermute x7, starting transfers between devices, moved(): lax.ppermute(block, 'tm', [(i, j) for i, j in route if 0 <= j < count])  12.7 us
    ppermute x7, waiting for transfers between devices, moved(): lax.ppermute(block, 'tm', [(i, j) for i, j in route if 0 <= j < count])  12.3 us
    unnamed x8, local copies, waits for them, and re-layouts  4.01 us
    pallas_call x1, Pallas kernels, first(): pl.pallas_call(functools.partial(first_kernel, count), out_shape=(jax.Sha...  2.75 us
    pallas_call x1, Pallas kernels, last(): pl.pallas_call(functools.partial(last_kernel, places), out_shape=jax.Shap...  2.39 us
    pallas_call x2, Pallas kernels, middle(): pl.pallas_call(functools.partial(middle_kernel, places), out_shape=[jax.S...  1.97 us
    another operation x1, other arithmetic, body(): pair = jnp.stack([keys, values])  1.19 us
  transfers between devices with their start and end apart: 7, of which 4 were waited for; matrix products, arithmetic and copies ran while one was open for 0% of the time, Pallas kernels for 13%

profile of v4, /device:TPU:0, one launch (start us, length us, event | category | flops | bytes accessed | tf_op | source)
XLA Modules:
  0.0 37.7 jit_solution(15162114363770752455)
XLA Ops:
  0.0 1.2 %pad_maximum_fusion.own_ref.inner_ref = bf16[2,128,1536]{2,1,0:T(8,128)(2,1)S(1)} fusion(bf16[1,128,1536]{2,1,0:T(8,128)(2,1)} %bitcast.3, bf16[1,128,1536]{2,1,0:T(8,128)(2,1)} %bitcast.4), kind=kLoop, calls=%fused_computation | loop fusion | flops 393216 | bytes 1572864 | tf_op jit(solution)/shard_map/stack | solution.py:275
  1.2 1.3 %collective-permute-start.1 = (bf16[2,128,1536]{2,1,0:T(8,128)(2,1)S(1)}, bf16[2,128,1536]{2,1,0:T(8,128)(2,1)S(1)}, u32[]{:S(2)}, u32[]{:S(2)}) collective-permute-start(bf16[2,128,1536]{2,1,0:T(8,128)(2,1)S(1)} %pad_maximum_fusion.own_ref.inner_ref), channel_id=1, source_target_pairs={{1,2},{2,1},{3,7},{4,0},{5,6},{6,5},{7,11},{8,4},{9,10},{10,9},{11... | collective-permute-start | bytes 2359304 | tf_op jit(solution)/shard_map/ppermute | solution.py:269
  2.5 3.8 %collective-permute-start = (bf16[2,128,1536]{2,1,0:T(8,128)(2,1)S(1)}, bf16[2,128,1536]{2,1,0:T(8,128)(2,1)}, u32[]{:S(2)}, u32[]{:S(2)}) collective-permute-start(bf16[2,128,1536]{2,1,0:T(8,128)(2,1)S(1)} %pad_maximum_fusion.own_ref.inner_ref), channel_id=1, source_target_pairs={{0,1},{1,0},{2,3},{3,2},{4,5},{5,4},{6,7},{7,6},{8,9},{9,8},{10,11... | collective-permute-start | bytes 2359304 | tf_op jit(solution)/shard_map/ppermute | solution.py:269
  6.3 3.5 %collective-permute-start.2 = (bf16[2,128,1536]{2,1,0:T(8,128)(2,1)S(1)}, bf16[2,128,1536]{2,1,0:T(8,128)(2,1)S(1)}, u32[]{:S(2)}, u32[]{:S(2)}) collective-permute-start(bf16[2,128,1536]{2,1,0:T(8,128)(2,1)S(1)} %pad_maximum_fusion.own_ref.inner_ref), channel_id=1, source_target_pairs={{0,4},{1,5},{4,8},{5,9},{6,2},{7,3},{8,12},{9,13},{10,6},{11,7},{1... | collective-permute-start | bytes 2359304 | tf_op jit(solution)/shard_map/ppermute | solution.py:269
  9.8 1.3 %collective-permute-start.3 = (bf16[2,128,1536]{2,1,0:T(8,128)(2,1)S(1)}, bf16[2,128,1536]{2,1,0:T(8,128)(2,1)S(1)}, u32[]{:S(2)}, u32[]{:S(2)}) collective-permute-start(bf16[2,128,1536]{2,1,0:T(8,128)(2,1)S(1)} %pad_maximum_fusion.own_ref.inner_ref), channel_id=1, source_target_pairs={{0,2},{3,1},{4,6},{7,5},{8,10},{11,9},{12,14},{15,13},{16,18},{19,... | collective-permute-start | bytes 2359304 | tf_op jit(solution)/shard_map/ppermute | solution.py:269
  11.1 5.0 %collective-permute-done.1.one_ref.ends_ref.inner_ref = bf16[2,128,1536]{2,1,0:T(8,128)(2,1)S(1)} collective-permute-done((bf16[2,128,1536]{2,1,0:T(8,128)(2,1)S(1)}, bf16[2,128,1536]{2,1,0:T(8,128)(2,1)S(1)}, u32[]{:S(2)}, u32[]{:S(2)}) %collective-permute-start.1) | collective-permute-done | bytes 786464 | tf_op jit(solution)/shard_map/ppermute | solution.py:269
  16.1 0.0 copy-start.1
  16.1 0.1 choose.2
  16.1 2.1 %collective-permute-start.4 = (bf16[2,128,1536]{2,1,0:T(8,128)(2,1)S(1)}, bf16[2,128,1536]{2,1,0:T(8,128)(2,1)S(1)}, u32[]{:S(2)}, u32[]{:S(2)}) collective-permute-start(bf16[2,128,1536]{2,1,0:T(8,128)(2,1)S(1)} %choose.2), channel_id=1, source_target_pairs={{0,3},{2,6},{3,0},{4,7},{5,1},{6,10},{7,4},{8,11},{9,5},{10,14},{1... | collective-permute-start | bytes 2359304 | tf_op jit(solution)/shard_map/ppermute | solution.py:269
  18.2 0.7 %collective-permute-start.6 = (bf16[2,128,1536]{2,1,0:T(8,128)(2,1)S(1)}, bf16[2,128,1536]{2,1,0:T(8,128)(2,1)S(1)}, u32[]{:S(2)}, u32[]{:S(2)}) collective-permute-start(bf16[2,128,1536]{2,1,0:T(8,128)(2,1)S(1)} %collective-permute-done.1.one_ref.ends_ref.inner_ref), channel_id=1, source_target_pairs={{1,4},{5,8},{6,3},{9,12},{10,7},{14,11},{17,20},{21,24},{22,19},{2... | collective-permute-start | bytes 2359304 | tf_op jit(solution)/shard_map/ppermute | solution.py:269
  18.9 0.0 collective-permute-done.mate_ref
  18.9 0.0 copy-start
  18.9 1.0 %copy-done = bf16[128,1536]{1,0:T(8,128)(2,1)S(1)} copy-done((bf16[128,1536]{1,0:T(8,128)(2,1)S(1)}, bf16[128,1536]{1,0:T(8,128)(2,1)}, u32[]{:S(2)}) %copy-start) | copy-done | bytes 393240
  19.9 0.0 copy-start.2
  19.9 2.3 %copy-done.2 = bf16[1536,1536]{1,0:T(8,128)(2,1)S(1)} copy-done((bf16[1536,1536]{1,0:T(8,128)(2,1)S(1)}, bf16[1536,1536]{1,0:T(8,128)(2,1)}, u32[]{:S(2)}) %copy-start.2) | copy-done | bytes 4718616
  22.3 0.0 copy-start.3
  22.3 0.7 %copy-done.3 = s32[2,8]{1,0:T(2,128)S(1)} copy-done((s32[2,8]{1,0:T(2,128)S(1)}, s32[2,8]{1,0:T(2,128)}, u32[]{:S(2)}) %copy-start.3) | copy-done | bytes 88
  23.0 2.7 %first.1 = (f32[128,1536]{1,0:T(8,128)S(1)}, f32[12,128,128]{2,1,0:T(8,128)S(1)}, f32[12,128,128]{2,1,0:T(8,128)S(1)}, bf16[1536,1536]{1,0:T(8,128)(2,1)S(1)}, f32[5,128,128]{2,1,0:T(8,128)S(1)}) custom-call(s32[1]{0:T(128)} %bitcast.index_ref, s32[2,8]{1,0:T(2,128)S(1)} %copy-done.3, bf16[128,1536]{1,0:T(8,128)(2,1)S(1)} %copy-done, ...), custom_call_target="tpu_custom_call" | custom-call | tf_op jit(solution)/shard_map/first/pallas_call | solution.py:204
  25.7 1.9 %collective-permute-done.2.refs_0_.before_ref = bf16[2,128,1536]{2,1,0:T(8,128)(2,1)S(1)} collective-permute-done((bf16[2,128,1536]{2,1,0:T(8,128)(2,1)S(1)}, bf16[2,128,1536]{2,1,0:T(8,128)(2,1)S(1)}, u32[]{:S(2)}, u32[]{:S(2)}) %collective-permute-start.2) | collective-permute-done | bytes 786464 | tf_op jit(solution)/shard_map/ppermute | solution.py:269
  27.6 0.0 collective-permute-done.3.refs_1_
  27.6 0.0 copy-done.1
  27.6 1.0 %middle.2 = (f32[128,1536]{1,0:T(8,128)S(1)}, f32[12,128,128]{2,1,0:T(8,128)S(1)}, f32[12,128,128]{2,1,0:T(8,128)S(1)}) custom-call(f32[5,128,128]{2,1,0:T(8,128)S(1)} %get-tuple-element.16.bias_ref, bf16[128,1536]{1,0:T(8,128)(2,1)S(1)} %copy-done.1, f32[128,1536]{1,0:T(8,128)S(1)} %get-tuple-element.17.acc_ref, ...), custom_call_target="tpu_custom_call" | custom-call | tf_op jit(solution)/shard_map/middle/pallas_call | solution.py:231
  28.6 4.2 %collective-permute-done.4.refs_0_.ends_ref = bf16[2,128,1536]{2,1,0:T(8,128)(2,1)S(1)} collective-permute-done((bf16[2,128,1536]{2,1,0:T(8,128)(2,1)S(1)}, bf16[2,128,1536]{2,1,0:T(8,128)(2,1)S(1)}, u32[]{:S(2)}, u32[]{:S(2)}) %collective-permute-start.4) | collective-permute-done | bytes 786464 | tf_op jit(solution)/shard_map/ppermute | solution.py:269
  32.9 0.1 choose.3
  32.9 0.1 collective-permute-start.5
  33.0 1.0 %middle.3 = (f32[128,1536]{1,0:T(8,128)S(1)}, f32[12,128,128]{2,1,0:T(8,128)S(1)}, f32[12,128,128]{2,1,0:T(8,128)S(1)}) custom-call(f32[5,128,128]{2,1,0:T(8,128)S(1)} %get-tuple-element.16.bias_ref, bf16[128,1536]{1,0:T(8,128)(2,1)S(1)} %copy-done.1, f32[128,1536]{1,0:T(8,128)S(1)} %get-tuple-element.20.acc_ref, ...), custom_call_target="tpu_custom_call" | custom-call | tf_op jit(solution)/shard_map/middle/pallas_call | solution.py:231
  34.0 0.0 collective-permute-done.6.block_ref
  34.0 0.1 after.1.relay_ref
  34.1 1.2 %collective-permute-done.5.swap_ref = bf16[2,128,1536]{2,1,0:T(8,128)(2,1)S(1)} collective-permute-done((bf16[2,128,1536]{2,1,0:T(8,128)(2,1)S(1)}, bf16[2,128,1536]{2,1,0:T(8,128)(2,1)S(1)}, u32[]{:S(2)}, u32[]{:S(2)}) %collective-permute-start.5) | collective-permute-done | bytes 786464 | tf_op jit(solution)/shard_map/ppermute | solution.py:269
  35.3 2.4 %last.1 = bf16[128,1536]{1,0:T(8,128)(2,1)} custom-call(f32[5,128,128]{2,1,0:T(8,128)S(1)} %get-tuple-element.16.bias_ref, bf16[128,1536]{1,0:T(8,128)(2,1)S(1)} %copy-done.1, f32[128,1536]{1,0:T(8,128)S(1)} %get-tuple-element.23.acc_ref, f32[12,128,128]{2,1,0:T(8,128)S(1)} %get-tuple-element.24.top_ref, f32[12,128,128]{2,1,0:T(8,128)S(1)} %get-tuple-element.25.total_ref, ...), custom_call_target="tpu_custom_call" | custom-call | tf_op jit(solution)/shard_map/last/pallas_call | solution.py:255
Async XLA Ops:
  1.2 14.9 %collective-permute-start.1 = (bf16[2,128,1536]{2,1,0:T(8,128)(2,1)S(1)}, bf16[2,128,1536]{2,1,0:T(8,128)(2,1)S(1)}, u32[]{:S(2)}, u32[]{:S(2)}) collective-permute-start(bf16[2,128,1536]{2,1,0:T(8,128)(2,1)S(1)} %pad_maximum_fusion.own_ref.inner_ref), channel_id=1, source_target_pairs={{1,2},{2,1},{3,7},{4,0},{5,6},{6,5},{7,11},{8,4},{9,10},{10,9},{11... | collective-permute-start | bytes 2359304 | tf_op jit(solution)/shard_map/ppermute | solution.py:269
  2.5 16.4 %collective-permute-start = (bf16[2,128,1536]{2,1,0:T(8,128)(2,1)S(1)}, bf16[2,128,1536]{2,1,0:T(8,128)(2,1)}, u32[]{:S(2)}, u32[]{:S(2)}) collective-permute-start(bf16[2,128,1536]{2,1,0:T(8,128)(2,1)S(1)} %pad_maximum_fusion.own_ref.inner_ref), channel_id=1, source_target_pairs={{0,1},{1,0},{2,3},{3,2},{4,5},{5,4},{6,7},{7,6},{8,9},{9,8},{10,11... | collective-permute-start | bytes 2359304 | tf_op jit(solution)/shard_map/ppermute | solution.py:269
  6.3 21.4 %collective-permute-start.2 = (bf16[2,128,1536]{2,1,0:T(8,128)(2,1)S(1)}, bf16[2,128,1536]{2,1,0:T(8,128)(2,1)S(1)}, u32[]{:S(2)}, u32[]{:S(2)}) collective-permute-start(bf16[2,128,1536]{2,1,0:T(8,128)(2,1)S(1)} %pad_maximum_fusion.own_ref.inner_ref), channel_id=1, source_target_pairs={{0,4},{1,5},{4,8},{5,9},{6,2},{7,3},{8,12},{9,13},{10,6},{11,7},{1... | collective-permute-start | bytes 2359304 | tf_op jit(solution)/shard_map/ppermute | solution.py:269
  9.8 17.9 %collective-permute-start.3 = (bf16[2,128,1536]{2,1,0:T(8,128)(2,1)S(1)}, bf16[2,128,1536]{2,1,0:T(8,128)(2,1)S(1)}, u32[]{:S(2)}, u32[]{:S(2)}) collective-permute-start(bf16[2,128,1536]{2,1,0:T(8,128)(2,1)S(1)} %pad_maximum_fusion.own_ref.inner_ref), channel_id=1, source_target_pairs={{0,2},{3,1},{4,6},{7,5},{8,10},{11,9},{12,14},{15,13},{16,18},{19,... | collective-permute-start | bytes 2359304 | tf_op jit(solution)/shard_map/ppermute | solution.py:269
  16.1 11.6 %copy-start.1 = (bf16[128,1536]{1,0:T(8,128)(2,1)S(1)}, bf16[128,1536]{1,0:T(8,128)(2,1)}, u32[]{:S(2)}) copy-start(bf16[128,1536]{1,0:T(8,128)(2,1)} %q_ref.7) | copy-start | bytes 1179652
  16.1 16.7 %collective-permute-start.4 = (bf16[2,128,1536]{2,1,0:T(8,128)(2,1)S(1)}, bf16[2,128,1536]{2,1,0:T(8,128)(2,1)S(1)}, u32[]{:S(2)}, u32[]{:S(2)}) collective-permute-start(bf16[2,128,1536]{2,1,0:T(8,128)(2,1)S(1)} %choose.2), channel_id=1, source_target_pairs={{0,3},{2,6},{3,0},{4,7},{5,1},{6,10},{7,4},{8,11},{9,5},{10,14},{1... | collective-permute-start | bytes 2359304 | tf_op jit(solution)/shard_map/ppermute | solution.py:269
  18.2 15.8 %collective-permute-start.6 = (bf16[2,128,1536]{2,1,0:T(8,128)(2,1)S(1)}, bf16[2,128,1536]{2,1,0:T(8,128)(2,1)S(1)}, u32[]{:S(2)}, u32[]{:S(2)}) collective-permute-start(bf16[2,128,1536]{2,1,0:T(8,128)(2,1)S(1)} %collective-permute-done.1.one_ref.ends_ref.inner_ref), channel_id=1, source_target_pairs={{1,4},{5,8},{6,3},{9,12},{10,7},{14,11},{17,20},{21,24},{22,19},{2... | collective-permute-start | bytes 2359304 | tf_op jit(solution)/shard_map/ppermute | solution.py:269
  18.9 1.0 %copy-start = (bf16[128,1536]{1,0:T(8,128)(2,1)S(1)}, bf16[128,1536]{1,0:T(8,128)(2,1)}, u32[]{:S(2)}) copy-start(bf16[128,1536]{1,0:T(8,128)(2,1)} %q_ref.7) | copy-start | bytes 1179652
  19.9 2.3 %copy-start.2 = (bf16[1536,1536]{1,0:T(8,128)(2,1)S(1)}, bf16[1536,1536]{1,0:T(8,128)(2,1)}, u32[]{:S(2)}) copy-start(bf16[1536,1536]{1,0:T(8,128)(2,1)} %weight_ref.1) | copy-start | bytes 14155780
  22.3 0.7 %copy-start.3 = (s32[2,8]{1,0:T(2,128)S(1)}, s32[2,8]{1,0:T(2,128)}, u32[]{:S(2)}) copy-start(s32[2,8]{1,0:T(2,128)} %picks_ref.1) | copy-start | bytes 196
  32.9 2.4 %collective-permute-start.5 = (bf16[2,128,1536]{2,1,0:T(8,128)(2,1)S(1)}, bf16[2,128,1536]{2,1,0:T(8,128)(2,1)S(1)}, u32[]{:S(2)}, u32[]{:S(2)}) collective-permute-start(bf16[2,128,1536]{2,1,0:T(8,128)(2,1)S(1)} %choose.3), channel_id=1, source_target_pairs={{0,1},{1,0},{2,3},{3,2},{4,5},{5,4},{6,7},{7,6},{8,9},{9,8},{10,11... | collective-permute-start | bytes 2359304 | tf_op jit(solution)/shard_map/ppermute | solution.py:269

commit v5 on v4

--- a/solution.py
+++ b/solution.py
@@ -15,10 +15,11 @@
 FAR = 8
 SCALE = HEAD_DIM ** (-0.5) * math.log2(math.e)
 UNUSED = -1e30
-LEAD = 2
+LEAD = 4
 NONE = 1 << 20
 
 STEPS = ((-4, 1, -1, 4), (4, 4, -4, -4), (3, -4, 4, -3))
+RELAYED = (4, 0, 0, -4)
 SIDE_STEPS = (2, 0, 0, -2)
 RELAY_STEPS = (0, 3, -3, 0)
 SWAP_STEPS = (1, -1, 1, -1)
@@ -35,20 +36,20 @@
 NT = (((1,), (1,)), ((), ()))
 
 
-def after_kernel(block_ref, before_ref, out_ref):
+def after_kernel(block_ref, out_ref):
     out_ref[...] = block_ref[...]
 
 
-def after(block, before, flops):
+def after(block, flops):
     return pl.pallas_call(
         after_kernel,
         out_shape=jax.ShapeDtypeStruct(block.shape, block.dtype),
-        in_specs=[VMEM, VMEM],
+        in_specs=[VMEM],
         out_specs=VMEM,
         cost_estimate=pl.CostEstimate(flops=flops, bytes_accessed=0, transcendentals=0),
         compiler_params=pltpu.CompilerParams(vmem_limit_bytes=4 * 1024 * 1024),
         name="after",
-    )(block, before)
+    )(block)
 
 
 def column_offset(column):
@@ -263,9 +264,9 @@
     )(bias, queries, acc, top, total, *rest)
 
 
-def moved(block, steps):
+def moved(block, steps, origins=(0, 0, 0, 0)):
     count = lax.axis_size("tm")
-    route = [(i, i + steps[i % 4]) for i in range(count) if steps[i % 4]]
+    route = [(i, i + steps[i % 4]) for i in range(count) if steps[i % 4] and 0 <= i + origins[i % 4] < count]
     return lax.ppermute(block, "tm", [(i, j) for i, j in route if 0 <= j < count])
 
 
@@ -276,12 +277,12 @@
     one = moved(pair, STEPS[0])
     two = moved(pair, STEPS[1])
     side = moved(pair, SIDE_STEPS)
-    three = moved(choose(index, one, pair), STEPS[2])
-    relay = after(moved(one, RELAY_STEPS), two, 10000000000)
+    three = moved(choose(index, one, pair), STEPS[2], RELAYED)
+    relay = after(moved(one, RELAY_STEPS), 10000000000)
     swap = moved(choose(index, three, one), SWAP_STEPS)
     mate = moved(pair, SWAP_STEPS)
     *state, held, bias = first(count, index, far_picks, queries, out_weight, pair, mate, one)
-    state = middle((0, 1), bias, queries, *state, two, side)
+    state = middle((0, 1), bias, queries, *state, after(two, 30000000000), side)
     state = middle((2,), bias, queries, *state, three)
     return last((3, 4), bias, queries, *state, swap, relay, held)
 

time: 38 us -> 37 us (0.974)
  local copies, waits for them, and re-layouts: 4.01 us -> 0.02 us
  waiting for transfers between devices: 12.3 us -> 14.5 us
  starting transfers between devices: 12.7 us -> 13.2 us
    unnamed x8, local copies, waits for them, and re-layouts: 4.01 us -> 0.02 us
    ppermute x7, waiting for transfers between devices: 12.3 us -> 14.5 us  [moved(): lax.ppermute(block, 'tm', [(i, j) for i, j in route if 0 <= j < count])]
    pallas_call x1 -> x2, Pallas kernels: 0.05 us -> 1.24 us  [after(): pl.pallas_call(after_kernel, out_shape=jax.ShapeDtypeStruct(block.shape,...]
    pallas_call x1, Pallas kernels: 2.75 us -> 2.04 us  [first(): pl.pallas_call(functools.partial(first_kernel, count), out_shape=(jax.Sha...]
    ppermute x7, starting transfers between devices: 12.7 us -> 13.2 us  [moved(): lax.ppermute(block, 'tm', [(i, j) for i, j in route if 0 <= j < count])]
  transfers between devices with their start and end apart: 7 -> 7, of which waited for: 4 -> 4; matrix products, arithmetic and copies ran while one was open for 0% -> 0% of each run, Pallas kernels for 13% -> 14%
where the time goes in v5:
time: 37 us; the launch traced here: 36.6 us
  waiting for transfers between devices  14.5 us (39%)
  starting transfers between devices  13.2 us (36%)
  Pallas kernels  7.49 us (20%)
  other arithmetic  1.19 us (3%)
    ppermute x7, waiting for transfers between devices, moved(): lax.ppermute(block, 'tm', [(i, j) for i, j in route if 0 <= j < count])  14.5 us
    ppermute x7, starting transfers between devices, moved(): lax.ppermute(block, 'tm', [(i, j) for i, j in route if 0 <= j < count])  13.2 us
    pallas_call x1, Pallas kernels, last(): pl.pallas_call(functools.partial(last_kernel, places), out_shape=jax.Shap...  2.34 us
    pallas_call x1, Pallas kernels, first(): pl.pallas_call(functools.partial(first_kernel, count), out_shape=(jax.Sha...  2.04 us
    pallas_call x2, Pallas kernels, middle(): pl.pallas_call(functools.partial(middle_kernel, places), out_shape=[jax.S...  1.78 us
    pallas_call x2, Pallas kernels, after(): pl.pallas_call(after_kernel, out_shape=jax.ShapeDtypeStruct(block.shape,...  1.24 us
    another operation x1, other arithmetic, body(): pair = jnp.stack([keys, values])  1.19 us
  transfers between devices with their start and end apart: 7, of which 4 were waited for; matrix products, arithmetic and copies ran while one was open for 0% of the time, Pallas kernels for 14%

profile of v5, /device:TPU:0, one launch (start us, length us, event | category | flops | bytes accessed | tf_op | source)
XLA Modules:
  0.0 36.6 jit_solution(14808466524001555844)
XLA Ops:
  0.0 1.2 %pad_maximum_fusion.own_ref.inner_ref = bf16[2,128,1536]{2,1,0:T(8,128)(2,1)S(1)} fusion(bf16[1,128,1536]{2,1,0:T(8,128)(2,1)} %bitcast.5, bf16[1,128,1536]{2,1,0:T(8,128)(2,1)} %bitcast.6), kind=kLoop, calls=%fused_computation | loop fusion | flops 393216 | bytes 1572864 | tf_op jit(solution)/shard_map/stack | solution.py:276
  1.2 1.3 %collective-permute-start.1 = (bf16[2,128,1536]{2,1,0:T(8,128)(2,1)S(1)}, bf16[2,128,1536]{2,1,0:T(8,128)(2,1)S(1)}, u32[]{:S(2)}, u32[]{:S(2)}) collective-permute-start(bf16[2,128,1536]{2,1,0:T(8,128)(2,1)S(1)} %pad_maximum_fusion.own_ref.inner_ref), channel_id=1, source_target_pairs={{1,2},{2,1},{3,7},{4,0},{5,6},{6,5},{7,11},{8,4},{9,10},{10,9},{11... | collective-permute-start | bytes 2359304 | tf_op jit(solution)/shard_map/ppermute | solution.py:270
  2.5 6.5 %collective-permute-start.2 = (bf16[2,128,1536]{2,1,0:T(8,128)(2,1)S(1)}, bf16[2,128,1536]{2,1,0:T(8,128)(2,1)}, u32[]{:S(2)}, u32[]{:S(2)}) collective-permute-start(bf16[2,128,1536]{2,1,0:T(8,128)(2,1)S(1)} %pad_maximum_fusion.own_ref.inner_ref), channel_id=1, source_target_pairs={{0,4},{1,5},{4,8},{5,9},{6,2},{7,3},{8,12},{9,13},{10,6},{11,7},{1... | collective-permute-start | bytes 2359304 | tf_op jit(solution)/shard_map/ppermute | solution.py:270
  9.0 1.3 %collective-permute-start = (bf16[2,128,1536]{2,1,0:T(8,128)(2,1)S(1)}, bf16[2,128,1536]{2,1,0:T(8,128)(2,1)S(1)}, u32[]{:S(2)}, u32[]{:S(2)}) collective-permute-start(bf16[2,128,1536]{2,1,0:T(8,128)(2,1)S(1)} %pad_maximum_fusion.own_ref.inner_ref), channel_id=1, source_target_pairs={{0,1},{1,0},{2,3},{3,2},{4,5},{5,4},{6,7},{7,6},{8,9},{9,8},{10,11... | collective-permute-start | bytes 2359304 | tf_op jit(solution)/shard_map/ppermute | solution.py:270
  10.3 1.3 %collective-permute-start.3 = (bf16[2,128,1536]{2,1,0:T(8,128)(2,1)S(1)}, bf16[2,128,1536]{2,1,0:T(8,128)(2,1)S(1)}, u32[]{:S(2)}, u32[]{:S(2)}) collective-permute-start(bf16[2,128,1536]{2,1,0:T(8,128)(2,1)S(1)} %pad_maximum_fusion.own_ref.inner_ref), channel_id=1, source_target_pairs={{0,2},{3,1},{4,6},{7,5},{8,10},{11,9},{12,14},{15,13},{16,18},{19,... | collective-permute-start | bytes 2359304 | tf_op jit(solution)/shard_map/ppermute | solution.py:270
  11.6 4.4 %collective-permute-done.1.one_ref.ends_ref.inner_ref = bf16[2,128,1536]{2,1,0:T(8,128)(2,1)S(1)} collective-permute-done((bf16[2,128,1536]{2,1,0:T(8,128)(2,1)S(1)}, bf16[2,128,1536]{2,1,0:T(8,128)(2,1)S(1)}, u32[]{:S(2)}, u32[]{:S(2)}) %collective-permute-start.1) | collective-permute-done | bytes 786464 | tf_op jit(solution)/shard_map/ppermute | solution.py:270
  16.1 0.0 slice-start
  16.1 0.1 choose.2
  16.1 0.0 copy-start
  16.2 0.0 slice-start.1
  16.2 0.0 copy-start.1
  16.2 2.0 %collective-permute-start.4 = (bf16[2,128,1536]{2,1,0:T(8,128)(2,1)S(1)}, bf16[2,128,1536]{2,1,0:T(8,128)(2,1)S(1)}, u32[]{:S(2)}, u32[]{:S(2)}) collective-permute-start(bf16[2,128,1536]{2,1,0:T(8,128)(2,1)S(1)} %choose.2), channel_id=1, source_target_pairs={{0,3},{2,6},{4,7},{5,1},{6,10},{7,4},{8,11},{9,5},{10,14},{11,8},{... | collective-permute-start | bytes 2359304 | tf_op jit(solution)/shard_map/ppermute | solution.py:270
  18.2 0.7 %collective-permute-start.6 = (bf16[2,128,1536]{2,1,0:T(8,128)(2,1)S(1)}, bf16[2,128,1536]{2,1,0:T(8,128)(2,1)S(1)}, u32[]{:S(2)}, u32[]{:S(2)}) collective-permute-start(bf16[2,128,1536]{2,1,0:T(8,128)(2,1)S(1)} %collective-permute-done.1.one_ref.ends_ref.inner_ref), channel_id=1, source_target_pairs={{1,4},{5,8},{6,3},{9,12},{10,7},{14,11},{17,20},{21,24},{22,19},{2... | collective-permute-start | bytes 2359304 | tf_op jit(solution)/shard_map/ppermute | solution.py:270
  18.9 6.5 %collective-permute-done.2.block_ref = bf16[2,128,1536]{2,1,0:T(8,128)(2,1)} collective-permute-done((bf16[2,128,1536]{2,1,0:T(8,128)(2,1)S(1)}, bf16[2,128,1536]{2,1,0:T(8,128)(2,1)}, u32[]{:S(2)}, u32[]{:S(2)}) %collective-permute-start.2) | collective-permute-done | bytes 786464 | tf_op jit(solution)/shard_map/ppermute | solution.py:270
  25.4 1.2 %after.2.refs_0_ = bf16[2,128,1536]{2,1,0:T(8,128)(2,1)S(1)} custom-call(bf16[2,128,1536]{2,1,0:T(8,128)(2,1)} %collective-permute-done.2.block_ref), custom_call_target="tpu_custom_call" | custom-call | flops 30000001024 | tf_op jit(solution)/shard_map/after/pallas_call | solution.py:44
  26.6 0.0 collective-permute-done.mate_ref
  26.6 0.0 slice-done
  26.6 0.0 copy-done
  26.6 0.0 slice-done.1
  26.6 0.0 copy-done.1
  26.6 2.0 %first.1 = (f32[128,1536]{1,0:T(8,128)S(1)}, f32[12,128,128]{2,1,0:T(8,128)S(1)}, f32[12,128,128]{2,1,0:T(8,128)S(1)}, bf16[1536,1536]{1,0:T(8,128)(2,1)S(1)}, f32[5,128,128]{2,1,0:T(8,128)S(1)}) custom-call(s32[1]{0:T(128)} %bitcast.index_ref, s32[2,8]{1,0:T(2,128)S(1)} %copy-done.1, bf16[128,1536]{1,0:T(8,128)(2,1)S(1)} %copy-done, ...), custom_call_target="tpu_custom_call" | custom-call | tf_op jit(solution)/shard_map/first/pallas_call | solution.py:205
  28.7 0.0 collective-permute-done.3.refs_1_
  28.7 1.0 %middle.2 = (f32[128,1536]{1,0:T(8,128)S(1)}, f32[12,128,128]{2,1,0:T(8,128)S(1)}, f32[12,128,128]{2,1,0:T(8,128)S(1)}) custom-call(f32[5,128,128]{2,1,0:T(8,128)S(1)} %get-tuple-element.16.bias_ref, bf16[128,1536]{1,0:T(8,128)(2,1)S(1)} %copy-done, f32[128,1536]{1,0:T(8,128)S(1)} %get-tuple-element.17.acc_ref, ...), custom_call_target="tpu_custom_call" | custom-call | tf_op jit(solution)/shard_map/middle/pallas_call | solution.py:232
  29.7 2.2 %collective-permute-done.4.refs_0_.ends_ref = bf16[2,128,1536]{2,1,0:T(8,128)(2,1)S(1)} collective-permute-done((bf16[2,128,1536]{2,1,0:T(8,128)(2,1)S(1)}, bf16[2,128,1536]{2,1,0:T(8,128)(2,1)S(1)}, u32[]{:S(2)}, u32[]{:S(2)}) %collective-permute-start.4) | collective-permute-done | bytes 786464 | tf_op jit(solution)/shard_map/ppermute | solution.py:270
  31.8 0.1 choose.3
  31.9 0.1 collective-permute-start.5
  32.0 0.8 %middle.3 = (f32[128,1536]{1,0:T(8,128)S(1)}, f32[12,128,128]{2,1,0:T(8,128)S(1)}, f32[12,128,128]{2,1,0:T(8,128)S(1)}) custom-call(f32[5,128,128]{2,1,0:T(8,128)S(1)} %get-tuple-element.16.bias_ref, bf16[128,1536]{1,0:T(8,128)(2,1)S(1)} %copy-done, f32[128,1536]{1,0:T(8,128)S(1)} %get-tuple-element.20.acc_ref, ...), custom_call_target="tpu_custom_call" | custom-call | tf_op jit(solution)/shard_map/middle/pallas_call | solution.py:232
  32.8 0.0 collective-permute-done.6.block_ref
  32.8 0.1 after.3.relay_ref
  32.8 1.4 %collective-permute-done.5.swap_ref = bf16[2,128,1536]{2,1,0:T(8,128)(2,1)S(1)} collective-permute-done((bf16[2,128,1536]{2,1,0:T(8,128)(2,1)S(1)}, bf16[2,128,1536]{2,1,0:T(8,128)(2,1)S(1)}, u32[]{:S(2)}, u32[]{:S(2)}) %collective-permute-start.5) | collective-permute-done | bytes 786464 | tf_op jit(solution)/shard_map/ppermute | solution.py:270
  34.2 2.3 %last.1 = bf16[128,1536]{1,0:T(8,128)(2,1)} custom-call(f32[5,128,128]{2,1,0:T(8,128)S(1)} %get-tuple-element.16.bias_ref, bf16[128,1536]{1,0:T(8,128)(2,1)S(1)} %copy-done, f32[128,1536]{1,0:T(8,128)S(1)} %get-tuple-element.23.acc_ref, f32[12,128,128]{2,1,0:T(8,128)S(1)} %get-tuple-element.24.top_ref, f32[12,128,128]{2,1,0:T(8,128)S(1)} %get-tuple-element.25.total_ref, ...), custom_call_target="tpu_custom_call" | custom-call | tf_op jit(solution)/shard_map/last/pallas_call | solution.py:256
  (1 shorter events, 0.0 us)
Async XLA Ops:
  1.2 14.9 %collective-permute-start.1 = (bf16[2,128,1536]{2,1,0:T(8,128)(2,1)S(1)}, bf16[2,128,1536]{2,1,0:T(8,128)(2,1)S(1)}, u32[]{:S(2)}, u32[]{:S(2)}) collective-permute-start(bf16[2,128,1536]{2,1,0:T(8,128)(2,1)S(1)} %pad_maximum_fusion.own_ref.inner_ref), channel_id=1, source_target_pairs={{1,2},{2,1},{3,7},{4,0},{5,6},{6,5},{7,11},{8,4},{9,10},{10,9},{11... | collective-permute-start | bytes 2359304 | tf_op jit(solution)/shard_map/ppermute | solution.py:270
  2.5 22.9 %collective-permute-start.2 = (bf16[2,128,1536]{2,1,0:T(8,128)(2,1)S(1)}, bf16[2,128,1536]{2,1,0:T(8,128)(2,1)}, u32[]{:S(2)}, u32[]{:S(2)}) collective-permute-start(bf16[2,128,1536]{2,1,0:T(8,128)(2,1)S(1)} %pad_maximum_fusion.own_ref.inner_ref), channel_id=1, source_target_pairs={{0,4},{1,5},{4,8},{5,9},{6,2},{7,3},{8,12},{9,13},{10,6},{11,7},{1... | collective-permute-start | bytes 2359304 | tf_op jit(solution)/shard_map/ppermute | solution.py:270
  9.0 17.6 %collective-permute-start = (bf16[2,128,1536]{2,1,0:T(8,128)(2,1)S(1)}, bf16[2,128,1536]{2,1,0:T(8,128)(2,1)S(1)}, u32[]{:S(2)}, u32[]{:S(2)}) collective-permute-start(bf16[2,128,1536]{2,1,0:T(8,128)(2,1)S(1)} %pad_maximum_fusion.own_ref.inner_ref), channel_id=1, source_target_pairs={{0,1},{1,0},{2,3},{3,2},{4,5},{5,4},{6,7},{7,6},{8,9},{9,8},{10,11... | collective-permute-start | bytes 2359304 | tf_op jit(solution)/shard_map/ppermute | solution.py:270
  10.3 18.4 %collective-permute-start.3 = (bf16[2,128,1536]{2,1,0:T(8,128)(2,1)S(1)}, bf16[2,128,1536]{2,1,0:T(8,128)(2,1)S(1)}, u32[]{:S(2)}, u32[]{:S(2)}) collective-permute-start(bf16[2,128,1536]{2,1,0:T(8,128)(2,1)S(1)} %pad_maximum_fusion.own_ref.inner_ref), channel_id=1, source_target_pairs={{0,2},{3,1},{4,6},{7,5},{8,10},{11,9},{12,14},{15,13},{16,18},{19,... | collective-permute-start | bytes 2359304 | tf_op jit(solution)/shard_map/ppermute | solution.py:270
  16.1 10.5 %slice-start = ((s8[4718592]{0:T(1024)(128)(4,1)}), s8[4194304]{0:T(1024)(128)(4,1)S(1)}, s32[]{:S(2)}) async-start(s8[4718592]{0:T(1024)(128)(4,1)} %bitcast.3), calls=%async_computation | async-start | bytes 8388608
  16.1 10.4 %copy-start = (bf16[128,1536]{1,0:T(8,128)(2,1)S(1)}, bf16[128,1536]{1,0:T(8,128)(2,1)}, u32[]{:S(2)}) copy-start(bf16[128,1536]{1,0:T(8,128)(2,1)} %q_ref.7) | copy-start | bytes 1179652
  16.2 10.4 %slice-start.1 = ((s8[4718592]{0:T(1024)(128)(4,1)}), s8[524288]{0:T(1024)(128)(4,1)S(1)}, s32[]{:S(2)}) async-start(s8[4718592]{0:T(1024)(128)(4,1)} %bitcast.3), calls=%async_computation.1 | async-start | bytes 1048576
  16.2 10.4 %copy-start.1 = (s32[2,8]{1,0:T(2,128)S(1)}, s32[2,8]{1,0:T(2,128)}, u32[]{:S(2)}) copy-start(s32[2,8]{1,0:T(2,128)} %picks_ref.1) | copy-start | bytes 196
  16.2 15.7 %collective-permute-start.4 = (bf16[2,128,1536]{2,1,0:T(8,128)(2,1)S(1)}, bf16[2,128,1536]{2,1,0:T(8,128)(2,1)S(1)}, u32[]{:S(2)}, u32[]{:S(2)}) collective-permute-start(bf16[2,128,1536]{2,1,0:T(8,128)(2,1)S(1)} %choose.2), channel_id=1, source_target_pairs={{0,3},{2,6},{4,7},{5,1},{6,10},{7,4},{8,11},{9,5},{10,14},{11,8},{... | collective-permute-start | bytes 2359304 | tf_op jit(solution)/shard_map/ppermute | solution.py:270
  18.2 14.6 %collective-permute-start.6 = (bf16[2,128,1536]{2,1,0:T(8,128)(2,1)S(1)}, bf16[2,128,1536]{2,1,0:T(8,128)(2,1)S(1)}, u32[]{:S(2)}, u32[]{:S(2)}) collective-permute-start(bf16[2,128,1536]{2,1,0:T(8,128)(2,1)S(1)} %collective-permute-done.1.one_ref.ends_ref.inner_ref), channel_id=1, source_target_pairs={{1,4},{5,8},{6,3},{9,12},{10,7},{14,11},{17,20},{21,24},{22,19},{2... | collective-permute-start | bytes 2359304 | tf_op jit(solution)/shard_map/ppermute | solution.py:270
  31.9 2.4 %collective-permute-start.5 = (bf16[2,128,1536]{2,1,0:T(8,128)(2,1)S(1)}, bf16[2,128,1536]{2,1,0:T(8,128)(2,1)S(1)}, u32[]{:S(2)}, u32[]{:S(2)}) collective-permute-start(bf16[2,128,1536]{2,1,0:T(8,128)(2,1)S(1)} %choose.3), channel_id=1, source_target_pairs={{0,1},{1,0},{2,3},{3,2},{4,5},{5,4},{6,7},{7,6},{8,9},{9,8},{10,11... | collective-permute-start | bytes 2359304 | tf_op jit(solution)/shard_map/ppermute | solution.py:270

commit v6 on v5

--- a/solution.py
+++ b/solution.py
@@ -16,6 +16,7 @@
 SCALE = HEAD_DIM ** (-0.5) * math.log2(math.e)
 UNUSED = -1e30
 LEAD = 4
+PIECES = 2
 NONE = 1 << 20
 
 STEPS = ((-4, 1, -1, 4), (4, 4, -4, -4), (3, -4, 4, -3))
@@ -241,14 +242,23 @@
 
 def last_kernel(
     places, bias_ref, q_ref, acc_ref, top_ref, total_ref, swap_ref, relay_ref, weight_ref, out_ref,
-    attended_ref
+    attended_ref, mixed_ref, sems
 ):
     def finish(head, top, kept, total, summed):
         cols = head_columns(head)
         attended_ref[:, cols] = ((acc_ref[:, cols] * kept + summed) / total).astype(jnp.bfloat16)
 
     attend(q_ref, (swap_ref, relay_ref), [bias_ref[i] for i in places], top_ref, total_ref, finish)
-    out_ref[...] = jnp.dot(attended_ref[...], weight_ref[...], preferred_element_type=jnp.float32).astype(jnp.bfloat16)
+    piece = q_ref.shape[1] // PIECES
+    copies = []
+    for i in range(PIECES):
+        cols = pl.ds(i * piece, piece)
+        part = jnp.dot(attended_ref[...], weight_ref[:, cols], preferred_element_type=jnp.float32)
+        mixed_ref[:, cols] = part.astype(jnp.bfloat16)
+        copies.append(pltpu.make_async_copy(mixed_ref.at[:, cols], out_ref.at[:, cols], sems.at[i]))
+        copies[-1].start()
+    for copy in copies:
+        copy.wait()
 
 
 def last(places, bias, queries, acc, top, total, *rest):
@@ -257,8 +267,12 @@
         functools.partial(last_kernel, places),
         out_shape=jax.ShapeDtypeStruct((rows, width), jnp.bfloat16),
         in_specs=[VMEM] * (5 + len(rest)),
-        out_specs=VMEM,
-        scratch_shapes=[pltpu.VMEM((rows, width), jnp.bfloat16)],
+        out_specs=ANY,
+        scratch_shapes=[
+            pltpu.VMEM((rows, width), jnp.bfloat16),
+            pltpu.VMEM((rows, width), jnp.bfloat16),
+            pltpu.SemaphoreType.DMA((PIECES,)),
+        ],
         compiler_params=pltpu.CompilerParams(vmem_limit_bytes=16 * 1024 * 1024),
         name="last",
     )(bias, queries, acc, top, total, *rest)
@@ -282,8 +296,8 @@
     swap = moved(choose(index, three, one), SWAP_STEPS)
     mate = moved(pair, SWAP_STEPS)
     *state, held, bias = first(count, index, far_picks, queries, out_weight, pair, mate, one)
-    state = middle((0, 1), bias, queries, *state, after(two, 30000000000), side)
-    state = middle((2,), bias, queries, *state, three)
+    state = middle((0,), bias, queries, *state, after(two, 30000000000))
+    state = middle((1, 2), bias, queries, *state, side, three)
     return last((3, 4), bias, queries, *state, swap, relay, held)
 
 

time: 37 us -> 36.9 us (level)
  no operation moved by 1% of the time
where the time goes in v6:
time: 36.9 us; the launch traced here: 36.5 us
  waiting for transfers between devices  14.4 us (39%)
  starting transfers between devices  13.2 us (36%)
  Pallas kernels  7.5 us (20%)
  other arithmetic  1.19 us (3%)
    ppermute x7, waiting for transfers between devices, moved(): lax.ppermute(block, 'tm', [(i, j) for i, j in route if 0 <= j < count])  14.4 us
    ppermute x7, starting transfers between devices, moved(): lax.ppermute(block, 'tm', [(i, j) for i, j in route if 0 <= j < count])  13.2 us
    pallas_call x1, Pallas kernels, last(): pl.pallas_call(functools.partial(last_kernel, places), out_shape=jax.Shap...  2.28 us
    pallas_call x1, Pallas kernels, first(): pl.pallas_call(functools.partial(first_kernel, count), out_shape=(jax.Sha...  2.07 us
    pallas_call x2, Pallas kernels, middle(): pl.pallas_call(functools.partial(middle_kernel, places), out_shape=[jax.S...  1.82 us
    pallas_call x2, Pallas kernels, after(): pl.pallas_call(after_kernel, out_shape=jax.ShapeDtypeStruct(block.shape,...  1.24 us
    another operation x1, other arithmetic, body(): pair = jnp.stack([keys, values])  1.19 us
  transfers between devices with their start and end apart: 7, of which 4 were waited for; matrix products, arithmetic and copies ran while one was open for 0% of the time, Pallas kernels for 14%

profile of v6, /device:TPU:0, one launch (start us, length us, event | category | flops | bytes accessed | tf_op | source)
XLA Modules:
  0.0 36.5 jit_solution(274915629192761043)
XLA Ops:
  0.0 1.2 %pad_maximum_fusion.own_ref.inner_ref = bf16[2,128,1536]{2,1,0:T(8,128)(2,1)S(1)} fusion(bf16[1,128,1536]{2,1,0:T(8,128)(2,1)} %bitcast.5, bf16[1,128,1536]{2,1,0:T(8,128)(2,1)} %bitcast.6), kind=kLoop, calls=%fused_computation | loop fusion | flops 393216 | bytes 1572864 | tf_op jit(solution)/shard_map/stack | solution.py:290
  1.2 1.3 %collective-permute-start.1 = (bf16[2,128,1536]{2,1,0:T(8,128)(2,1)S(1)}, bf16[2,128,1536]{2,1,0:T(8,128)(2,1)S(1)}, u32[]{:S(2)}, u32[]{:S(2)}) collective-permute-start(bf16[2,128,1536]{2,1,0:T(8,128)(2,1)S(1)} %pad_maximum_fusion.own_ref.inner_ref), channel_id=1, source_target_pairs={{1,2},{2,1},{3,7},{4,0},{5,6},{6,5},{7,11},{8,4},{9,10},{10,9},{11... | collective-permute-start | bytes 2359304 | tf_op jit(solution)/shard_map/ppermute | solution.py:284
  2.5 6.5 %collective-permute-start.2 = (bf16[2,128,1536]{2,1,0:T(8,128)(2,1)S(1)}, bf16[2,128,1536]{2,1,0:T(8,128)(2,1)}, u32[]{:S(2)}, u32[]{:S(2)}) collective-permute-start(bf16[2,128,1536]{2,1,0:T(8,128)(2,1)S(1)} %pad_maximum_fusion.own_ref.inner_ref), channel_id=1, source_target_pairs={{0,4},{1,5},{4,8},{5,9},{6,2},{7,3},{8,12},{9,13},{10,6},{11,7},{1... | collective-permute-start | bytes 2359304 | tf_op jit(solution)/shard_map/ppermute | solution.py:284
  9.0 1.3 %collective-permute-start = (bf16[2,128,1536]{2,1,0:T(8,128)(2,1)S(1)}, bf16[2,128,1536]{2,1,0:T(8,128)(2,1)S(1)}, u32[]{:S(2)}, u32[]{:S(2)}) collective-permute-start(bf16[2,128,1536]{2,1,0:T(8,128)(2,1)S(1)} %pad_maximum_fusion.own_ref.inner_ref), channel_id=1, source_target_pairs={{0,1},{1,0},{2,3},{3,2},{4,5},{5,4},{6,7},{7,6},{8,9},{9,8},{10,11... | collective-permute-start | bytes 2359304 | tf_op jit(solution)/shard_map/ppermute | solution.py:284
  10.3 1.3 %collective-permute-start.3 = (bf16[2,128,1536]{2,1,0:T(8,128)(2,1)S(1)}, bf16[2,128,1536]{2,1,0:T(8,128)(2,1)S(1)}, u32[]{:S(2)}, u32[]{:S(2)}) collective-permute-start(bf16[2,128,1536]{2,1,0:T(8,128)(2,1)S(1)} %pad_maximum_fusion.own_ref.inner_ref), channel_id=1, source_target_pairs={{0,2},{3,1},{4,6},{7,5},{8,10},{11,9},{12,14},{15,13},{16,18},{19,... | collective-permute-start | bytes 2359304 | tf_op jit(solution)/shard_map/ppermute | solution.py:284
  11.6 4.4 %collective-permute-done.1.one_ref.ends_ref.inner_ref = bf16[2,128,1536]{2,1,0:T(8,128)(2,1)S(1)} collective-permute-done((bf16[2,128,1536]{2,1,0:T(8,128)(2,1)S(1)}, bf16[2,128,1536]{2,1,0:T(8,128)(2,1)S(1)}, u32[]{:S(2)}, u32[]{:S(2)}) %collective-permute-start.1) | collective-permute-done | bytes 786464 | tf_op jit(solution)/shard_map/ppermute | solution.py:284
  16.1 0.0 slice-start
  16.1 0.1 choose.2
  16.1 0.0 copy-start
  16.2 0.0 slice-start.1
  16.2 0.0 copy-start.1
  16.2 2.0 %collective-permute-start.4 = (bf16[2,128,1536]{2,1,0:T(8,128)(2,1)S(1)}, bf16[2,128,1536]{2,1,0:T(8,128)(2,1)S(1)}, u32[]{:S(2)}, u32[]{:S(2)}) collective-permute-start(bf16[2,128,1536]{2,1,0:T(8,128)(2,1)S(1)} %choose.2), channel_id=1, source_target_pairs={{0,3},{2,6},{4,7},{5,1},{6,10},{7,4},{8,11},{9,5},{10,14},{11,8},{... | collective-permute-start | bytes 2359304 | tf_op jit(solution)/shard_map/ppermute | solution.py:284
  18.2 0.7 %collective-permute-start.6 = (bf16[2,128,1536]{2,1,0:T(8,128)(2,1)S(1)}, bf16[2,128,1536]{2,1,0:T(8,128)(2,1)S(1)}, u32[]{:S(2)}, u32[]{:S(2)}) collective-permute-start(bf16[2,128,1536]{2,1,0:T(8,128)(2,1)S(1)} %collective-permute-done.1.one_ref.ends_ref.inner_ref), channel_id=1, source_target_pairs={{1,4},{5,8},{6,3},{9,12},{10,7},{14,11},{17,20},{21,24},{22,19},{2... | collective-permute-start | bytes 2359304 | tf_op jit(solution)/shard_map/ppermute | solution.py:284
  18.9 6.5 %collective-permute-done.2.block_ref = bf16[2,128,1536]{2,1,0:T(8,128)(2,1)} collective-permute-done((bf16[2,128,1536]{2,1,0:T(8,128)(2,1)S(1)}, bf16[2,128,1536]{2,1,0:T(8,128)(2,1)}, u32[]{:S(2)}, u32[]{:S(2)}) %collective-permute-start.2) | collective-permute-done | bytes 786464 | tf_op jit(solution)/shard_map/ppermute | solution.py:284
  25.4 1.2 %after.2.refs_0_ = bf16[2,128,1536]{2,1,0:T(8,128)(2,1)S(1)} custom-call(bf16[2,128,1536]{2,1,0:T(8,128)(2,1)} %collective-permute-done.2.block_ref), custom_call_target="tpu_custom_call" | custom-call | flops 30000001024 | tf_op jit(solution)/shard_map/after/pallas_call | solution.py:45
  26.6 0.0 collective-permute-done.mate_ref
  26.6 0.0 slice-done
  26.6 0.0 copy-done
  26.6 0.0 slice-done.1
  26.6 0.0 copy-done.1
  26.6 2.1 %first.1 = (f32[128,1536]{1,0:T(8,128)S(1)}, f32[12,128,128]{2,1,0:T(8,128)S(1)}, f32[12,128,128]{2,1,0:T(8,128)S(1)}, bf16[1536,1536]{1,0:T(8,128)(2,1)S(1)}, f32[5,128,128]{2,1,0:T(8,128)S(1)}) custom-call(s32[1]{0:T(128)} %bitcast.index_ref, s32[2,8]{1,0:T(2,128)S(1)} %copy-done.1, bf16[128,1536]{1,0:T(8,128)(2,1)S(1)} %copy-done, ...), custom_call_target="tpu_custom_call" | custom-call | tf_op jit(solution)/shard_map/first/pallas_call | solution.py:206
  28.7 0.8 %middle.2 = (f32[128,1536]{1,0:T(8,128)S(1)}, f32[12,128,128]{2,1,0:T(8,128)S(1)}, f32[12,128,128]{2,1,0:T(8,128)S(1)}) custom-call(f32[5,128,128]{2,1,0:T(8,128)S(1)} %get-tuple-element.16.bias_ref, bf16[128,1536]{1,0:T(8,128)(2,1)S(1)} %copy-done, f32[128,1536]{1,0:T(8,128)S(1)} %get-tuple-element.17.acc_ref, ...), custom_call_target="tpu_custom_call" | custom-call | tf_op jit(solution)/shard_map/middle/pallas_call | solution.py:233
  29.5 2.3 %collective-permute-done.4.refs_1_.ends_ref = bf16[2,128,1536]{2,1,0:T(8,128)(2,1)S(1)} collective-permute-done((bf16[2,128,1536]{2,1,0:T(8,128)(2,1)S(1)}, bf16[2,128,1536]{2,1,0:T(8,128)(2,1)S(1)}, u32[]{:S(2)}, u32[]{:S(2)}) %collective-permute-start.4) | collective-permute-done | bytes 786464 | tf_op jit(solution)/shard_map/ppermute | solution.py:284
  31.8 0.1 choose.3
  31.9 0.1 collective-permute-start.5
  32.0 0.0 collective-permute-done.3.refs_0_
  32.0 1.0 %middle.3 = (f32[128,1536]{1,0:T(8,128)S(1)}, f32[12,128,128]{2,1,0:T(8,128)S(1)}, f32[12,128,128]{2,1,0:T(8,128)S(1)}) custom-call(f32[5,128,128]{2,1,0:T(8,128)S(1)} %get-tuple-element.16.bias_ref, bf16[128,1536]{1,0:T(8,128)(2,1)S(1)} %copy-done, f32[128,1536]{1,0:T(8,128)S(1)} %get-tuple-element.20.acc_ref, ...), custom_call_target="tpu_custom_call" | custom-call | tf_op jit(solution)/shard_map/middle/pallas_call | solution.py:233
  33.0 0.0 collective-permute-done.6.block_ref
  33.0 0.1 after.3.relay_ref
  33.1 1.2 %collective-permute-done.5.swap_ref = bf16[2,128,1536]{2,1,0:T(8,128)(2,1)S(1)} collective-permute-done((bf16[2,128,1536]{2,1,0:T(8,128)(2,1)S(1)}, bf16[2,128,1536]{2,1,0:T(8,128)(2,1)S(1)}, u32[]{:S(2)}, u32[]{:S(2)}) %collective-permute-start.5) | collective-permute-done | bytes 786464 | tf_op jit(solution)/shard_map/ppermute | solution.py:284
  34.2 2.3 %last.1 = bf16[128,1536]{1,0:T(8,128)(2,1)} custom-call(f32[5,128,128]{2,1,0:T(8,128)S(1)} %get-tuple-element.16.bias_ref, bf16[128,1536]{1,0:T(8,128)(2,1)S(1)} %copy-done, f32[128,1536]{1,0:T(8,128)S(1)} %get-tuple-element.23.acc_ref, f32[12,128,128]{2,1,0:T(8,128)S(1)} %get-tuple-element.24.top_ref, f32[12,128,128]{2,1,0:T(8,128)S(1)} %get-tuple-element.25.total_ref, ...), custom_call_target="tpu_custom_call" | custom-call | tf_op jit(solution)/shard_map/last/pallas_call | solution.py:266
  (1 shorter events, 0.0 us)
Async XLA Ops:
  1.2 14.9 %collective-permute-start.1 = (bf16[2,128,1536]{2,1,0:T(8,128)(2,1)S(1)}, bf16[2,128,1536]{2,1,0:T(8,128)(2,1)S(1)}, u32[]{:S(2)}, u32[]{:S(2)}) collective-permute-start(bf16[2,128,1536]{2,1,0:T(8,128)(2,1)S(1)} %pad_maximum_fusion.own_ref.inner_ref), channel_id=1, source_target_pairs={{1,2},{2,1},{3,7},{4,0},{5,6},{6,5},{7,11},{8,4},{9,10},{10,9},{11... | collective-permute-start | bytes 2359304 | tf_op jit(solution)/shard_map/ppermute | solution.py:284
  2.5 22.9 %collective-permute-start.2 = (bf16[2,128,1536]{2,1,0:T(8,128)(2,1)S(1)}, bf16[2,128,1536]{2,1,0:T(8,128)(2,1)}, u32[]{:S(2)}, u32[]{:S(2)}) collective-permute-start(bf16[2,128,1536]{2,1,0:T(8,128)(2,1)S(1)} %pad_maximum_fusion.own_ref.inner_ref), channel_id=1, source_target_pairs={{0,4},{1,5},{4,8},{5,9},{6,2},{7,3},{8,12},{9,13},{10,6},{11,7},{1... | collective-permute-start | bytes 2359304 | tf_op jit(solution)/shard_map/ppermute | solution.py:284
  9.0 17.6 %collective-permute-start = (bf16[2,128,1536]{2,1,0:T(8,128)(2,1)S(1)}, bf16[2,128,1536]{2,1,0:T(8,128)(2,1)S(1)}, u32[]{:S(2)}, u32[]{:S(2)}) collective-permute-start(bf16[2,128,1536]{2,1,0:T(8,128)(2,1)S(1)} %pad_maximum_fusion.own_ref.inner_ref), channel_id=1, source_target_pairs={{0,1},{1,0},{2,3},{3,2},{4,5},{5,4},{6,7},{7,6},{8,9},{9,8},{10,11... | collective-permute-start | bytes 2359304 | tf_op jit(solution)/shard_map/ppermute | solution.py:284
  10.3 21.7 %collective-permute-start.3 = (bf16[2,128,1536]{2,1,0:T(8,128)(2,1)S(1)}, bf16[2,128,1536]{2,1,0:T(8,128)(2,1)S(1)}, u32[]{:S(2)}, u32[]{:S(2)}) collective-permute-start(bf16[2,128,1536]{2,1,0:T(8,128)(2,1)S(1)} %pad_maximum_fusion.own_ref.inner_ref), channel_id=1, source_target_pairs={{0,2},{3,1},{4,6},{7,5},{8,10},{11,9},{12,14},{15,13},{16,18},{19,... | collective-permute-start | bytes 2359304 | tf_op jit(solution)/shard_map/ppermute | solution.py:284
  16.1 10.5 %slice-start = ((s8[4718592]{0:T(1024)(128)(4,1)}), s8[4194304]{0:T(1024)(128)(4,1)S(1)}, s32[]{:S(2)}) async-start(s8[4718592]{0:T(1024)(128)(4,1)} %bitcast.3), calls=%async_computation | async-start | bytes 8388608
  16.1 10.4 %copy-start = (bf16[128,1536]{1,0:T(8,128)(2,1)S(1)}, bf16[128,1536]{1,0:T(8,128)(2,1)}, u32[]{:S(2)}) copy-start(bf16[128,1536]{1,0:T(8,128)(2,1)} %q_ref.7) | copy-start | bytes 1179652
  16.2 10.4 %slice-start.1 = ((s8[4718592]{0:T(1024)(128)(4,1)}), s8[524288]{0:T(1024)(128)(4,1)S(1)}, s32[]{:S(2)}) async-start(s8[4718592]{0:T(1024)(128)(4,1)} %bitcast.3), calls=%async_computation.1 | async-start | bytes 1048576
  16.2 10.4 %copy-start.1 = (s32[2,8]{1,0:T(2,128)S(1)}, s32[2,8]{1,0:T(2,128)}, u32[]{:S(2)}) copy-start(s32[2,8]{1,0:T(2,128)} %picks_ref.1) | copy-start | bytes 196
  16.2 15.7 %collective-permute-start.4 = (bf16[2,128,1536]{2,1,0:T(8,128)(2,1)S(1)}, bf16[2,128,1536]{2,1,0:T(8,128)(2,1)S(1)}, u32[]{:S(2)}, u32[]{:S(2)}) collective-permute-start(bf16[2,128,1536]{2,1,0:T(8,128)(2,1)S(1)} %choose.2), channel_id=1, source_target_pairs={{0,3},{2,6},{4,7},{5,1},{6,10},{7,4},{8,11},{9,5},{10,14},{11,8},{... | collective-permute-start | bytes 2359304 | tf_op jit(solution)/shard_map/ppermute | solution.py:284
  18.2 14.8 %collective-permute-start.6 = (bf16[2,128,1536]{2,1,0:T(8,128)(2,1)S(1)}, bf16[2,128,1536]{2,1,0:T(8,128)(2,1)S(1)}, u32[]{:S(2)}, u32[]{:S(2)}) collective-permute-start(bf16[2,128,1536]{2,1,0:T(8,128)(2,1)S(1)} %collective-permute-done.1.one_ref.ends_ref.inner_ref), channel_id=1, source_target_pairs={{1,4},{5,8},{6,3},{9,12},{10,7},{14,11},{17,20},{21,24},{22,19},{2... | collective-permute-start | bytes 2359304 | tf_op jit(solution)/shard_map/ppermute | solution.py:284
  31.9 2.4 %collective-permute-start.5 = (bf16[2,128,1536]{2,1,0:T(8,128)(2,1)S(1)}, bf16[2,128,1536]{2,1,0:T(8,128)(2,1)S(1)}, u32[]{:S(2)}, u32[]{:S(2)}) collective-permute-start(bf16[2,128,1536]{2,1,0:T(8,128)(2,1)S(1)} %choose.3), channel_id=1, source_target_pairs={{0,1},{1,0},{2,3},{3,2},{4,5},{5,4},{6,7},{7,6},{8,9},{9,8},{10,11... | collective-permute-start | bytes 2359304 | tf_op jit(solution)/shard_map/ppermute | solution.py:284

commit v7 on v6

--- a/solution.py
+++ b/solution.py
@@ -15,7 +15,7 @@
 FAR = 8
 SCALE = HEAD_DIM ** (-0.5) * math.log2(math.e)
 UNUSED = -1e30
-LEAD = 4
+LEAD = 6
 PIECES = 2
 NONE = 1 << 20
 

time: 36.9 us -> 37 us (level)
  no operation moved by 1% of the time
where the time goes in v7:
time: 37 us; the launch traced here: 36.6 us
  waiting for transfers between devices  14.4 us (39%)
  starting transfers between devices  13.2 us (36%)
  Pallas kernels  7.6 us (21%)
  other arithmetic  1.19 us (3%)
    ppermute x7, waiting for transfers between devices, moved(): lax.ppermute(block, 'tm', [(i, j) for i, j in route if 0 <= j < count])  14.4 us
    ppermute x7, starting transfers between devices, moved(): lax.ppermute(block, 'tm', [(i, j) for i, j in route if 0 <= j < count])  13.2 us
    pallas_call x1, Pallas kernels, last(): pl.pallas_call(functools.partial(last_kernel, places), out_shape=jax.Shap...  2.32 us
    pallas_call x1, Pallas kernels, first(): pl.pallas_call(functools.partial(first_kernel, count), out_shape=(jax.Sha...  2.12 us
    pallas_call x2, Pallas kernels, middle(): pl.pallas_call(functools.partial(middle_kernel, places), out_shape=[jax.S...  1.82 us
    pallas_call x2, Pallas kernels, after(): pl.pallas_call(after_kernel, out_shape=jax.ShapeDtypeStruct(block.shape,...  1.24 us
    another operation x1, other arithmetic, body(): pair = jnp.stack([keys, values])  1.19 us
  transfers between devices with their start and end apart: 7, of which 4 were waited for; matrix products, arithmetic and copies ran while one was open for 0% of the time, Pallas kernels for 14%

profile of v7, /device:TPU:0, one launch (start us, length us, event | category | flops | bytes accessed | tf_op | source)
XLA Modules:
  0.0 36.6 jit_solution(4155775211401624625)
XLA Ops:
  0.0 1.2 %pad_maximum_fusion.own_ref.inner_ref = bf16[2,128,1536]{2,1,0:T(8,128)(2,1)S(1)} fusion(bf16[1,128,1536]{2,1,0:T(8,128)(2,1)} %bitcast.5, bf16[1,128,1536]{2,1,0:T(8,128)(2,1)} %bitcast.6), kind=kLoop, calls=%fused_computation | loop fusion | flops 393216 | bytes 1572864 | tf_op jit(solution)/shard_map/stack | solution.py:290
  1.2 1.3 %collective-permute-start.1 = (bf16[2,128,1536]{2,1,0:T(8,128)(2,1)S(1)}, bf16[2,128,1536]{2,1,0:T(8,128)(2,1)S(1)}, u32[]{:S(2)}, u32[]{:S(2)}) collective-permute-start(bf16[2,128,1536]{2,1,0:T(8,128)(2,1)S(1)} %pad_maximum_fusion.own_ref.inner_ref), channel_id=1, source_target_pairs={{1,2},{2,1},{3,7},{4,0},{5,6},{6,5},{7,11},{8,4},{9,10},{10,9},{11... | collective-permute-start | bytes 2359304 | tf_op jit(solution)/shard_map/ppermute | solution.py:284
  2.5 6.5 %collective-permute-start.2 = (bf16[2,128,1536]{2,1,0:T(8,128)(2,1)S(1)}, bf16[2,128,1536]{2,1,0:T(8,128)(2,1)}, u32[]{:S(2)}, u32[]{:S(2)}) collective-permute-start(bf16[2,128,1536]{2,1,0:T(8,128)(2,1)S(1)} %pad_maximum_fusion.own_ref.inner_ref), channel_id=1, source_target_pairs={{0,4},{1,5},{4,8},{5,9},{6,2},{7,3},{8,12},{9,13},{10,6},{11,7},{1... | collective-permute-start | bytes 2359304 | tf_op jit(solution)/shard_map/ppermute | solution.py:284
  9.0 1.3 %collective-permute-start = (bf16[2,128,1536]{2,1,0:T(8,128)(2,1)S(1)}, bf16[2,128,1536]{2,1,0:T(8,128)(2,1)S(1)}, u32[]{:S(2)}, u32[]{:S(2)}) collective-permute-start(bf16[2,128,1536]{2,1,0:T(8,128)(2,1)S(1)} %pad_maximum_fusion.own_ref.inner_ref), channel_id=1, source_target_pairs={{0,1},{1,0},{2,3},{3,2},{4,5},{5,4},{6,7},{7,6},{8,9},{9,8},{10,11... | collective-permute-start | bytes 2359304 | tf_op jit(solution)/shard_map/ppermute | solution.py:284
  10.3 1.3 %collective-permute-start.3 = (bf16[2,128,1536]{2,1,0:T(8,128)(2,1)S(1)}, bf16[2,128,1536]{2,1,0:T(8,128)(2,1)S(1)}, u32[]{:S(2)}, u32[]{:S(2)}) collective-permute-start(bf16[2,128,1536]{2,1,0:T(8,128)(2,1)S(1)} %pad_maximum_fusion.own_ref.inner_ref), channel_id=1, source_target_pairs={{0,2},{3,1},{4,6},{7,5},{8,10},{11,9},{12,14},{15,13},{16,18},{19,... | collective-permute-start | bytes 2359304 | tf_op jit(solution)/shard_map/ppermute | solution.py:284
  11.6 4.4 %collective-permute-done.1.one_ref.ends_ref.inner_ref = bf16[2,128,1536]{2,1,0:T(8,128)(2,1)S(1)} collective-permute-done((bf16[2,128,1536]{2,1,0:T(8,128)(2,1)S(1)}, bf16[2,128,1536]{2,1,0:T(8,128)(2,1)S(1)}, u32[]{:S(2)}, u32[]{:S(2)}) %collective-permute-start.1) | collective-permute-done | bytes 786464 | tf_op jit(solution)/shard_map/ppermute | solution.py:284
  16.1 0.0 slice-start
  16.1 0.1 choose.2
  16.1 0.0 copy-start
  16.2 0.0 slice-start.1
  16.2 0.0 copy-start.1
  16.2 2.0 %collective-permute-start.4 = (bf16[2,128,1536]{2,1,0:T(8,128)(2,1)S(1)}, bf16[2,128,1536]{2,1,0:T(8,128)(2,1)S(1)}, u32[]{:S(2)}, u32[]{:S(2)}) collective-permute-start(bf16[2,128,1536]{2,1,0:T(8,128)(2,1)S(1)} %choose.2), channel_id=1, source_target_pairs={{0,3},{2,6},{4,7},{5,1},{6,10},{7,4},{8,11},{9,5},{10,14},{11,8},{... | collective-permute-start | bytes 2359304 | tf_op jit(solution)/shard_map/ppermute | solution.py:284
  18.2 0.7 %collective-permute-start.6 = (bf16[2,128,1536]{2,1,0:T(8,128)(2,1)S(1)}, bf16[2,128,1536]{2,1,0:T(8,128)(2,1)S(1)}, u32[]{:S(2)}, u32[]{:S(2)}) collective-permute-start(bf16[2,128,1536]{2,1,0:T(8,128)(2,1)S(1)} %collective-permute-done.1.one_ref.ends_ref.inner_ref), channel_id=1, source_target_pairs={{1,4},{5,8},{6,3},{9,12},{10,7},{14,11},{17,20},{21,24},{22,19},{2... | collective-permute-start | bytes 2359304 | tf_op jit(solution)/shard_map/ppermute | solution.py:284
  18.9 6.5 %collective-permute-done.2.block_ref = bf16[2,128,1536]{2,1,0:T(8,128)(2,1)} collective-permute-done((bf16[2,128,1536]{2,1,0:T(8,128)(2,1)S(1)}, bf16[2,128,1536]{2,1,0:T(8,128)(2,1)}, u32[]{:S(2)}, u32[]{:S(2)}) %collective-permute-start.2) | collective-permute-done | bytes 786464 | tf_op jit(solution)/shard_map/ppermute | solution.py:284
  25.4 1.2 %after.2.refs_0_ = bf16[2,128,1536]{2,1,0:T(8,128)(2,1)S(1)} custom-call(bf16[2,128,1536]{2,1,0:T(8,128)(2,1)} %collective-permute-done.2.block_ref), custom_call_target="tpu_custom_call" | custom-call | flops 30000001024 | tf_op jit(solution)/shard_map/after/pallas_call | solution.py:45
  26.6 0.0 collective-permute-done.mate_ref
  26.6 0.0 slice-done
  26.6 0.0 copy-done
  26.6 0.0 slice-done.1
  26.6 0.0 copy-done.1
  26.6 2.1 %first.1 = (f32[128,1536]{1,0:T(8,128)S(1)}, f32[12,128,128]{2,1,0:T(8,128)S(1)}, f32[12,128,128]{2,1,0:T(8,128)S(1)}, bf16[1536,1536]{1,0:T(8,128)(2,1)S(1)}, f32[5,128,128]{2,1,0:T(8,128)S(1)}) custom-call(s32[1]{0:T(128)} %bitcast.index_ref, s32[2,8]{1,0:T(2,128)S(1)} %copy-done.1, bf16[128,1536]{1,0:T(8,128)(2,1)S(1)} %copy-done, ...), custom_call_target="tpu_custom_call" | custom-call | tf_op jit(solution)/shard_map/first/pallas_call | solution.py:206
  28.7 0.8 %middle.2 = (f32[128,1536]{1,0:T(8,128)S(1)}, f32[12,128,128]{2,1,0:T(8,128)S(1)}, f32[12,128,128]{2,1,0:T(8,128)S(1)}) custom-call(f32[5,128,128]{2,1,0:T(8,128)S(1)} %get-tuple-element.16.bias_ref, bf16[128,1536]{1,0:T(8,128)(2,1)S(1)} %copy-done, f32[128,1536]{1,0:T(8,128)S(1)} %get-tuple-element.17.acc_ref, ...), custom_call_target="tpu_custom_call" | custom-call | tf_op jit(solution)/shard_map/middle/pallas_call | solution.py:233
  29.6 2.3 %collective-permute-done.4.refs_1_.ends_ref = bf16[2,128,1536]{2,1,0:T(8,128)(2,1)S(1)} collective-permute-done((bf16[2,128,1536]{2,1,0:T(8,128)(2,1)S(1)}, bf16[2,128,1536]{2,1,0:T(8,128)(2,1)S(1)}, u32[]{:S(2)}, u32[]{:S(2)}) %collective-permute-start.4) | collective-permute-done | bytes 786464 | tf_op jit(solution)/shard_map/ppermute | solution.py:284
  31.8 0.1 choose.3
  31.9 0.1 collective-permute-start.5
  32.0 0.0 collective-permute-done.3.refs_0_
  32.0 1.0 %middle.3 = (f32[128,1536]{1,0:T(8,128)S(1)}, f32[12,128,128]{2,1,0:T(8,128)S(1)}, f32[12,128,128]{2,1,0:T(8,128)S(1)}) custom-call(f32[5,128,128]{2,1,0:T(8,128)S(1)} %get-tuple-element.16.bias_ref, bf16[128,1536]{1,0:T(8,128)(2,1)S(1)} %copy-done, f32[128,1536]{1,0:T(8,128)S(1)} %get-tuple-element.20.acc_ref, ...), custom_call_target="tpu_custom_call" | custom-call | tf_op jit(solution)/shard_map/middle/pallas_call | solution.py:233
  33.0 0.0 collective-permute-done.6.block_ref
  33.0 0.1 after.3.relay_ref
  33.1 1.2 %collective-permute-done.5.swap_ref = bf16[2,128,1536]{2,1,0:T(8,128)(2,1)S(1)} collective-permute-done((bf16[2,128,1536]{2,1,0:T(8,128)(2,1)S(1)}, bf16[2,128,1536]{2,1,0:T(8,128)(2,1)S(1)}, u32[]{:S(2)}, u32[]{:S(2)}) %collective-permute-start.5) | collective-permute-done | bytes 786464 | tf_op jit(solution)/shard_map/ppermute | solution.py:284
  34.2 2.3 %last.1 = bf16[128,1536]{1,0:T(8,128)(2,1)} custom-call(f32[5,128,128]{2,1,0:T(8,128)S(1)} %get-tuple-element.16.bias_ref, bf16[128,1536]{1,0:T(8,128)(2,1)S(1)} %copy-done, f32[128,1536]{1,0:T(8,128)S(1)} %get-tuple-element.23.acc_ref, f32[12,128,128]{2,1,0:T(8,128)S(1)} %get-tuple-element.24.top_ref, f32[12,128,128]{2,1,0:T(8,128)S(1)} %get-tuple-element.25.total_ref, ...), custom_call_target="tpu_custom_call" | custom-call | tf_op jit(solution)/shard_map/last/pallas_call | solution.py:266
  (1 shorter events, 0.0 us)
Async XLA Ops:
  1.2 14.9 %collective-permute-start.1 = (bf16[2,128,1536]{2,1,0:T(8,128)(2,1)S(1)}, bf16[2,128,1536]{2,1,0:T(8,128)(2,1)S(1)}, u32[]{:S(2)}, u32[]{:S(2)}) collective-permute-start(bf16[2,128,1536]{2,1,0:T(8,128)(2,1)S(1)} %pad_maximum_fusion.own_ref.inner_ref), channel_id=1, source_target_pairs={{1,2},{2,1},{3,7},{4,0},{5,6},{6,5},{7,11},{8,4},{9,10},{10,9},{11... | collective-permute-start | bytes 2359304 | tf_op jit(solution)/shard_map/ppermute | solution.py:284
  2.5 22.9 %collective-permute-start.2 = (bf16[2,128,1536]{2,1,0:T(8,128)(2,1)S(1)}, bf16[2,128,1536]{2,1,0:T(8,128)(2,1)}, u32[]{:S(2)}, u32[]{:S(2)}) collective-permute-start(bf16[2,128,1536]{2,1,0:T(8,128)(2,1)S(1)} %pad_maximum_fusion.own_ref.inner_ref), channel_id=1, source_target_pairs={{0,4},{1,5},{4,8},{5,9},{6,2},{7,3},{8,12},{9,13},{10,6},{11,7},{1... | collective-permute-start | bytes 2359304 | tf_op jit(solution)/shard_map/ppermute | solution.py:284
  9.0 17.6 %collective-permute-start = (bf16[2,128,1536]{2,1,0:T(8,128)(2,1)S(1)}, bf16[2,128,1536]{2,1,0:T(8,128)(2,1)S(1)}, u32[]{:S(2)}, u32[]{:S(2)}) collective-permute-start(bf16[2,128,1536]{2,1,0:T(8,128)(2,1)S(1)} %pad_maximum_fusion.own_ref.inner_ref), channel_id=1, source_target_pairs={{0,1},{1,0},{2,3},{3,2},{4,5},{5,4},{6,7},{7,6},{8,9},{9,8},{10,11... | collective-permute-start | bytes 2359304 | tf_op jit(solution)/shard_map/ppermute | solution.py:284
  10.3 21.7 %collective-permute-start.3 = (bf16[2,128,1536]{2,1,0:T(8,128)(2,1)S(1)}, bf16[2,128,1536]{2,1,0:T(8,128)(2,1)S(1)}, u32[]{:S(2)}, u32[]{:S(2)}) collective-permute-start(bf16[2,128,1536]{2,1,0:T(8,128)(2,1)S(1)} %pad_maximum_fusion.own_ref.inner_ref), channel_id=1, source_target_pairs={{0,2},{3,1},{4,6},{7,5},{8,10},{11,9},{12,14},{15,13},{16,18},{19,... | collective-permute-start | bytes 2359304 | tf_op jit(solution)/shard_map/ppermute | solution.py:284
  16.1 10.5 %slice-start = ((s8[4718592]{0:T(1024)(128)(4,1)}), s8[4194304]{0:T(1024)(128)(4,1)S(1)}, s32[]{:S(2)}) async-start(s8[4718592]{0:T(1024)(128)(4,1)} %bitcast.3), calls=%async_computation | async-start | bytes 8388608
  16.1 10.4 %copy-start = (bf16[128,1536]{1,0:T(8,128)(2,1)S(1)}, bf16[128,1536]{1,0:T(8,128)(2,1)}, u32[]{:S(2)}) copy-start(bf16[128,1536]{1,0:T(8,128)(2,1)} %q_ref.7) | copy-start | bytes 1179652
  16.2 10.4 %slice-start.1 = ((s8[4718592]{0:T(1024)(128)(4,1)}), s8[524288]{0:T(1024)(128)(4,1)S(1)}, s32[]{:S(2)}) async-start(s8[4718592]{0:T(1024)(128)(4,1)} %bitcast.3), calls=%async_computation.1 | async-start | bytes 1048576
  16.2 10.4 %copy-start.1 = (s32[2,8]{1,0:T(2,128)S(1)}, s32[2,8]{1,0:T(2,128)}, u32[]{:S(2)}) copy-start(s32[2,8]{1,0:T(2,128)} %picks_ref.1) | copy-start | bytes 196
  16.2 15.7 %collective-permute-start.4 = (bf16[2,128,1536]{2,1,0:T(8,128)(2,1)S(1)}, bf16[2,128,1536]{2,1,0:T(8,128)(2,1)S(1)}, u32[]{:S(2)}, u32[]{:S(2)}) collective-permute-start(bf16[2,128,1536]{2,1,0:T(8,128)(2,1)S(1)} %choose.2), channel_id=1, source_target_pairs={{0,3},{2,6},{4,7},{5,1},{6,10},{7,4},{8,11},{9,5},{10,14},{11,8},{... | collective-permute-start | bytes 2359304 | tf_op jit(solution)/shard_map/ppermute | solution.py:284
  18.2 14.8 %collective-permute-start.6 = (bf16[2,128,1536]{2,1,0:T(8,128)(2,1)S(1)}, bf16[2,128,1536]{2,1,0:T(8,128)(2,1)S(1)}, u32[]{:S(2)}, u32[]{:S(2)}) collective-permute-start(bf16[2,128,1536]{2,1,0:T(8,128)(2,1)S(1)} %collective-permute-done.1.one_ref.ends_ref.inner_ref), channel_id=1, source_target_pairs={{1,4},{5,8},{6,3},{9,12},{10,7},{14,11},{17,20},{21,24},{22,19},{2... | collective-permute-start | bytes 2359304 | tf_op jit(solution)/shard_map/ppermute | solution.py:284
  31.9 2.4 %collective-permute-start.5 = (bf16[2,128,1536]{2,1,0:T(8,128)(2,1)S(1)}, bf16[2,128,1536]{2,1,0:T(8,128)(2,1)S(1)}, u32[]{:S(2)}, u32[]{:S(2)}) collective-permute-start(bf16[2,128,1536]{2,1,0:T(8,128)(2,1)S(1)} %choose.3), channel_id=1, source_target_pairs={{0,1},{1,0},{2,3},{3,2},{4,5},{5,4},{6,7},{7,6},{8,9},{9,8},{10,11... | collective-permute-start | bytes 2359304 | tf_op jit(solution)/shard_map/ppermute | solution.py:284
